TPU v7x, 256 devices: a whole 4x4x8 slice. The times are simulated.
256 devices in a mesh: ctx: 128 (over z, y, x_hi, core), kvh: 2 (over x_lo).
Axes of the slice: x: 4 (x_hi: 2, x_lo: 2; x = x_hi * 2 + x_lo), y: 4, z: 8, core: 2. Of those that a mesh axis runs over, the one named last changes fastest.
Arguments:
- queries: bfloat16 [256, 4, 16, 128], P('ctx', 'kvh'), may hold values from -12 to 12
- k_cache: bfloat16 [196608, 4, 128], P('ctx', 'kvh'), may hold values from -8 to 8
- v_cache: bfloat16 [196608, 4, 128], P('ctx', 'kvh'), may hold values from -6 to 6
- block_owner: int32 [1536], P('ctx'), may hold values from 0 to 1535, each once
- cached_lens: int32 [4], replicated, may hold values from 1 to 49086, as said below
- new_counts: int32 [4], replicated, may hold values from 1 to 64, 192 in all
Outputs:
- attended: bfloat16 [256, 64, 128], P(('ctx', 'kvh'))
Inputs may be any that keep to these rules, and one draw needn't show every extreme that they name: `block_owner`: each sequence's new tokens follow its cached tokens; every logical block is held by exactly one physical block. `cached_lens`: one sequence has exactly 49086 cached tokens; the four add up to 65448. `new_counts`: one sequence has exactly 64 new tokens; the four add up to 192.
All inputs are finite; a program needn't handle non-finite values.
Results may differ from a plain program's by a relative error of at most 0.013.
Values may be sent and summed in bfloat16 or wider, within the bound.
No kernel may reach another device: no remote copies, remote signals or barrier semaphores. Data moves between devices by JAX's collectives and lax.ppermute only.
A program may use at most 64 MiB of HBM per device.

v0:
```python
import math

import jax
import jax.numpy as jnp
from jax import lax
from jax.sharding import PartitionSpec as P


def key_layout(block_owner, block_size, blocks_per_seq):
    ident = jnp.repeat(block_owner, block_size)
    within = jnp.tile(jnp.arange(block_size, dtype=jnp.int32), block_owner.shape[0])
    return (ident // blocks_per_seq, ident % blocks_per_seq * block_size + within)


def query_layout(first_row, row_count, cached_lens, new_counts, seq_slots):
    token_ids = first_row + jnp.arange(row_count, dtype=jnp.int32)
    query_seq = token_ids // seq_slots
    within = token_ids % seq_slots
    matches = query_seq[:, None] == jnp.arange(cached_lens.shape[0], dtype=jnp.int32)[None, :]
    offset = jnp.sum(jnp.where(matches, cached_lens[None, :], 0), axis=1)
    limit = jnp.sum(jnp.where(matches, new_counts[None, :], 0), axis=1)
    return (query_seq, offset + within, within < limit)


def partial_attention(query_block, k_cache, v_cache, visible, score_scale):
    scores = (
        jnp.einsum("qhgd,khd->qhgk", query_block, k_cache, preferred_element_type=jnp.float32)
        * score_scale
    )
    shown = visible[:, None, None, :]
    maxima = jnp.max(jnp.where(shown, scores, -1e30), axis=-1)
    weights = jnp.where(shown, jnp.exp(scores - maxima[..., None]), 0.0)
    sums = jnp.sum(weights, axis=-1)
    context = jnp.einsum(
        "qhgk,khd->qhgd", weights.astype(jnp.bfloat16), v_cache, preferred_element_type=jnp.float32
    )
    return (context, maxima, sums)


def per_device(queries, k_cache, v_cache, block_owner, cached_lens, new_counts):
    cycle_size = lax.axis_size("ctx")
    tok_local, kv_local, group, head_size = queries.shape
    seqs_count = cached_lens.shape[0]
    blocks_per_seq = block_owner.shape[0] * cycle_size // seqs_count
    seq_slots = tok_local * cycle_size // seqs_count
    block_size = k_cache.shape[0] // block_owner.shape[0]
    score_scale = head_size ** (-0.5)
    key_seq, key_pos = key_layout(block_owner, block_size, blocks_per_seq)
    piece = lax.all_gather(queries, "ctx", axis=0, tiled=True)
    piece_rows = piece.shape[0]
    sub_rows = math.gcd(piece_rows, 32)

    def one_block(number):
        first_row = number * sub_rows
        query_seq, query_pos, usable = query_layout(
            first_row, sub_rows, cached_lens, new_counts, seq_slots
        )
        visible = (
            (query_seq[:, None] == key_seq[None, :])
            & (key_pos[None, :] <= query_pos[:, None])
            & usable[:, None]
        )
        query_block = lax.dynamic_slice_in_dim(piece, number * sub_rows, sub_rows, 0)
        return partial_attention(query_block, k_cache, v_cache, visible, score_scale)

    context, maxima, sums = lax.map(one_block, jnp.arange(piece_rows // sub_rows, dtype=jnp.int32))
    context = context.reshape((piece_rows, kv_local, group, head_size))
    maxima = maxima.reshape((piece_rows, kv_local, group))
    sums = sums.reshape((piece_rows, kv_local, group))
    context, maxima, sums = (context, maxima, sums)
    highest = lax.pmax(maxima, "ctx")
    factor = jnp.exp(maxima - highest)
    summed, denom = (
        lax.psum_scatter(context * factor[..., None], "ctx", scatter_dimension=0, tiled=True),
        lax.psum_scatter(sums * factor, "ctx", scatter_dimension=0, tiled=True),
    )
    result = summed / jnp.where(denom > 0.0, denom, 1.0)[..., None]
    result = result.astype(jnp.bfloat16).reshape(tok_local, kv_local * group, head_size)
    return lax.all_to_all(result, "kvh", split_axis=0, concat_axis=1, tiled=True)


def solution(mesh):
    in_specs = (
        P("ctx", "kvh", None, None),
        P("ctx", "kvh", None),
        P("ctx", "kvh", None),
        P("ctx"),
        P(),
        P(),
    )
    out_specs = P(("ctx", "kvh"), None, None)
    return jax.shard_map(
        per_device, mesh=mesh, in_specs=in_specs, out_specs=out_specs, check_vma=False
    )
```

profile of v0, /device:TPU:2, one launch (start us, length us, event | category | flops | bytes accessed | tf_op | source)
XLA Modules:
  0.0 1561.9 jit_solution(15172346407316104335)
XLA Ops:
  11.8 109.1 %all-gather.2.cloned.1.call-done = bf16[256,2,16,128]{3,2,0,1:T(8,128)(2,1)} async-done(((bf16[2,2,16,128]{3,2,0,1:T(8,128)(2,1)}), bf16[256,2,16,128]{3,2,0,1:T(8,128)(2,1)}) %all-gather.2.cloned.1.call-update) | async-done | bytes 2097168 | tf_op jit(solution)/shard_map/all_gather | solution.py:49
  120.9 113.3 %while.18 = (s32[]{:T(128)}, f32[8,32,2,16,128]{4,3,2,1,0:T(8,128)}, f32[8,32,2,16]{1,0,3,2:T(8,128)S(1)}, f32[8,32,2,16]{1,0,3,2:T(8,128)S(1)}, s32[8]{0:T(128)...) while((s32[]{:T(128)}, ...), condition=%wide.region_5.6_spmd.clone.clone, body=%wide.region_0.5_spmd.clone.clone.sunk | while | flops 822819712 | bytes 47720536 | solution.py:66
  123.1 2.3 fusion.40
  125.4 2.7 copy-done
  128.1 1.7 fusion.42
  130.0 4.0 fusion.41
  137.3 2.3 fusion.40
  139.6 2.7 copy-done
  144.1 4.0 fusion.41
  151.5 2.3 fusion.40
  153.8 2.7 copy-done
  158.3 4.0 fusion.41
  165.6 2.3 fusion.40
  167.9 2.7 copy-done
  172.4 4.0 fusion.41
  179.8 2.3 fusion.40
  182.1 2.7 copy-done
  186.6 4.0 fusion.41
  194.0 2.3 fusion.40
  196.3 2.7 copy-done
  200.8 4.0 fusion.41
  208.2 2.3 fusion.40
  210.5 2.7 copy-done
  215.0 4.0 fusion.41
  222.3 2.3 fusion.40
  224.7 2.7 copy-done
  229.2 4.0 fusion.41
  234.3 650.1 %pmax.7 = f32[256,2,16]{0,2,1:T(8,128)S(1)} all-reduce(f32[256,2,16]{0,2,1:T(8,128)S(1)} %reshape.130), channel_id=1, replica_groups=mesh['ctx'=128,'kvh'=2] {'ctx'}, use_global_device_ids=true, to_apply=%region_6.7 | all-reduce | flops 8192 | bytes 65536 | tf_op jit(solution)/shard_map/pmax | solution.py:71
  884.7 4.1 bitcast_multiply_fusion
  890.3 645.0 %all-reduce = f32[256,2,16]{2,1,0:T(2,128)S(1)} all-reduce(f32[256,2,16]{2,1,0:T(2,128)S(1)} %copy.35), channel_id=3, replica_groups=mesh['ctx'=128,'kvh'=2] {'ctx'}, use_global_device_ids=true, to_apply=%region_8.9.clone | all-reduce | flops 8192 | bytes 65536
  1535.3 12.8 reduce-scatter.2.cloned.1.call-done
  1548.9 5.6 all_to_all.12
  (135 shorter events, 41.6 us)
Async XLA Ops:
  6.5 114.3 %all-gather.2.cloned.1.call-start = ((), (), s32[]{:S(2)}) async-start(), calls=%async_computation.2 | async-start | bytes 2113536 | tf_op jit(solution)/shard_map/all_gather | solution.py:49
  7.9 1540.2 %reduce-scatter.2.cloned.1.call-start = ((), (), s32[]{:S(2)}) async-start(), calls=%async_computation.3 | async-start | bytes 4227072 | tf_op jit(solution)/shard_map/reduce_scatter | solution.py:74
  125.4 2.7 copy-start
  139.6 2.7 copy-start
  153.8 2.7 copy-start
  167.9 2.7 copy-start
  182.1 2.7 copy-start
  196.3 2.7 copy-start
  210.5 2.7 copy-start
  224.6 2.7 copy-start
  884.7 4.2 copy-start.1
Sparse Core Ops, SparseCore 0:
  11.2 109.6 all-gather.1
  889.0 659.0 reduce-scatter.1
where the time goes:
time: 1560 us
  blocking collectives  1300 us (83%)
  waiting for transfers between devices  122 us (8%)
  matrix products  50.7 us (3%)
  local copies, waits for them, and re-layouts  40.9 us (3%)
  other arithmetic  27.7 us (2%)
    pmax x1, blocking collectives, per_device(): highest = lax.pmax(maxima, 'ctx')  650 us
    unnamed x1, blocking collectives  645 us
    all_gather x1, waiting for transfers between devices, per_device(): piece = lax.all_gather(queries, 'ctx', axis=0, tiled=True)  109 us
    dot_general x8, matrix products, partial_attention(): jnp.einsum('qhgk,khd->qhgd', weights.astype(jnp.bfloat16), v_cache, prefe...  32.3 us
  transfers between devices with their start and end apart: 2, of which 2 were waited for; matrix products, arithmetic and copies ran while one was open for 0% of the time, Pallas kernels for 0%

commit v1 on v0

v1 whole, which is shorter than its diff:
```python
import functools

import jax
import jax.numpy as jnp
from jax import lax
from jax.experimental import pallas as pl
from jax.experimental.pallas import tpu as pltpu
from jax.sharding import Mesh, PartitionSpec as P

LOG2E = 1.4426950408889634
FLOOR = -1e29
MASKED = -1e30

BLK = 128
OWN = 12
BOTH = 2 * OWN
HEADS = 2
GROUP = 16
HD = 128
SEQS = 4
UNITS = SEQS * HEADS
MSG = HD + 8
BEYOND = 1 << 20
PAIRS = (BOTH + SEQS) // 2
WIDE = HEADS * BLK
LAST = HEADS * GROUP + 8
SMEM = pl.BlockSpec(memory_space=pltpu.SMEM)
VMEM = pl.BlockSpec(memory_space=pltpu.VMEM)
COST = pl.CostEstimate(flops=1_000_000_000, bytes_accessed=4 << 20, transcendentals=0)


def split3(x):
    hi = x.astype(jnp.bfloat16).astype(jnp.float32)
    rest = x - hi
    mid = rest.astype(jnp.bfloat16).astype(jnp.float32)
    return hi, mid, rest - mid


def prep_kernel(own_ids, peer_ids, cached, counts, k0, k1, v0, v1, list_ref, k_ref, v_ref):
    blocks_per_seq = (BOTH * 64) // SEQS
    found = []
    for b in range(BOTH):
        ident = own_ids[b] if b < OWN else peer_ids[b - OWN]
        s = sum((ident >= n * blocks_per_seq).astype(jnp.int32) for n in range(1, SEQS))
        number = ident - s * blocks_per_seq
        found.append((s, number, number * BLK <= cached[s] + counts[s] - 1))
    at = []
    end = jnp.int32(0)
    for n in range(SEQS):
        at.append(end)
        here = sum(((s == n) & hit).astype(jnp.int32) for s, _, hit in found)
        end = end + ((here + 1) & -2)
    pairs = ((end >> 1) + 1) & -2
    for e in range(2 * PAIRS):
        list_ref[0, e] = 0
        list_ref[1, e] = BEYOND
    for p in range(PAIRS):
        list_ref[2, p] = sum((p >= (at[n] >> 1)).astype(jnp.int32) for n in range(1, SEQS))
    for n in range(SEQS):
        list_ref[2, 16 + n] = at[n]
    for b, (s, number, hit) in enumerate(found):
        e = jnp.where(hit, list_ref[2, 16 + s], 31)
        list_ref[0, e] = b
        list_ref[1, e] = number
        list_ref[2, 16 + s] += hit.astype(jnp.int32)
    list_ref[2, 31] = pairs

    def place_pair(p, _):
        for i in range(2):
            here = slice(i * BLK, (i + 1) * BLK)
            b = list_ref[0, 2 * p + i]

            def put(k_from, v_from, first):
                rows = pl.ds(pl.multiple_of((b - first) * BLK, BLK), BLK)
                for h in range(HEADS):
                    k_ref[p, h, here, :] = k_from[h, rows, :]
                    v_ref[p, h, :, here] = jnp.transpose(v_from[h, rows, :])

            pl.when(b < OWN)(lambda: put(k0, v0, 0))
            pl.when(b >= OWN)(lambda: put(k1, v1, OWN))
        return 0

    lax.fori_loop(0, pairs, place_pair, 0)


def attend_kernel(steps, *refs):
    n = len(steps)
    lists, cached, counts, place = refs[:4]
    q_refs, (k_ref, v_ref) = refs[4:4 + 2 * n], refs[4 + 2 * n:6 + 2 * n]
    out_refs, (m_ref, l_ref, acc_ref, t_ref) = refs[6 + 2 * n:6 + 3 * n], refs[6 + 3 * n:]
    rows = BLK * n
    lane = lax.broadcasted_iota(jnp.int32, (1, rows), 1)
    far = steps[0] if n == 1 else jnp.where(lane < BLK, steps[0], steps[1])
    within = (
        32 * ((lane >> 5) & 1)
        + 8 * ((place[1] + far) & 3)
        + 4 * (((lane >> 6) + place[2]) & 1)
        + 2 * place[3]
        + ((lane >> 4) & 1)
    )
    slot = lax.broadcasted_iota(jnp.int32, (BLK, rows), 0)
    scale = LOG2E * HD ** -0.5
    count = lists[2, 31]
    m_ref[...] = jnp.full(m_ref.shape, FLOOR, jnp.float32)
    l_ref[...] = jnp.zeros(l_ref.shape, jnp.float32)
    acc_ref[...] = jnp.zeros(acc_ref.shape, jnp.float32)

    def score(j, _):
        for p in (2 * j, 2 * j + 1):
            s = lists[2, p]
            qpos = jnp.where(within < counts[s], cached[s] + within, -1)
            for h in range(HEADS):
                unit = s * HEADS + h
                q = jnp.concatenate(
                    [r[pl.ds(2 * s, 2), :, h].reshape(BLK // 2, HD) for r in q_refs], axis=0
                )
                t = lax.dot_general(
                    k_ref[p, h], q, (((1,), (1,)), ((), ())), preferred_element_type=jnp.float32
                )
                top = None
                for i in range(2):
                    limit = qpos - lists[1, 2 * p + i] * BLK
                    part = jnp.where(slot <= limit, t[i * BLK:(i + 1) * BLK] * scale, MASKED)
                    t_ref[p, h, i * BLK:(i + 1) * BLK, :] = part
                    peak = jnp.max(part.reshape(BLK // 8, 8, rows), axis=0)
                    top = peak if top is None else jnp.maximum(top, peak)
                m_ref[unit] = jnp.maximum(m_ref[unit], top)
        return 0

    lax.fori_loop(0, count >> 1, score, 0)
    for unit in range(UNITS):
        m_ref[unit] = jnp.broadcast_to(
            jnp.max(m_ref[unit], axis=0, keepdims=True), (8, rows)
        )

    def weigh(j, _):
        for p in (2 * j, 2 * j + 1):
            s = lists[2, p]
            for h in range(HEADS):
                unit = s * HEADS + h
                w = jnp.exp2(t_ref[p, h].reshape(2 * BLK // 8, 8, rows) - m_ref[unit][None])
                l_ref[unit] += jnp.sum(w, axis=0)
                acc_ref[unit] += jnp.dot(
                    v_ref[p, h],
                    w.reshape(2 * BLK, rows).astype(jnp.bfloat16),
                    preferred_element_type=jnp.float32,
                )
        return 0

    lax.fori_loop(0, count >> 1, weigh, 0)

    for unit in range(UNITS):
        total = jnp.sum(l_ref[unit], axis=0, keepdims=True)
        some = total > 0.0
        safe = jnp.where(some, total, 1.0)
        lse = jnp.where(some, m_ref[unit, 0:1, :] + jnp.log(safe) * LOG2E, MASKED)
        ctx = acc_ref[unit] * (1.0 / safe)
        tail = jnp.concatenate(split3(lse) + (jnp.zeros((5, rows), jnp.float32),), axis=0)
        for i, out_ref in enumerate(out_refs):
            cols = slice(i * BLK, (i + 1) * BLK)
            there = slice(unit * BLK, (unit + 1) * BLK)
            out_ref[0:HD, there] = ctx[:, cols].astype(jnp.bfloat16)
            out_ref[HD:MSG, there] = tail[:, cols].astype(jnp.bfloat16)


def logs_of(ref, there):
    t = ref[HD:MSG, there].astype(jnp.float32)
    return t[0:1] + t[1:2] + t[2:3]


def join_kernel(in0, in1, out_ref):
    for unit in range(UNITS):
        there = slice(unit * BLK, (unit + 1) * BLK)
        logs = [logs_of(r, there) for r in (in0, in1)]
        top = jnp.maximum(*logs)
        w = [jnp.exp2(x - top) for x in logs]
        out_ref[0:HD, there] = (
            in0[0:HD, there].astype(jnp.float32) * w[0]
            + in1[0:HD, there].astype(jnp.float32) * w[1]
        )
        out_ref[HD:MSG, there] = jnp.concatenate(
            [top, w[0] + w[1], jnp.zeros((6, BLK), jnp.float32)], axis=0
        )


def fold_kernel(place, joined, in0, in1, out_ref):
    def dest(s, e):
        return 8 * s + 4 * ((e >> 1) & 1) + 2 * ((place[2] + (e >> 2)) & 1) + (e & 1)

    for s in range(SEQS):
        tails = []
        for h in range(HEADS):
            unit = s * HEADS + h
            there = slice(unit * BLK, (unit + 1) * BLK)
            logs = [joined[HD:HD + 1, there], logs_of(in0, there), logs_of(in1, there)]
            top = functools.reduce(jnp.maximum, logs)
            w = [jnp.exp2(x - top) for x in logs]
            total = joined[HD + 1:HD + 2, there] * w[0] + w[1] + w[2]
            inv = 1.0 / total
            ctx = (
                joined[0:HD, there] * (w[0] * inv)
                + in0[0:HD, there].astype(jnp.float32) * (w[1] * inv)
                + in1[0:HD, there].astype(jnp.float32) * (w[2] * inv)
            )
            ctx = jnp.transpose(ctx).astype(jnp.bfloat16)
            for e in range(8):
                out_ref[dest(s, e), h * GROUP:(h + 1) * GROUP, :] = ctx[e * GROUP:(e + 1) * GROUP]
            tails.extend(split3(top + jnp.log(total) * LOG2E))
        tail = jnp.concatenate(tails + [jnp.zeros((2, BLK), jnp.float32)], axis=0)
        for e in range(8):
            turned = tail if e == 0 else pltpu.roll(tail, BLK - GROUP * e, 1)
            out_ref[dest(s, e), 32:LAST, :] = turned.astype(jnp.bfloat16)


def finish_kernel(in_ref, out_ref):
    for kvh in range(2):
        sources = [2 * n + kvh for n in range(16)]
        t = jnp.concatenate(
            [in_ref[n, 32:LAST, :].astype(jnp.float32) for n in sources], axis=0
        )
        t = jnp.transpose(t)[0:GROUP]
        cols = t + pltpu.roll(t, BLK - 1, 1) + pltpu.roll(t, BLK - 2, 1)
        for h in range(HEADS):
            logs = []
            for n in range(16):
                at = n * 8 + 3 * h
                logs.append(jnp.broadcast_to(cols[:, at:at + 1], (GROUP, HD)))
            top = functools.reduce(jnp.maximum, logs)
            total = jnp.zeros((GROUP, HD), jnp.float32)
            ctx = jnp.zeros((GROUP, HD), jnp.float32)
            for n in range(16):
                w = jnp.exp2(logs[n] - top)
                total = total + w
                ctx = ctx + w * in_ref[
                    sources[n], h * GROUP:(h + 1) * GROUP, :
                ].astype(jnp.float32)
            first = kvh * 32 + h * GROUP
            out_ref[0, first:first + GROUP, :] = (ctx / total).astype(jnp.bfloat16)


def turn(x, axis, size, step):
    return lax.ppermute(x, axis, [((i + step) % size, i) for i in range(size)])


def params(mib):
    return pltpu.CompilerParams(vmem_limit_bytes=mib << 20)


def per_device(queries, k_cache, v_cache, block_owner, cached_lens, new_counts):
    k0, v0 = (x.reshape(OWN * WIDE, HD) for x in (k_cache, v_cache))
    k1, v1, ids = (turn(x, "core", 2, 1) for x in (k0, v0, block_owner))
    k0, k1, v0, v1 = (
        jnp.transpose(x.reshape(OWN * BLK, HEADS, HD), (1, 0, 2)) for x in (k0, k1, v0, v1)
    )
    place = jnp.stack([lax.axis_index(a).astype(jnp.int32) for a in ("z", "y", "xh", "core")])

    q = jnp.broadcast_to(queries[None], (8,) + queries.shape)
    q = lax.all_to_all(q, "z", split_axis=0, concat_axis=0, tiled=True)
    lists, k, v = pl.pallas_call(
        prep_kernel,
        out_shape=[
            jax.ShapeDtypeStruct((3, 32), jnp.int32),
            jax.ShapeDtypeStruct((PAIRS, HEADS, 2 * BLK, HD), jnp.bfloat16),
            jax.ShapeDtypeStruct((PAIRS, HEADS, HD, 2 * BLK), jnp.bfloat16),
        ],
        in_specs=[SMEM] * 4 + [VMEM] * 4,
        out_specs=[SMEM, VMEM, VMEM],
        compiler_params=params(8),
        cost_estimate=COST,
        name="prep",
    )(block_owner, ids, cached_lens, new_counts, k0, k1, v0, v1)

    q, lists, k, v = lax.optimization_barrier((q, lists, k, v))
    both = [q, turn(q, "xh", 2, 1)]
    near, back = ([turn(x, "y", 4, n) for x in both] for n in (1, 3))
    qs = [both, near, [turn(near[0], "y", 4, 1), turn(back[1], "y", 4, 3)], back]

    def attend(place, *steps):
        n = len(steps)
        rows = n * BLK
        return pl.pallas_call(
            functools.partial(attend_kernel, steps),
            out_shape=[jax.ShapeDtypeStruct((MSG, 8 * BLK), jnp.bfloat16)] * n,
            in_specs=[SMEM] * 4 + [VMEM] * (2 * n + 2),
            out_specs=[VMEM] * n,
            scratch_shapes=[
                pltpu.VMEM((UNITS, 8, rows), jnp.float32),
                pltpu.VMEM((UNITS, 8, rows), jnp.float32),
                pltpu.VMEM((UNITS, HD, rows), jnp.float32),
                pltpu.VMEM((PAIRS, HEADS, 2 * BLK, rows), jnp.float32),
            ],
            compiler_params=params(12),
            cost_estimate=COST,
            name="attend" + "".join(map(str, steps)),
        )(lists, cached_lens, new_counts, place, *[x for i in steps for x in qs[i]], k, v)

    msg1, msg3 = attend(place, 1, 3)
    (msg2,) = attend(place, 2)
    (msg0,) = attend(place, 0)
    joined = pl.pallas_call(
        join_kernel,
        out_shape=jax.ShapeDtypeStruct((MSG, 8 * BLK), jnp.float32),
        in_specs=[VMEM] * 2,
        out_specs=VMEM,
        compiler_params=params(8),
        cost_estimate=COST,
        name="join",
    )(turn(msg1, "y", 4, -1), turn(msg3, "y", 4, -3))
    msg = pl.pallas_call(
        fold_kernel,
        out_shape=jax.ShapeDtypeStruct((32, LAST, HD), jnp.bfloat16),
        in_specs=[SMEM] + [VMEM] * 3,
        out_specs=VMEM,
        compiler_params=params(8),
        name="fold",
    )(place, joined, msg0, turn(msg2, "y", 4, -2))
    msg = lax.all_to_all(msg, ("z", "xh", "kvh"), split_axis=0, concat_axis=0, tiled=True)
    return pl.pallas_call(
        finish_kernel,
        out_shape=jax.ShapeDtypeStruct((1, 64, HD), jnp.bfloat16),
        in_specs=[VMEM],
        out_specs=VMEM,
        compiler_params=params(4),
        name="finish",
    )(msg)


def solution(mesh):
    split = Mesh(mesh.devices.reshape(8, 4, 2, 2, 2), ("z", "y", "xh", "core", "kvh"))
    ctx = ("z", "y", "xh", "core")
    in_specs = (
        P(ctx, "kvh", None, None),
        P(ctx, "kvh", None),
        P(ctx, "kvh", None),
        P(ctx),
        P(),
        P(),
    )
    return jax.shard_map(
        per_device,
        mesh=split,
        in_specs=in_specs,
        out_specs=P(ctx + ("kvh",), None, None),
        check_vma=False,
    )
```

time: 1560 us -> 75.7 us (0.05)
  the two profiles are of different devices: /device:TPU:2 before, /device:TPU:32 now
where the time goes in v1:
time: 75.7 us; the launch traced here: 74.7 us
  starting transfers between devices  26.1 us (34%)
  blocking collectives  21.6 us (29%)
  Pallas kernels  10.3 us (14%)
  waiting for transfers between devices  10.2 us (13%)
  local copies, waits for them, and re-layouts  6.34 us (8%)
    all_to_all x1, blocking collectives, per_device(): lax.all_to_all(msg, ('z', 'xh', 'kvh'), split_axis=0, concat_axis=0, tile...  21.6 us
    ppermute x13, starting transfers between devices, turn(): return lax.ppermute(x, axis, [((i + step) % size, i) for i in range(size)])  17.5 us
    all_to_all x1, starting transfers between devices, per_device(): q = lax.all_to_all(q, 'z', split_axis=0, concat_axis=0, tiled=True)  8.57 us
    ppermute x13, waiting for transfers between devices, turn(): return lax.ppermute(x, axis, [((i + step) % size, i) for i in range(size)])  8.16 us
    pallas_call x3, Pallas kernels, attend(): pl.pallas_call(functools.partial(attend_kernel, steps), out_shape=[jax.Sh...  5.62 us
    unnamed x10, local copies, waits for them, and re-layouts  3.18 us
    pallas_call x1, Pallas kernels, per_device(): pl.pallas_call(prep_kernel, out_shape=[jax.ShapeDtypeStruct((3, 32), jnp....  2.59 us
    all_to_all x1, waiting for transfers between devices, per_device(): q = lax.all_to_all(q, 'z', split_axis=0, concat_axis=0, tiled=True)  2.03 us
  transfers between devices with their start and end apart: 14, of which 7 were waited for; matrix products, arithmetic and copies ran while one was open for 4% of the time, Pallas kernels for 11%

profile of v1, /device:TPU:32, one launch (start us, length us, event | category | flops | bytes accessed | tf_op | source)
XLA Modules:
  0.0 74.7 jit_solution(18260918520919734163)
XLA Ops:
  0.0 0.5 collective-permute-start.1
  0.5 1.4 %broadcast_in_dim.2 = bf16[8,2,2,16,128]{4,3,2,1,0:T(8,128)(2,1)} broadcast(bf16[2,2,16,128]{3,2,1,0:T(8,128)(2,1)} %param.6), dimensions={1,2,3,4} | broadcast | bytes 147456 | tf_op jit(solution)/shard_map/broadcast_in_dim | solution.py:257
  1.9 8.6 %all-to-all-start = ((bf16[8,2,2,16,128]{4,3,2,1,0:T(8,128)(2,1)}), bf16[8,2,2,16,128]{4,3,2,1,0:T(8,128)(2,1)S(1)}, u32[]{:S(2)}, u32[]{:S(2)}) async-start(bf16[8,2,2,16,128]{4,3,2,1,0:T(8,128)(2,1)} %broadcast_in_dim.2), calls=%async_computation | async-start | bytes 262144 | tf_op jit(solution)/shard_map/all_to_all | solution.py:258
  10.5 1.6 %copy_bitcast_fusion.1 = (bf16[2,1536,128]{2,1,0:T(8,128)(2,1)S(1)}, bf16[2,1536,128]{2,1,0:T(8,128)(2,1)S(1)}) fusion(bf16[1536,2,128]{2,1,0:T(2,128)(2,1)} %param.8, bf16[1536,2,128]{2,1,0:T(2,128)(2,1)} %param.7), kind=kLoop, calls=%fused_computation.1 | loop fusion | bytes 3145728 | tf_op jit(solution)/shard_map/transpose | solution.py:253
  12.3 0.4 copy-done.2
  12.7 2.6 %prep.1 = (s32[3,32]{1,0:T(4,128)S(1)}, bf16[14,2,256,128]{3,2,1,0:T(8,128)(2,1)S(1)}, bf16[14,2,128,256]{3,2,1,0:T(8,128)(2,1)S(1)}) custom-call(s32[12]{0:T(128)S(1)} %copy-done.4, s32[12]{0:T(128)S(1)} %collective-permute-done.peer_ids, s32[4]{0:T(128)S(1)} %copy-done.2, s32[4]{0:T(128)S(1)} %copy-done.3, bf16[2,1536,128]{2,1,0:T(8,128)(2,1)S(1)} %get-tuple-element.24.k0, ...), custom_call_target="tpu_custom_call" | custom-call | flops 1000000000 | bytes 4194304 | tf_op jit(solution)/shard_map/prep/pallas_call | solution.py:259
  15.3 1.3 %copy-done = bf16[14,2,128,256]{3,2,1,0:T(8,128)(2,1)} copy-done((bf16[14,2,128,256]{3,2,1,0:T(8,128)(2,1)}, bf16[14,2,128,256]{3,2,1,0:T(8,128)(2,1)S(1)}, u32[]{:S(2)}) %copy-start) | copy-done | bytes 1835032
  16.6 2.0 %all-to-all-done.refs_4_ = bf16[8,2,2,16,128]{4,3,2,1,0:T(8,128)(2,1)S(1)} async-done(((bf16[8,2,2,16,128]{4,3,2,1,0:T(8,128)(2,1)}), bf16[8,2,2,16,128]{4,3,2,1,0:T(8,128)(2,1)S(1)}, u32[]{:S(2)}, u32[]{:S(2)}) %all-to-all-start) | async-done | bytes 131104 | tf_op jit(solution)/shard_map/all_to_all | solution.py:258
  18.6 3.0 %collective-permute-start.4 = (bf16[8,2,2,16,128]{4,3,2,1,0:T(8,128)(2,1)S(1)}, bf16[8,2,2,16,128]{4,3,2,1,0:T(8,128)(2,1)S(1)}, u32[]{:S(2)}, u32[]{:S(2)}) collective-permute-start(bf16[8,2,2,16,128]{4,3,2,1,0:T(8,128)(2,1)S(1)} %all-to-all-done.refs_4_), channel_id=1, source_target_pairs={{4,0},{0,4},{5,1},{1,5},{6,2},{2,6},{7,3},{3,7},{12,8},{8,12},{13,... | collective-permute-start | bytes 393224 | tf_op jit(solution)/shard_map/ppermute | solution.py:242
  21.7 3.0 %collective-permute-start.3 = (bf16[8,2,2,16,128]{4,3,2,1,0:T(8,128)(2,1)S(1)}, bf16[8,2,2,16,128]{4,3,2,1,0:T(8,128)(2,1)S(1)}, u32[]{:S(2)}, u32[]{:S(2)}) collective-permute-start(bf16[8,2,2,16,128]{4,3,2,1,0:T(8,128)(2,1)S(1)} %all-to-all-done.refs_4_), channel_id=1, source_target_pairs={{8,0},{16,8},{24,16},{0,24},{9,1},{17,9},{25,17},{1,25},{10,2},{18... | collective-permute-start | bytes 393224 | tf_op jit(solution)/shard_map/ppermute | solution.py:242
  24.7 0.4 collective-permute-done.4.refs_5_
  25.1 1.6 %collective-permute-start.7 = (bf16[8,2,2,16,128]{4,3,2,1,0:T(8,128)(2,1)S(1)}, bf16[8,2,2,16,128]{4,3,2,1,0:T(8,128)(2,1)S(1)}, u32[]{:S(2)}, u32[]{:S(2)}) collective-permute-start(bf16[8,2,2,16,128]{4,3,2,1,0:T(8,128)(2,1)S(1)} %collective-permute-done.4.refs_5_), channel_id=1, source_target_pairs={{24,0},{0,8},{8,16},{16,24},{25,1},{1,9},{9,17},{17,25},{26,2},{2,... | collective-permute-start | bytes 393224 | tf_op jit(solution)/shard_map/ppermute | solution.py:242
  26.7 1.6 %collective-permute-start.6 = (bf16[8,2,2,16,128]{4,3,2,1,0:T(8,128)(2,1)S(1)}, bf16[8,2,2,16,128]{4,3,2,1,0:T(8,128)(2,1)S(1)}, u32[]{:S(2)}, u32[]{:S(2)}) collective-permute-start(bf16[8,2,2,16,128]{4,3,2,1,0:T(8,128)(2,1)S(1)} %all-to-all-done.refs_4_), channel_id=1, source_target_pairs={{24,0},{0,8},{8,16},{16,24},{25,1},{1,9},{9,17},{17,25},{26,2},{2,... | collective-permute-start | bytes 393224 | tf_op jit(solution)/shard_map/ppermute | solution.py:242
  28.3 1.7 %collective-permute-start.5 = (bf16[8,2,2,16,128]{4,3,2,1,0:T(8,128)(2,1)S(1)}, bf16[8,2,2,16,128]{4,3,2,1,0:T(8,128)(2,1)S(1)}, u32[]{:S(2)}, u32[]{:S(2)}) collective-permute-start(bf16[8,2,2,16,128]{4,3,2,1,0:T(8,128)(2,1)S(1)} %collective-permute-done.4.refs_5_), channel_id=1, source_target_pairs={{8,0},{16,8},{24,16},{0,24},{9,1},{17,9},{25,17},{1,25},{10,2},{18... | collective-permute-start | bytes 393224 | tf_op jit(solution)/shard_map/ppermute | solution.py:242
  29.9 0.9 %collective-permute-start.10 = (bf16[8,2,2,16,128]{4,3,2,1,0:T(8,128)(2,1)S(1)}, bf16[8,2,2,16,128]{4,3,2,1,0:T(8,128)(2,1)S(1)}, u32[]{:S(2)}, u32[]{:S(2)}) collective-permute-start(bf16[8,2,2,16,128]{4,3,2,1,0:T(8,128)(2,1)S(1)} %collective-permute-done.3.refs_4_), channel_id=1, source_target_pairs={{8,0},{16,8},{24,16},{0,24},{9,1},{17,9},{25,17},{1,25},{10,2},{18... | collective-permute-start | bytes 393224 | tf_op jit(solution)/shard_map/ppermute | solution.py:242
  30.9 0.4 collective-permute-done.7.refs_7_
  31.3 0.9 %collective-permute-start.11 = (bf16[8,2,2,16,128]{4,3,2,1,0:T(8,128)(2,1)S(1)}, bf16[8,2,2,16,128]{4,3,2,1,0:T(8,128)(2,1)S(1)}, u32[]{:S(2)}, u32[]{:S(2)}) collective-permute-start(bf16[8,2,2,16,128]{4,3,2,1,0:T(8,128)(2,1)S(1)} %collective-permute-done.7.refs_7_), channel_id=1, source_target_pairs={{24,0},{0,8},{8,16},{16,24},{25,1},{1,9},{9,17},{17,25},{26,2},{2,... | collective-permute-start | bytes 393224 | tf_op jit(solution)/shard_map/ppermute | solution.py:242
  32.3 1.7 %collective-permute-done.6.refs_6_ = bf16[8,2,2,16,128]{4,3,2,1,0:T(8,128)(2,1)S(1)} collective-permute-done((bf16[8,2,2,16,128]{4,3,2,1,0:T(8,128)(2,1)S(1)}, bf16[8,2,2,16,128]{4,3,2,1,0:T(8,128)(2,1)S(1)}, u32[]{:S(2)}, u32[]{:S(2)}) %collective-permute-start.6) | collective-permute-done | bytes 131104 | tf_op jit(solution)/shard_map/ppermute | solution.py:242
  34.0 1.5 %copy-done.1 = bf16[14,2,128,256]{3,2,1,0:T(8,128)(2,1)S(1)} copy-done((bf16[14,2,128,256]{3,2,1,0:T(8,128)(2,1)S(1)}, bf16[14,2,128,256]{3,2,1,0:T(8,128)(2,1)}, u32[]{:S(2)}) %copy-start.1) | copy-done | bytes 1835032
  35.5 2.1 %attend13.1 = (bf16[136,1024]{1,0:T(8,128)(2,1)S(1)}, bf16[136,1024]{1,0:T(8,128)(2,1)S(1)}) custom-call(s32[3,32]{1,0:T(4,128)S(1)} %get-tuple-element.17.refs_0_, s32[4]{0:T(128)S(1)} %copy-done.2, s32[4]{0:T(128)S(1)} %copy-done.3, s32[4]{0:T(128)S(1)} %pad_add_fusion.refs_3_.place, bf16[8,2,2,16,128]{4,3,2,1,0:T(8,128)(2,1)S(1)} %collective-permute-done.3.refs_4_, ...), custom_call_target="tpu_custom_call" | custom-call | flops 1000000000 | bytes 4194304 | tf_op jit(solution)/shard_map/attend13/pallas_call | solution.py:281
  37.7 1.2 %collective-permute-start.8 = (bf16[136,1024]{1,0:T(8,128)(2,1)S(1)}, bf16[136,1024]{1,0:T(8,128)(2,1)S(1)}, u32[]{:S(2)}, u32[]{:S(2)}) collective-permute-start(bf16[136,1024]{1,0:T(8,128)(2,1)S(1)} %get-tuple-element.21), channel_id=1, source_target_pairs={{24,0},{0,8},{8,16},{16,24},{25,1},{1,9},{9,17},{17,25},{26,2},{2,... | collective-permute-start | bytes 835592 | tf_op jit(solution)/shard_map/ppermute | solution.py:242
  38.9 2.1 %collective-permute-start.9 = (bf16[136,1024]{1,0:T(8,128)(2,1)S(1)}, bf16[136,1024]{1,0:T(8,128)(2,1)S(1)}, u32[]{:S(2)}, u32[]{:S(2)}) collective-permute-start(bf16[136,1024]{1,0:T(8,128)(2,1)S(1)} %get-tuple-element.22), channel_id=1, source_target_pairs={{8,0},{16,8},{24,16},{0,24},{9,1},{17,9},{25,17},{1,25},{10,2},{18... | collective-permute-start | bytes 835592 | tf_op jit(solution)/shard_map/ppermute | solution.py:242
  41.0 1.7 %attend2.1 = bf16[136,1024]{1,0:T(8,128)(2,1)S(1)} custom-call(s32[3,32]{1,0:T(4,128)S(1)} %get-tuple-element.17.refs_0_, s32[4]{0:T(128)S(1)} %copy-done.2, s32[4]{0:T(128)S(1)} %copy-done.3, s32[4]{0:T(128)S(1)} %pad_add_fusion.refs_3_.place, bf16[8,2,2,16,128]{4,3,2,1,0:T(8,128)(2,1)S(1)} %collective-permute-done.10.refs_4_, ...), custom_call_target="tpu_custom_call" | custom-call | flops 1000000000 | bytes 4194304 | tf_op jit(solution)/shard_map/attend2/pallas_call | solution.py:281
  42.7 1.1 %collective-permute-start.12 = (bf16[136,1024]{1,0:T(8,128)(2,1)S(1)}, bf16[136,1024]{1,0:T(8,128)(2,1)S(1)}, u32[]{:S(2)}, u32[]{:S(2)}) collective-permute-start(bf16[136,1024]{1,0:T(8,128)(2,1)S(1)} %attend2.1), channel_id=1, source_target_pairs={{16,0},{24,8},{0,16},{8,24},{17,1},{25,9},{1,17},{9,25},{18,2},{26... | collective-permute-start | bytes 835592 | tf_op jit(solution)/shard_map/ppermute | solution.py:242
  43.8 1.7 %attend0.1.in0 = bf16[136,1024]{1,0:T(8,128)(2,1)S(1)} custom-call(s32[3,32]{1,0:T(4,128)S(1)} %get-tuple-element.17.refs_0_, s32[4]{0:T(128)S(1)} %copy-done.2, s32[4]{0:T(128)S(1)} %copy-done.3, s32[4]{0:T(128)S(1)} %pad_add_fusion.refs_3_.place, bf16[8,2,2,16,128]{4,3,2,1,0:T(8,128)(2,1)S(1)} %all-to-all-done.refs_4_, ...), custom_call_target="tpu_custom_call" | custom-call | flops 1000000000 | bytes 4194304 | tf_op jit(solution)/shard_map/attend0/pallas_call | solution.py:281
  45.5 2.7 %collective-permute-done.8.in0 = bf16[136,1024]{1,0:T(8,128)(2,1)S(1)} collective-permute-done((bf16[136,1024]{1,0:T(8,128)(2,1)S(1)}, bf16[136,1024]{1,0:T(8,128)(2,1)S(1)}, u32[]{:S(2)}, u32[]{:S(2)}) %collective-permute-start.8) | collective-permute-done | bytes 278560 | tf_op jit(solution)/shard_map/ppermute | solution.py:242
  48.2 1.8 %collective-permute-done.9.in1 = bf16[136,1024]{1,0:T(8,128)(2,1)S(1)} collective-permute-done((bf16[136,1024]{1,0:T(8,128)(2,1)S(1)}, bf16[136,1024]{1,0:T(8,128)(2,1)S(1)}, u32[]{:S(2)}, u32[]{:S(2)}) %collective-permute-start.9) | collective-permute-done | bytes 278560 | tf_op jit(solution)/shard_map/ppermute | solution.py:242
  50.0 0.1 join.1.joined
  50.2 1.0 %collective-permute-done.12.in1 = bf16[136,1024]{1,0:T(8,128)(2,1)S(1)} collective-permute-done((bf16[136,1024]{1,0:T(8,128)(2,1)S(1)}, bf16[136,1024]{1,0:T(8,128)(2,1)S(1)}, u32[]{:S(2)}, u32[]{:S(2)}) %collective-permute-start.12) | collective-permute-done | bytes 278560 | tf_op jit(solution)/shard_map/ppermute | solution.py:242
  51.2 0.8 %fold.1 = bf16[32,40,128]{2,1,0:T(8,128)(2,1)S(1)} custom-call(s32[4]{0:T(128)S(1)} %pad_add_fusion.refs_3_.place, f32[136,1024]{1,0:T(8,128)S(1)} %join.1.joined, bf16[136,1024]{1,0:T(8,128)(2,1)S(1)} %attend0.1.in0, bf16[136,1024]{1,0:T(8,128)(2,1)S(1)} %collective-permute-done.12.in1), custom_call_target="tpu_custom_call" | custom-call | tf_op jit(solution)/shard_map/fold/pallas_call | solution.py:309
  52.0 21.6 %all_to_all.10.in_ref = bf16[32,40,128]{2,1,0:T(8,128)(2,1)S(1)} all-to-all(bf16[32,40,128]{2,1,0:T(8,128)(2,1)S(1)} %fold.1), channel_id=1, replica_groups=mesh['z'=8,'y'=4,'xh'=2,'core'=2,'kvh'=2] {'z','xh','kvh'}, dimensions={0} | all-to-all | bytes 655360 | tf_op jit(solution)/shard_map/all_to_all | solution.py:317
  73.6 1.1 %finish.1 = bf16[1,64,128]{2,1,0:T(8,128)(2,1)} custom-call(bf16[32,40,128]{2,1,0:T(8,128)(2,1)S(1)} %all_to_all.10.in_ref), custom_call_target="tpu_custom_call" | custom-call | tf_op jit(solution)/shard_map/finish/pallas_call | solution.py:318
  (19 shorter events, 0.4 us)
Async XLA Ops:
  0.0 12.1 %collective-permute-start.2 = (bf16[3072,128]{1,0:T(8,128)(2,1)}, bf16[3072,128]{1,0:T(8,128)(2,1)S(1)}, u32[]{:S(2)}, u32[]{:S(2)}) collective-permute-start(bf16[3072,128]{1,0:T(8,128)(2,1)} %bitcast.22), channel_id=1, source_target_pairs={{2,0},{0,2},{3,1},{1,3},{6,4},{4,6},{7,5},{5,7},{10,8},{8,10},{11,... | collective-permute-start | bytes 2359304 | tf_op jit(solution)/shard_map/ppermute | solution.py:242
  0.0 12.2 %collective-permute-start.1 = (bf16[3072,128]{1,0:T(8,128)(2,1)}, bf16[3072,128]{1,0:T(8,128)(2,1)S(1)}, u32[]{:S(2)}, u32[]{:S(2)}) collective-permute-start(bf16[3072,128]{1,0:T(8,128)(2,1)} %bitcast.23), channel_id=1, source_target_pairs={{2,0},{0,2},{3,1},{1,3},{6,4},{4,6},{7,5},{5,7},{10,8},{8,10},{11,... | collective-permute-start | bytes 2359304 | tf_op jit(solution)/shard_map/ppermute | solution.py:242
  0.5 11.8 %collective-permute-start = (s32[12]{0:T(128)}, s32[12]{0:T(128)S(1)}, u32[]{:S(2)}, u32[]{:S(2)}) collective-permute-start(s32[12]{0:T(128)} %own_ids.1), channel_id=1, source_target_pairs={{2,0},{0,2},{3,1},{1,3},{6,4},{4,6},{7,5},{5,7},{10,8},{8,10},{11,... | collective-permute-start | bytes 152 | tf_op jit(solution)/shard_map/ppermute | solution.py:242
  1.9 16.7 %all-to-all-start = ((bf16[8,2,2,16,128]{4,3,2,1,0:T(8,128)(2,1)}), bf16[8,2,2,16,128]{4,3,2,1,0:T(8,128)(2,1)S(1)}, u32[]{:S(2)}, u32[]{:S(2)}) async-start(bf16[8,2,2,16,128]{4,3,2,1,0:T(8,128)(2,1)} %broadcast_in_dim.2), calls=%async_computation | async-start | bytes 262144 | tf_op jit(solution)/shard_map/all_to_all | solution.py:258
  12.0 0.7 copy-start.2
  12.1 0.7 copy-start.3
  12.1 0.7 copy-start.4
  15.3 1.3 %copy-start = (bf16[14,2,128,256]{3,2,1,0:T(8,128)(2,1)}, bf16[14,2,128,256]{3,2,1,0:T(8,128)(2,1)S(1)}, u32[]{:S(2)}) copy-start(bf16[14,2,128,256]{3,2,1,0:T(8,128)(2,1)S(1)} %get-tuple-element.20.refs_9_.refs_7_) | copy-start | bytes 5505028
  18.6 6.5 %collective-permute-start.4 = (bf16[8,2,2,16,128]{4,3,2,1,0:T(8,128)(2,1)S(1)}, bf16[8,2,2,16,128]{4,3,2,1,0:T(8,128)(2,1)S(1)}, u32[]{:S(2)}, u32[]{:S(2)}) collective-permute-start(bf16[8,2,2,16,128]{4,3,2,1,0:T(8,128)(2,1)S(1)} %all-to-all-done.refs_4_), channel_id=1, source_target_pairs={{4,0},{0,4},{5,1},{1,5},{6,2},{2,6},{7,3},{3,7},{12,8},{8,12},{13,... | collective-permute-start | bytes 393224 | tf_op jit(solution)/shard_map/ppermute | solution.py:242
  21.7 8.3 %collective-permute-start.3 = (bf16[8,2,2,16,128]{4,3,2,1,0:T(8,128)(2,1)S(1)}, bf16[8,2,2,16,128]{4,3,2,1,0:T(8,128)(2,1)S(1)}, u32[]{:S(2)}, u32[]{:S(2)}) collective-permute-start(bf16[8,2,2,16,128]{4,3,2,1,0:T(8,128)(2,1)S(1)} %all-to-all-done.refs_4_), channel_id=1, source_target_pairs={{8,0},{16,8},{24,16},{0,24},{9,1},{17,9},{25,17},{1,25},{10,2},{18... | collective-permute-start | bytes 393224 | tf_op jit(solution)/shard_map/ppermute | solution.py:242
  25.1 6.2 %collective-permute-start.7 = (bf16[8,2,2,16,128]{4,3,2,1,0:T(8,128)(2,1)S(1)}, bf16[8,2,2,16,128]{4,3,2,1,0:T(8,128)(2,1)S(1)}, u32[]{:S(2)}, u32[]{:S(2)}) collective-permute-start(bf16[8,2,2,16,128]{4,3,2,1,0:T(8,128)(2,1)S(1)} %collective-permute-done.4.refs_5_), channel_id=1, source_target_pairs={{24,0},{0,8},{8,16},{16,24},{25,1},{1,9},{9,17},{17,25},{26,2},{2,... | collective-permute-start | bytes 393224 | tf_op jit(solution)/shard_map/ppermute | solution.py:242
  26.7 7.3 %collective-permute-start.6 = (bf16[8,2,2,16,128]{4,3,2,1,0:T(8,128)(2,1)S(1)}, bf16[8,2,2,16,128]{4,3,2,1,0:T(8,128)(2,1)S(1)}, u32[]{:S(2)}, u32[]{:S(2)}) collective-permute-start(bf16[8,2,2,16,128]{4,3,2,1,0:T(8,128)(2,1)S(1)} %all-to-all-done.refs_4_), channel_id=1, source_target_pairs={{24,0},{0,8},{8,16},{16,24},{25,1},{1,9},{9,17},{17,25},{26,2},{2,... | collective-permute-start | bytes 393224 | tf_op jit(solution)/shard_map/ppermute | solution.py:242
  28.3 5.7 %collective-permute-start.5 = (bf16[8,2,2,16,128]{4,3,2,1,0:T(8,128)(2,1)S(1)}, bf16[8,2,2,16,128]{4,3,2,1,0:T(8,128)(2,1)S(1)}, u32[]{:S(2)}, u32[]{:S(2)}) collective-permute-start(bf16[8,2,2,16,128]{4,3,2,1,0:T(8,128)(2,1)S(1)} %collective-permute-done.4.refs_5_), channel_id=1, source_target_pairs={{8,0},{16,8},{24,16},{0,24},{9,1},{17,9},{25,17},{1,25},{10,2},{18... | collective-permute-start | bytes 393224 | tf_op jit(solution)/shard_map/ppermute | solution.py:242
  29.9 11.0 %collective-permute-start.10 = (bf16[8,2,2,16,128]{4,3,2,1,0:T(8,128)(2,1)S(1)}, bf16[8,2,2,16,128]{4,3,2,1,0:T(8,128)(2,1)S(1)}, u32[]{:S(2)}, u32[]{:S(2)}) collective-permute-start(bf16[8,2,2,16,128]{4,3,2,1,0:T(8,128)(2,1)S(1)} %collective-permute-done.3.refs_4_), channel_id=1, source_target_pairs={{8,0},{16,8},{24,16},{0,24},{9,1},{17,9},{25,17},{1,25},{10,2},{18... | collective-permute-start | bytes 393224 | tf_op jit(solution)/shard_map/ppermute | solution.py:242
  31.3 9.7 %collective-permute-start.11 = (bf16[8,2,2,16,128]{4,3,2,1,0:T(8,128)(2,1)S(1)}, bf16[8,2,2,16,128]{4,3,2,1,0:T(8,128)(2,1)S(1)}, u32[]{:S(2)}, u32[]{:S(2)}) collective-permute-start(bf16[8,2,2,16,128]{4,3,2,1,0:T(8,128)(2,1)S(1)} %collective-permute-done.7.refs_7_), channel_id=1, source_target_pairs={{24,0},{0,8},{8,16},{16,24},{25,1},{1,9},{9,17},{17,25},{26,2},{2,... | collective-permute-start | bytes 393224 | tf_op jit(solution)/shard_map/ppermute | solution.py:242
  34.0 1.5 %copy-start.1 = (bf16[14,2,128,256]{3,2,1,0:T(8,128)(2,1)S(1)}, bf16[14,2,128,256]{3,2,1,0:T(8,128)(2,1)}, u32[]{:S(2)}) copy-start(bf16[14,2,128,256]{3,2,1,0:T(8,128)(2,1)} %copy-done) | copy-start | bytes 5505028
  37.7 10.6 %collective-permute-start.8 = (bf16[136,1024]{1,0:T(8,128)(2,1)S(1)}, bf16[136,1024]{1,0:T(8,128)(2,1)S(1)}, u32[]{:S(2)}, u32[]{:S(2)}) collective-permute-start(bf16[136,1024]{1,0:T(8,128)(2,1)S(1)} %get-tuple-element.21), channel_id=1, source_target_pairs={{24,0},{0,8},{8,16},{16,24},{25,1},{1,9},{9,17},{17,25},{26,2},{2,... | collective-permute-start | bytes 835592 | tf_op jit(solution)/shard_map/ppermute | solution.py:242
  38.9 11.1 %collective-permute-start.9 = (bf16[136,1024]{1,0:T(8,128)(2,1)S(1)}, bf16[136,1024]{1,0:T(8,128)(2,1)S(1)}, u32[]{:S(2)}, u32[]{:S(2)}) collective-permute-start(bf16[136,1024]{1,0:T(8,128)(2,1)S(1)} %get-tuple-element.22), channel_id=1, source_target_pairs={{8,0},{16,8},{24,16},{0,24},{9,1},{17,9},{25,17},{1,25},{10,2},{18... | collective-permute-start | bytes 835592 | tf_op jit(solution)/shard_map/ppermute | solution.py:242
  42.7 8.5 %collective-permute-start.12 = (bf16[136,1024]{1,0:T(8,128)(2,1)S(1)}, bf16[136,1024]{1,0:T(8,128)(2,1)S(1)}, u32[]{:S(2)}, u32[]{:S(2)}) collective-permute-start(bf16[136,1024]{1,0:T(8,128)(2,1)S(1)} %attend2.1), channel_id=1, source_target_pairs={{16,0},{24,8},{0,16},{8,24},{17,1},{25,9},{1,17},{9,25},{18,2},{26... | collective-permute-start | bytes 835592 | tf_op jit(solution)/shard_map/ppermute | solution.py:242

commit v2 on v1

--- a/solution.py
+++ b/solution.py
@@ -36,7 +36,7 @@
     return hi, mid, rest - mid
 
 
-def prep_kernel(own_ids, peer_ids, cached, counts, k0, k1, v0, v1, list_ref, k_ref, v_ref):
+def select_kernel(own_ids, peer_ids, cached, counts, list_ref):
     blocks_per_seq = (BOTH * 64) // SEQS
     found = []
     for b in range(BOTH):
@@ -65,10 +65,12 @@
         list_ref[2, 16 + s] += hit.astype(jnp.int32)
     list_ref[2, 31] = pairs
 
+
+def pack_kernel(lists, k0, k1, v0, v1, k_ref, v_ref):
     def place_pair(p, _):
         for i in range(2):
             here = slice(i * BLK, (i + 1) * BLK)
-            b = list_ref[0, 2 * p + i]
+            b = lists[0, 2 * p + i]
 
             def put(k_from, v_from, first):
                 rows = pl.ds(pl.multiple_of((b - first) * BLK, BLK), BLK)
@@ -80,7 +82,7 @@
             pl.when(b >= OWN)(lambda: put(k1, v1, OWN))
         return 0
 
-    lax.fori_loop(0, pairs, place_pair, 0)
+    lax.fori_loop(0, lists[2, 31], place_pair, 0)
 
 
 def attend_kernel(steps, *refs):
@@ -254,26 +256,35 @@
     )
     place = jnp.stack([lax.axis_index(a).astype(jnp.int32) for a in ("z", "y", "xh", "core")])
 
+    lists = pl.pallas_call(
+        select_kernel,
+        out_shape=jax.ShapeDtypeStruct((3, 32), jnp.int32),
+        in_specs=[SMEM] * 4,
+        out_specs=SMEM,
+        compiler_params=params(12),
+        name="select",
+    )(block_owner, ids, cached_lens, new_counts)
+
     q = jnp.broadcast_to(queries[None], (8,) + queries.shape)
     q = lax.all_to_all(q, "z", split_axis=0, concat_axis=0, tiled=True)
-    lists, k, v = pl.pallas_call(
-        prep_kernel,
+    q, lists = lax.optimization_barrier((q, lists))
+    k, v = pl.pallas_call(
+        pack_kernel,
         out_shape=[
-            jax.ShapeDtypeStruct((3, 32), jnp.int32),
             jax.ShapeDtypeStruct((PAIRS, HEADS, 2 * BLK, HD), jnp.bfloat16),
             jax.ShapeDtypeStruct((PAIRS, HEADS, HD, 2 * BLK), jnp.bfloat16),
         ],
-        in_specs=[SMEM] * 4 + [VMEM] * 4,
-        out_specs=[SMEM, VMEM, VMEM],
-        compiler_params=params(8),
+        in_specs=[SMEM] + [VMEM] * 4,
+        out_specs=[VMEM, VMEM],
+        compiler_params=params(12),
         cost_estimate=COST,
-        name="prep",
-    )(block_owner, ids, cached_lens, new_counts, k0, k1, v0, v1)
-
-    q, lists, k, v = lax.optimization_barrier((q, lists, k, v))
-    both = [q, turn(q, "xh", 2, 1)]
-    near, back = ([turn(x, "y", 4, n) for x in both] for n in (1, 3))
-    qs = [both, near, [turn(near[0], "y", 4, 1), turn(back[1], "y", 4, 3)], back]
+        name="pack",
+    )(lists, k0, k1, v0, v1)
+    over, near, back, k, v = lax.optimization_barrier(
+        (turn(q, "xh", 2, 1), turn(q, "y", 4, 1), turn(q, "y", 4, 3), k, v)
+    )
+    near, back = [near, turn(over, "y", 4, 1)], [back, turn(over, "y", 4, 3)]
+    qs = [[q, over], near, [turn(near[0], "y", 4, 1), turn(back[1], "y", 4, 3)], back]
 
     def attend(place, *steps):
         n = len(steps)
@@ -302,7 +313,7 @@
         out_shape=jax.ShapeDtypeStruct((MSG, 8 * BLK), jnp.float32),
         in_specs=[VMEM] * 2,
         out_specs=VMEM,
-        compiler_params=params(8),
+        compiler_params=params(12),
         cost_estimate=COST,
         name="join",
     )(turn(msg1, "y", 4, -1), turn(msg3, "y", 4, -3))
@@ -311,7 +322,7 @@
         out_shape=jax.ShapeDtypeStruct((32, LAST, HD), jnp.bfloat16),
         in_specs=[SMEM] + [VMEM] * 3,
         out_specs=VMEM,
-        compiler_params=params(8),
+        compiler_params=params(12),
         name="fold",
     )(place, joined, msg0, turn(msg2, "y", 4, -2))
     msg = lax.all_to_all(msg, ("z", "xh", "kvh"), split_axis=0, concat_axis=0, tiled=True)
@@ -320,7 +331,7 @@
         out_shape=jax.ShapeDtypeStruct((1, 64, HD), jnp.bfloat16),
         in_specs=[VMEM],
         out_specs=VMEM,
-        compiler_params=params(4),
+        compiler_params=params(12),
         name="finish",
     )(msg)
 

time: 75.7 us -> 75.2 us (level)
  blocking collectives: 21.6 us -> 18.1 us
  waiting for transfers between devices: 10.2 us -> 13.3 us
  starting transfers between devices: 26.1 us -> 24.1 us
  local copies, waits for them, and re-layouts: 6.34 us -> 7.89 us
    all_to_all x1, blocking collectives: 21.6 us -> 18.1 us  [per_device(): lax.all_to_all(msg, ('z', 'xh', 'kvh'), split_axis=0, concat_axis=0, tile...]
    ppermute x13, waiting for transfers between devices: 8.16 us -> 10.6 us  [turn(): return lax.ppermute(x, axis, [((i + step) % size, i) for i in range(size)])]
    ppermute x13, starting transfers between devices: 17.5 us -> 15.5 us  [turn(): return lax.ppermute(x, axis, [((i + step) % size, i) for i in range(size)])]
    unnamed x10 -> x14, local copies, waits for them, and re-layouts: 3.18 us -> 4.73 us
    pallas_call x1 -> x2, Pallas kernels: 2.59 us -> 3.13 us  [the longest x1 1.91 us: per_device(): pl.pallas_call(select_kernel, out_shape=jax.ShapeDtypeStruct((3, 32), jnp...]
  transfers between devices with their start and end apart: 14 -> 14, of which waited for: 7 -> 6; matrix products, arithmetic and copies ran while one was open for 4% -> 4% of each run, Pallas kernels for 11% -> 12%
where the time goes in v2:
time: 75.2 us; the launch traced here: 74.4 us
  starting transfers between devices  24.1 us (32%)
  blocking collectives  18.1 us (24%)
  waiting for transfers between devices  13.3 us (18%)
  Pallas kernels  10.8 us (14%)
  local copies, waits for them, and re-layouts  7.89 us (10%)
    all_to_all x1, blocking collectives, per_device(): lax.all_to_all(msg, ('z', 'xh', 'kvh'), split_axis=0, concat_axis=0, tile...  18.1 us
    ppermute x13, starting transfers between devices, turn(): return lax.ppermute(x, axis, [((i + step) % size, i) for i in range(size)])  15.5 us
    ppermute x13, waiting for transfers between devices, turn(): return lax.ppermute(x, axis, [((i + step) % size, i) for i in range(size)])  10.6 us
    all_to_all x1, starting transfers between devices, per_device(): q = lax.all_to_all(q, 'z', split_axis=0, concat_axis=0, tiled=True)  8.57 us
    pallas_call x3, Pallas kernels, attend(): pl.pallas_call(functools.partial(attend_kernel, steps), out_shape=[jax.Sh...  5.63 us
    unnamed x14, local copies, waits for them, and re-layouts  4.73 us
    all_to_all x1, waiting for transfers between devices, per_device(): q = lax.all_to_all(q, 'z', split_axis=0, concat_axis=0, tiled=True)  2.64 us
    pallas_call x1, Pallas kernels, per_device(): pl.pallas_call(select_kernel, out_shape=jax.ShapeDtypeStruct((3, 32), jnp...  1.91 us
  transfers between devices with their start and end apart: 14, of which 6 were waited for; matrix products, arithmetic and copies ran while one was open for 4% of the time, Pallas kernels for 12%

profile of v2, /device:TPU:32, one launch (start us, length us, event | category | flops | bytes accessed | tf_op | source)
XLA Modules:
  0.0 74.4 jit_solution(13700018598141606122)
XLA Ops:
  0.0 0.5 collective-permute-start.4
  0.5 1.4 %broadcast_in_dim.2 = bf16[8,2,2,16,128]{4,3,2,1,0:T(8,128)(2,1)} broadcast(bf16[2,2,16,128]{3,2,1,0:T(8,128)(2,1)} %param.6), dimensions={1,2,3,4} | broadcast | bytes 147456 | tf_op jit(solution)/shard_map/broadcast_in_dim | solution.py:268
  1.9 8.6 %all-to-all-start = ((bf16[8,2,2,16,128]{4,3,2,1,0:T(8,128)(2,1)}), bf16[8,2,2,16,128]{4,3,2,1,0:T(8,128)(2,1)S(1)}, u32[]{:S(2)}, u32[]{:S(2)}) async-start(bf16[8,2,2,16,128]{4,3,2,1,0:T(8,128)(2,1)} %broadcast_in_dim.2), calls=%async_computation | async-start | bytes 262144 | tf_op jit(solution)/shard_map/all_to_all | solution.py:269
  10.5 1.3 %collective-permute-done.peer_ids = s32[12]{0:T(128)S(1)} collective-permute-done((s32[12]{0:T(128)}, s32[12]{0:T(128)S(1)}, u32[]{:S(2)}, u32[]{:S(2)}) %collective-permute-start) | collective-permute-done | bytes 80 | tf_op jit(solution)/shard_map/ppermute | solution.py:244
  11.7 0.7 copy-done.2
  12.4 0.7 copy-done.4
  13.0 0.7 copy-done.6
  13.7 1.9 %select.1.lists.refs_0_ = s32[3,32]{1,0:T(4,128)S(1)} custom-call(s32[12]{0:T(128)S(1)} %copy-done.6, s32[12]{0:T(128)S(1)} %collective-permute-done.peer_ids, s32[4]{0:T(128)S(1)} %copy-done.2, s32[4]{0:T(128)S(1)} %copy-done.4), custom_call_target="tpu_custom_call" | custom-call | tf_op jit(solution)/shard_map/select/pallas_call | solution.py:259
  15.6 2.6 %all-to-all-done.refs_4_ = bf16[8,2,2,16,128]{4,3,2,1,0:T(8,128)(2,1)S(1)} async-done(((bf16[8,2,2,16,128]{4,3,2,1,0:T(8,128)(2,1)}), bf16[8,2,2,16,128]{4,3,2,1,0:T(8,128)(2,1)S(1)}, u32[]{:S(2)}, u32[]{:S(2)}) %all-to-all-start) | async-done | bytes 131104 | tf_op jit(solution)/shard_map/all_to_all | solution.py:269
  18.2 3.0 %collective-permute-start.1 = (bf16[8,2,2,16,128]{4,3,2,1,0:T(8,128)(2,1)S(1)}, bf16[8,2,2,16,128]{4,3,2,1,0:T(8,128)(2,1)S(1)}, u32[]{:S(2)}, u32[]{:S(2)}) collective-permute-start(bf16[8,2,2,16,128]{4,3,2,1,0:T(8,128)(2,1)S(1)} %all-to-all-done.refs_4_), channel_id=1, source_target_pairs={{4,0},{0,4},{5,1},{1,5},{6,2},{2,6},{7,3},{3,7},{12,8},{8,12},{13,... | collective-permute-start | bytes 393224 | tf_op jit(solution)/shard_map/ppermute | solution.py:244
  21.3 3.0 %collective-permute-start.2 = (bf16[8,2,2,16,128]{4,3,2,1,0:T(8,128)(2,1)S(1)}, bf16[8,2,2,16,128]{4,3,2,1,0:T(8,128)(2,1)S(1)}, u32[]{:S(2)}, u32[]{:S(2)}) collective-permute-start(bf16[8,2,2,16,128]{4,3,2,1,0:T(8,128)(2,1)S(1)} %all-to-all-done.refs_4_), channel_id=1, source_target_pairs={{8,0},{16,8},{24,16},{0,24},{9,1},{17,9},{25,17},{1,25},{10,2},{18... | collective-permute-start | bytes 393224 | tf_op jit(solution)/shard_map/ppermute | solution.py:244
  24.3 1.6 %copy_bitcast_fusion.1 = (bf16[2,1536,128]{2,1,0:T(8,128)(2,1)S(1)}, bf16[2,1536,128]{2,1,0:T(8,128)(2,1)S(1)}) fusion(bf16[1536,2,128]{2,1,0:T(2,128)(2,1)} %param.8, bf16[1536,2,128]{2,1,0:T(2,128)(2,1)} %param.7), kind=kLoop, calls=%fused_computation.1 | loop fusion | bytes 3145728 | tf_op jit(solution)/shard_map/transpose | solution.py:255
  25.9 0.1 copy.17
  26.0 0.1 copy.18
  26.1 1.2 %pack.1 = (bf16[14,2,256,128]{3,2,1,0:T(8,128)(2,1)S(1)}, bf16[14,2,128,256]{3,2,1,0:T(8,128)(2,1)S(1)}) custom-call(s32[3,32]{1,0:T(4,128)S(1)} %select.1.lists.refs_0_, bf16[2,1536,128]{2,1,0:T(8,128)(2,1)S(1)} %get-tuple-element.28.k0, bf16[2,1536,128]{2,1,0:T(8,128)(2,1)S(1)} %bitcast.19, bf16[2,1536,128]{2,1,0:T(8,128)(2,1)S(1)} %get-tuple-element.27.v0, ...), custom_call_target="tpu_custom_call" | custom-call | flops 1000000000 | bytes 4194304 | tf_op jit(solution)/shard_map/pack/pallas_call | solution.py:271
  27.4 1.3 %copy-done = bf16[14,2,128,256]{3,2,1,0:T(8,128)(2,1)} copy-done((bf16[14,2,128,256]{3,2,1,0:T(8,128)(2,1)}, bf16[14,2,128,256]{3,2,1,0:T(8,128)(2,1)S(1)}, u32[]{:S(2)}) %copy-start) | copy-done | bytes 1835032
  28.6 1.8 %collective-permute-done.3.refs_6_ = bf16[8,2,2,16,128]{4,3,2,1,0:T(8,128)(2,1)S(1)} collective-permute-done((bf16[8,2,2,16,128]{4,3,2,1,0:T(8,128)(2,1)S(1)}, bf16[8,2,2,16,128]{4,3,2,1,0:T(8,128)(2,1)S(1)}, u32[]{:S(2)}, u32[]{:S(2)}) %collective-permute-start.3) | collective-permute-done | bytes 131104 | tf_op jit(solution)/shard_map/ppermute | solution.py:244
  30.5 3.2 %collective-permute-start.6 = (bf16[8,2,2,16,128]{4,3,2,1,0:T(8,128)(2,1)S(1)}, bf16[8,2,2,16,128]{4,3,2,1,0:T(8,128)(2,1)S(1)}, u32[]{:S(2)}, u32[]{:S(2)}) collective-permute-start(bf16[8,2,2,16,128]{4,3,2,1,0:T(8,128)(2,1)S(1)} %collective-permute-done.1.refs_5_), channel_id=1, source_target_pairs={{8,0},{16,8},{24,16},{0,24},{9,1},{17,9},{25,17},{1,25},{10,2},{18... | collective-permute-start | bytes 393224 | tf_op jit(solution)/shard_map/ppermute | solution.py:244
  33.7 0.3 collective-permute-start.10
  34.0 3.3 %collective-permute-done.7.refs_7_ = bf16[8,2,2,16,128]{4,3,2,1,0:T(8,128)(2,1)S(1)} collective-permute-done((bf16[8,2,2,16,128]{4,3,2,1,0:T(8,128)(2,1)S(1)}, bf16[8,2,2,16,128]{4,3,2,1,0:T(8,128)(2,1)S(1)}, u32[]{:S(2)}, u32[]{:S(2)}) %collective-permute-start.7) | collective-permute-done | bytes 131104 | tf_op jit(solution)/shard_map/ppermute | solution.py:244
  37.4 1.5 %copy-done.1 = bf16[14,2,128,256]{3,2,1,0:T(8,128)(2,1)S(1)} copy-done((bf16[14,2,128,256]{3,2,1,0:T(8,128)(2,1)S(1)}, bf16[14,2,128,256]{3,2,1,0:T(8,128)(2,1)}, u32[]{:S(2)}) %copy-start.1) | copy-done | bytes 1835032
  38.9 2.1 %attend13.1 = (bf16[136,1024]{1,0:T(8,128)(2,1)S(1)}, bf16[136,1024]{1,0:T(8,128)(2,1)S(1)}) custom-call(s32[3,32]{1,0:T(4,128)S(1)} %select.1.lists.refs_0_, s32[4]{0:T(128)S(1)} %copy-done.3, s32[4]{0:T(128)S(1)} %copy-done.5, s32[4]{0:T(128)S(1)} %pad_add_fusion.refs_3_.place, bf16[8,2,2,16,128]{4,3,2,1,0:T(8,128)(2,1)S(1)} %collective-permute-done.2.refs_4_, ...), custom_call_target="tpu_custom_call" | custom-call | flops 1000000000 | bytes 4194304 | tf_op jit(solution)/shard_map/attend13/pallas_call | solution.py:292
  41.2 3.3 %collective-permute-start.9 = (bf16[136,1024]{1,0:T(8,128)(2,1)S(1)}, bf16[136,1024]{1,0:T(8,128)(2,1)S(1)}, u32[]{:S(2)}, u32[]{:S(2)}) collective-permute-start(bf16[136,1024]{1,0:T(8,128)(2,1)S(1)} %get-tuple-element.26), channel_id=1, source_target_pairs={{8,0},{16,8},{24,16},{0,24},{9,1},{17,9},{25,17},{1,25},{10,2},{18... | collective-permute-start | bytes 835592 | tf_op jit(solution)/shard_map/ppermute | solution.py:244
  44.5 1.7 %attend2.1 = bf16[136,1024]{1,0:T(8,128)(2,1)S(1)} custom-call(s32[3,32]{1,0:T(4,128)S(1)} %select.1.lists.refs_0_, s32[4]{0:T(128)S(1)} %copy-done.3, s32[4]{0:T(128)S(1)} %copy-done.5, s32[4]{0:T(128)S(1)} %pad_add_fusion.refs_3_.place, bf16[8,2,2,16,128]{4,3,2,1,0:T(8,128)(2,1)S(1)} %collective-permute-done.10.refs_4_, ...), custom_call_target="tpu_custom_call" | custom-call | flops 1000000000 | bytes 4194304 | tf_op jit(solution)/shard_map/attend2/pallas_call | solution.py:292
  46.2 2.1 %collective-permute-start.12 = (bf16[136,1024]{1,0:T(8,128)(2,1)S(1)}, bf16[136,1024]{1,0:T(8,128)(2,1)S(1)}, u32[]{:S(2)}, u32[]{:S(2)}) collective-permute-start(bf16[136,1024]{1,0:T(8,128)(2,1)S(1)} %attend2.1), channel_id=1, source_target_pairs={{16,0},{24,8},{0,16},{8,24},{17,1},{25,9},{1,17},{9,25},{18,2},{26... | collective-permute-start | bytes 835592 | tf_op jit(solution)/shard_map/ppermute | solution.py:244
  48.3 1.7 %attend0.1.in0 = bf16[136,1024]{1,0:T(8,128)(2,1)S(1)} custom-call(s32[3,32]{1,0:T(4,128)S(1)} %select.1.lists.refs_0_, s32[4]{0:T(128)S(1)} %copy-done.3, s32[4]{0:T(128)S(1)} %copy-done.5, s32[4]{0:T(128)S(1)} %pad_add_fusion.refs_3_.place, bf16[8,2,2,16,128]{4,3,2,1,0:T(8,128)(2,1)S(1)} %all-to-all-done.refs_4_, ...), custom_call_target="tpu_custom_call" | custom-call | flops 1000000000 | bytes 4194304 | tf_op jit(solution)/shard_map/attend0/pallas_call | solution.py:292
  50.0 1.3 %collective-permute-done.8.in0 = bf16[136,1024]{1,0:T(8,128)(2,1)S(1)} collective-permute-done((bf16[136,1024]{1,0:T(8,128)(2,1)S(1)}, bf16[136,1024]{1,0:T(8,128)(2,1)S(1)}, u32[]{:S(2)}, u32[]{:S(2)}) %collective-permute-start.8) | collective-permute-done | bytes 278560 | tf_op jit(solution)/shard_map/ppermute | solution.py:244
  51.3 0.1 join.1.joined
  51.5 2.9 %collective-permute-done.12.in1 = bf16[136,1024]{1,0:T(8,128)(2,1)S(1)} collective-permute-done((bf16[136,1024]{1,0:T(8,128)(2,1)S(1)}, bf16[136,1024]{1,0:T(8,128)(2,1)S(1)}, u32[]{:S(2)}, u32[]{:S(2)}) %collective-permute-start.12) | collective-permute-done | bytes 278560 | tf_op jit(solution)/shard_map/ppermute | solution.py:244
  54.4 0.8 %fold.1 = bf16[32,40,128]{2,1,0:T(8,128)(2,1)S(1)} custom-call(s32[4]{0:T(128)S(1)} %pad_add_fusion.refs_3_.place, f32[136,1024]{1,0:T(8,128)S(1)} %join.1.joined, bf16[136,1024]{1,0:T(8,128)(2,1)S(1)} %attend0.1.in0, bf16[136,1024]{1,0:T(8,128)(2,1)S(1)} %collective-permute-done.12.in1), custom_call_target="tpu_custom_call" | custom-call | tf_op jit(solution)/shard_map/fold/pallas_call | solution.py:320
  55.2 18.1 %all_to_all.10.in_ref = bf16[32,40,128]{2,1,0:T(8,128)(2,1)S(1)} all-to-all(bf16[32,40,128]{2,1,0:T(8,128)(2,1)S(1)} %fold.1), channel_id=1, replica_groups=mesh['z'=8,'y'=4,'xh'=2,'core'=2,'kvh'=2] {'z','xh','kvh'}, dimensions={0} | all-to-all | bytes 655360 | tf_op jit(solution)/shard_map/all_to_all | solution.py:328
  73.3 1.1 %finish.1 = bf16[1,64,128]{2,1,0:T(8,128)(2,1)} custom-call(bf16[32,40,128]{2,1,0:T(8,128)(2,1)S(1)} %all_to_all.10.in_ref), custom_call_target="tpu_custom_call" | custom-call | tf_op jit(solution)/shard_map/finish/pallas_call | solution.py:329
  (24 shorter events, 0.2 us)
Async XLA Ops:
  0.0 25.9 %collective-permute-start.5 = (bf16[3072,128]{1,0:T(8,128)(2,1)}, bf16[3072,128]{1,0:T(8,128)(2,1)S(1)}, u32[]{:S(2)}, u32[]{:S(2)}) collective-permute-start(bf16[3072,128]{1,0:T(8,128)(2,1)} %bitcast.22), channel_id=1, source_target_pairs={{2,0},{0,2},{3,1},{1,3},{6,4},{4,6},{7,5},{5,7},{10,8},{8,10},{11,... | collective-permute-start | bytes 2359304 | tf_op jit(solution)/shard_map/ppermute | solution.py:244
  0.0 26.0 %collective-permute-start.4 = (bf16[3072,128]{1,0:T(8,128)(2,1)}, bf16[3072,128]{1,0:T(8,128)(2,1)S(1)}, u32[]{:S(2)}, u32[]{:S(2)}) collective-permute-start(bf16[3072,128]{1,0:T(8,128)(2,1)} %bitcast.23), channel_id=1, source_target_pairs={{2,0},{0,2},{3,1},{1,3},{6,4},{4,6},{7,5},{5,7},{10,8},{8,10},{11,... | collective-permute-start | bytes 2359304 | tf_op jit(solution)/shard_map/ppermute | solution.py:244
  1.9 16.3 %all-to-all-start = ((bf16[8,2,2,16,128]{4,3,2,1,0:T(8,128)(2,1)}), bf16[8,2,2,16,128]{4,3,2,1,0:T(8,128)(2,1)S(1)}, u32[]{:S(2)}, u32[]{:S(2)}) async-start(bf16[8,2,2,16,128]{4,3,2,1,0:T(8,128)(2,1)} %broadcast_in_dim.2), calls=%async_computation | async-start | bytes 262144 | tf_op jit(solution)/shard_map/all_to_all | solution.py:269
  10.5 1.3 %collective-permute-start = (s32[12]{0:T(128)}, s32[12]{0:T(128)S(1)}, u32[]{:S(2)}, u32[]{:S(2)}) collective-permute-start(s32[12]{0:T(128)} %own_ids.1), channel_id=1, source_target_pairs={{2,0},{0,2},{3,1},{1,3},{6,4},{4,6},{7,5},{5,7},{10,8},{8,10},{11,... | collective-permute-start | bytes 152 | tf_op jit(solution)/shard_map/ppermute | solution.py:244
  11.7 0.7 copy-start.2
  12.4 0.7 copy-start.4
  13.0 0.7 copy-start.6
  18.2 10.4 %collective-permute-start.1 = (bf16[8,2,2,16,128]{4,3,2,1,0:T(8,128)(2,1)S(1)}, bf16[8,2,2,16,128]{4,3,2,1,0:T(8,128)(2,1)S(1)}, u32[]{:S(2)}, u32[]{:S(2)}) collective-permute-start(bf16[8,2,2,16,128]{4,3,2,1,0:T(8,128)(2,1)S(1)} %all-to-all-done.refs_4_), channel_id=1, source_target_pairs={{4,0},{0,4},{5,1},{1,5},{6,2},{2,6},{7,3},{3,7},{12,8},{8,12},{13,... | collective-permute-start | bytes 393224 | tf_op jit(solution)/shard_map/ppermute | solution.py:244
  21.3 7.4 %collective-permute-start.2 = (bf16[8,2,2,16,128]{4,3,2,1,0:T(8,128)(2,1)S(1)}, bf16[8,2,2,16,128]{4,3,2,1,0:T(8,128)(2,1)S(1)}, u32[]{:S(2)}, u32[]{:S(2)}) collective-permute-start(bf16[8,2,2,16,128]{4,3,2,1,0:T(8,128)(2,1)S(1)} %all-to-all-done.refs_4_), channel_id=1, source_target_pairs={{8,0},{16,8},{24,16},{0,24},{9,1},{17,9},{25,17},{1,25},{10,2},{18... | collective-permute-start | bytes 393224 | tf_op jit(solution)/shard_map/ppermute | solution.py:244
  24.3 6.2 %collective-permute-start.3 = (bf16[8,2,2,16,128]{4,3,2,1,0:T(8,128)(2,1)S(1)}, bf16[8,2,2,16,128]{4,3,2,1,0:T(8,128)(2,1)S(1)}, u32[]{:S(2)}, u32[]{:S(2)}) collective-permute-start(bf16[8,2,2,16,128]{4,3,2,1,0:T(8,128)(2,1)S(1)} %all-to-all-done.refs_4_), channel_id=1, source_target_pairs={{24,0},{0,8},{8,16},{16,24},{25,1},{1,9},{9,17},{17,25},{26,2},{2,... | collective-permute-start | bytes 393224 | tf_op jit(solution)/shard_map/ppermute | solution.py:244
  26.1 11.3 %copy-start.3 = (s32[4]{0:T(128)S(1)}, s32[4]{0:T(128)}, u32[]{:S(2)}) copy-start(s32[4]{0:T(128)} %refs_1_.5) | copy-start | bytes 52
  26.1 11.3 %copy-start.5 = (s32[4]{0:T(128)S(1)}, s32[4]{0:T(128)}, u32[]{:S(2)}) copy-start(s32[4]{0:T(128)} %refs_2_.5) | copy-start | bytes 52
  27.4 1.3 %copy-start = (bf16[14,2,128,256]{3,2,1,0:T(8,128)(2,1)}, bf16[14,2,128,256]{3,2,1,0:T(8,128)(2,1)S(1)}, u32[]{:S(2)}) copy-start(bf16[14,2,128,256]{3,2,1,0:T(8,128)(2,1)S(1)} %get-tuple-element.24.refs_9_.refs_7_) | copy-start | bytes 5505028
  30.5 6.9 %collective-permute-start.7 = (bf16[8,2,2,16,128]{4,3,2,1,0:T(8,128)(2,1)S(1)}, bf16[8,2,2,16,128]{4,3,2,1,0:T(8,128)(2,1)S(1)}, u32[]{:S(2)}, u32[]{:S(2)}) collective-permute-start(bf16[8,2,2,16,128]{4,3,2,1,0:T(8,128)(2,1)S(1)} %collective-permute-done.1.refs_5_), channel_id=1, source_target_pairs={{24,0},{0,8},{8,16},{16,24},{25,1},{1,9},{9,17},{17,25},{26,2},{2,... | collective-permute-start | bytes 393224 | tf_op jit(solution)/shard_map/ppermute | solution.py:244
  30.5 6.9 %collective-permute-start.6 = (bf16[8,2,2,16,128]{4,3,2,1,0:T(8,128)(2,1)S(1)}, bf16[8,2,2,16,128]{4,3,2,1,0:T(8,128)(2,1)S(1)}, u32[]{:S(2)}, u32[]{:S(2)}) collective-permute-start(bf16[8,2,2,16,128]{4,3,2,1,0:T(8,128)(2,1)S(1)} %collective-permute-done.1.refs_5_), channel_id=1, source_target_pairs={{8,0},{16,8},{24,16},{0,24},{9,1},{17,9},{25,17},{1,25},{10,2},{18... | collective-permute-start | bytes 393224 | tf_op jit(solution)/shard_map/ppermute | solution.py:244
  33.7 10.8 %collective-permute-start.10 = (bf16[8,2,2,16,128]{4,3,2,1,0:T(8,128)(2,1)S(1)}, bf16[8,2,2,16,128]{4,3,2,1,0:T(8,128)(2,1)S(1)}, u32[]{:S(2)}, u32[]{:S(2)}) collective-permute-start(bf16[8,2,2,16,128]{4,3,2,1,0:T(8,128)(2,1)S(1)} %collective-permute-done.2.refs_4_), channel_id=1, source_target_pairs={{8,0},{16,8},{24,16},{0,24},{9,1},{17,9},{25,17},{1,25},{10,2},{18... | collective-permute-start | bytes 393224 | tf_op jit(solution)/shard_map/ppermute | solution.py:244
  37.3 7.2 %collective-permute-start.11 = (bf16[8,2,2,16,128]{4,3,2,1,0:T(8,128)(2,1)S(1)}, bf16[8,2,2,16,128]{4,3,2,1,0:T(8,128)(2,1)S(1)}, u32[]{:S(2)}, u32[]{:S(2)}) collective-permute-start(bf16[8,2,2,16,128]{4,3,2,1,0:T(8,128)(2,1)S(1)} %collective-permute-done.7.refs_7_), channel_id=1, source_target_pairs={{24,0},{0,8},{8,16},{16,24},{25,1},{1,9},{9,17},{17,25},{26,2},{2,... | collective-permute-start | bytes 393224 | tf_op jit(solution)/shard_map/ppermute | solution.py:244
  37.4 1.5 %copy-start.1 = (bf16[14,2,128,256]{3,2,1,0:T(8,128)(2,1)S(1)}, bf16[14,2,128,256]{3,2,1,0:T(8,128)(2,1)}, u32[]{:S(2)}) copy-start(bf16[14,2,128,256]{3,2,1,0:T(8,128)(2,1)} %copy-done) | copy-start | bytes 5505028
  41.1 10.3 %collective-permute-start.8 = (bf16[136,1024]{1,0:T(8,128)(2,1)S(1)}, bf16[136,1024]{1,0:T(8,128)(2,1)S(1)}, u32[]{:S(2)}, u32[]{:S(2)}) collective-permute-start(bf16[136,1024]{1,0:T(8,128)(2,1)S(1)} %get-tuple-element.25), channel_id=1, source_target_pairs={{24,0},{0,8},{8,16},{16,24},{25,1},{1,9},{9,17},{17,25},{26,2},{2,... | collective-permute-start | bytes 835592 | tf_op jit(solution)/shard_map/ppermute | solution.py:244
  41.2 10.2 %collective-permute-start.9 = (bf16[136,1024]{1,0:T(8,128)(2,1)S(1)}, bf16[136,1024]{1,0:T(8,128)(2,1)S(1)}, u32[]{:S(2)}, u32[]{:S(2)}) collective-permute-start(bf16[136,1024]{1,0:T(8,128)(2,1)S(1)} %get-tuple-element.26), channel_id=1, source_target_pairs={{8,0},{16,8},{24,16},{0,24},{9,1},{17,9},{25,17},{1,25},{10,2},{18... | collective-permute-start | bytes 835592 | tf_op jit(solution)/shard_map/ppermute | solution.py:244
  46.2 8.1 %collective-permute-start.12 = (bf16[136,1024]{1,0:T(8,128)(2,1)S(1)}, bf16[136,1024]{1,0:T(8,128)(2,1)S(1)}, u32[]{:S(2)}, u32[]{:S(2)}) collective-permute-start(bf16[136,1024]{1,0:T(8,128)(2,1)S(1)} %attend2.1), channel_id=1, source_target_pairs={{16,0},{24,8},{0,16},{8,24},{17,1},{25,9},{1,17},{9,25},{18,2},{26... | collective-permute-start | bytes 835592 | tf_op jit(solution)/shard_map/ppermute | solution.py:244

commit v3 on v2

--- a/solution.py
+++ b/solution.py
@@ -87,17 +87,17 @@
 
 def attend_kernel(steps, *refs):
     n = len(steps)
-    lists, cached, counts, place = refs[:4]
-    q_refs, (k_ref, v_ref) = refs[4:4 + 2 * n], refs[4 + 2 * n:6 + 2 * n]
-    out_refs, (m_ref, l_ref, acc_ref, t_ref) = refs[6 + 2 * n:6 + 3 * n], refs[6 + 3 * n:]
+    lists, cached, counts = refs[:3]
+    q_refs, (k_ref, v_ref) = refs[3:3 + 2 * n], refs[3 + 2 * n:5 + 2 * n]
+    out_refs, (m_ref, l_ref, acc_ref, t_ref) = refs[5 + 2 * n:5 + 3 * n], refs[5 + 3 * n:]
     rows = BLK * n
     lane = lax.broadcasted_iota(jnp.int32, (1, rows), 1)
     far = steps[0] if n == 1 else jnp.where(lane < BLK, steps[0], steps[1])
     within = (
         32 * ((lane >> 5) & 1)
-        + 8 * ((place[1] + far) & 3)
-        + 4 * (((lane >> 6) + place[2]) & 1)
-        + 2 * place[3]
+        + 8 * ((lax.axis_index("y") + far) & 3)
+        + 4 * (((lane >> 6) + lax.axis_index("xh")) & 1)
+        + 2 * lax.axis_index("core")
         + ((lane >> 4) & 1)
     )
     slot = lax.broadcasted_iota(jnp.int32, (BLK, rows), 0)
@@ -185,9 +185,9 @@
         )
 
 
-def fold_kernel(place, joined, in0, in1, out_ref):
+def fold_kernel(joined, in0, in1, out_ref):
     def dest(s, e):
-        return 8 * s + 4 * ((e >> 1) & 1) + 2 * ((place[2] + (e >> 2)) & 1) + (e & 1)
+        return 8 * s + 4 * ((e >> 1) & 1) + 2 * ((lax.axis_index("xh") + (e >> 2)) & 1) + (e & 1)
 
     for s in range(SEQS):
         tails = []
@@ -251,10 +251,6 @@
 def per_device(queries, k_cache, v_cache, block_owner, cached_lens, new_counts):
     k0, v0 = (x.reshape(OWN * WIDE, HD) for x in (k_cache, v_cache))
     k1, v1, ids = (turn(x, "core", 2, 1) for x in (k0, v0, block_owner))
-    k0, k1, v0, v1 = (
-        jnp.transpose(x.reshape(OWN * BLK, HEADS, HD), (1, 0, 2)) for x in (k0, k1, v0, v1)
-    )
-    place = jnp.stack([lax.axis_index(a).astype(jnp.int32) for a in ("z", "y", "xh", "core")])
 
     lists = pl.pallas_call(
         select_kernel,
@@ -267,7 +263,10 @@
 
     q = jnp.broadcast_to(queries[None], (8,) + queries.shape)
     q = lax.all_to_all(q, "z", split_axis=0, concat_axis=0, tiled=True)
-    q, lists = lax.optimization_barrier((q, lists))
+    q, lists, *caches = lax.optimization_barrier((q, lists, k0, k1, v0, v1))
+    k0, k1, v0, v1 = (
+        jnp.transpose(x.reshape(OWN * BLK, HEADS, HD), (1, 0, 2)) for x in caches
+    )
     k, v = pl.pallas_call(
         pack_kernel,
         out_shape=[
@@ -286,13 +285,13 @@
     near, back = [near, turn(over, "y", 4, 1)], [back, turn(over, "y", 4, 3)]
     qs = [[q, over], near, [turn(near[0], "y", 4, 1), turn(back[1], "y", 4, 3)], back]
 
-    def attend(place, *steps):
+    def attend(*steps):
         n = len(steps)
         rows = n * BLK
         return pl.pallas_call(
             functools.partial(attend_kernel, steps),
             out_shape=[jax.ShapeDtypeStruct((MSG, 8 * BLK), jnp.bfloat16)] * n,
-            in_specs=[SMEM] * 4 + [VMEM] * (2 * n + 2),
+            in_specs=[SMEM] * 3 + [VMEM] * (2 * n + 2),
             out_specs=[VMEM] * n,
             scratch_shapes=[
                 pltpu.VMEM((UNITS, 8, rows), jnp.float32),
@@ -303,11 +302,11 @@
             compiler_params=params(12),
             cost_estimate=COST,
             name="attend" + "".join(map(str, steps)),
-        )(lists, cached_lens, new_counts, place, *[x for i in steps for x in qs[i]], k, v)
-
-    msg1, msg3 = attend(place, 1, 3)
-    (msg2,) = attend(place, 2)
-    (msg0,) = attend(place, 0)
+        )(lists, cached_lens, new_counts, *[x for i in steps for x in qs[i]], k, v)
+
+    msg1, msg3 = attend(1, 3)
+    (msg2,) = attend(2)
+    (msg0,) = attend(0)
     joined = pl.pallas_call(
         join_kernel,
         out_shape=jax.ShapeDtypeStruct((MSG, 8 * BLK), jnp.float32),
@@ -320,11 +319,11 @@
     msg = pl.pallas_call(
         fold_kernel,
         out_shape=jax.ShapeDtypeStruct((32, LAST, HD), jnp.bfloat16),
-        in_specs=[SMEM] + [VMEM] * 3,
+        in_specs=[VMEM] * 3,
         out_specs=VMEM,
         compiler_params=params(12),
         name="fold",
-    )(place, joined, msg0, turn(msg2, "y", 4, -2))
+    )(joined, msg0, turn(msg2, "y", 4, -2))
     msg = lax.all_to_all(msg, ("z", "xh", "kvh"), split_axis=0, concat_axis=0, tiled=True)
     return pl.pallas_call(
         finish_kernel,

time: 75.2 us -> 72.8 us (0.968)
  local copies, waits for them, and re-layouts: 7.89 us -> 4.9 us
  waiting for transfers between devices: 13.3 us -> 14.6 us
  starting transfers between devices: 24.1 us -> 24.9 us
    unnamed x14 -> x12, local copies, waits for them, and re-layouts: 4.73 us -> 1.98 us
    ppermute x13, waiting for transfers between devices: 10.6 us -> 12 us  [turn(): return lax.ppermute(x, axis, [((i + step) % size, i) for i in range(size)])]
    ppermute x13, starting transfers between devices: 15.5 us -> 16.3 us  [turn(): return lax.ppermute(x, axis, [((i + step) % size, i) for i in range(size)])]
    transpose x1 -> x2, local copies, waits for them, and re-layouts: 1.57 us -> 1.54 us  [per_device(): jnp.transpose(x.reshape(OWN * BLK, HEADS, HD), (1, 0, 2))]
where the time goes in v3:
time: 72.8 us; the launch traced here: 72.7 us
  starting transfers between devices  24.9 us (34%)
  blocking collectives  18 us (25%)
  waiting for transfers between devices  14.6 us (20%)
  Pallas kernels  10.2 us (14%)
  local copies, waits for them, and re-layouts  4.9 us (7%)
    all_to_all x1, blocking collectives, per_device(): lax.all_to_all(msg, ('z', 'xh', 'kvh'), split_axis=0, concat_axis=0, tile...  18 us
    ppermute x13, starting transfers between devices, turn(): return lax.ppermute(x, axis, [((i + step) % size, i) for i in range(size)])  16.3 us
    ppermute x13, waiting for transfers between devices, turn(): return lax.ppermute(x, axis, [((i + step) % size, i) for i in range(size)])  12 us
    all_to_all x1, starting transfers between devices, per_device(): q = lax.all_to_all(q, 'z', split_axis=0, concat_axis=0, tiled=True)  8.57 us
    pallas_call x3, Pallas kernels, attend(): pl.pallas_call(functools.partial(attend_kernel, steps), out_shape=[jax.Sh...  5.58 us
    all_to_all x1, waiting for transfers between devices, per_device(): q = lax.all_to_all(q, 'z', split_axis=0, concat_axis=0, tiled=True)  2.64 us
    unnamed x12, local copies, waits for them, and re-layouts  1.98 us
    pallas_call x1, Pallas kernels, per_device(): pl.pallas_call(select_kernel, out_shape=jax.ShapeDtypeStruct((3, 32), jnp...  1.91 us
  transfers between devices with their start and end apart: 14, of which 6 were waited for; matrix products, arithmetic and copies ran while one was open for 4% of the time, Pallas kernels for 12%

profile of v3, /device:TPU:32, one launch (start us, length us, event | category | flops | bytes accessed | tf_op | source)
XLA Modules:
  0.0 72.7 jit_solution(11221281191110913646)
XLA Ops:
  0.0 0.5 collective-permute-start.2
  0.5 1.4 %broadcast_in_dim.2 = bf16[8,2,2,16,128]{4,3,2,1,0:T(8,128)(2,1)} broadcast(bf16[2,2,16,128]{3,2,1,0:T(8,128)(2,1)} %param.6), dimensions={1,2,3,4} | broadcast | bytes 147456 | tf_op jit(solution)/shard_map/broadcast_in_dim | solution.py:264
  1.9 8.6 %all-to-all-start = ((bf16[8,2,2,16,128]{4,3,2,1,0:T(8,128)(2,1)}), bf16[8,2,2,16,128]{4,3,2,1,0:T(8,128)(2,1)S(1)}, u32[]{:S(2)}, u32[]{:S(2)}) async-start(bf16[8,2,2,16,128]{4,3,2,1,0:T(8,128)(2,1)} %broadcast_in_dim.2), calls=%async_computation | async-start | bytes 262144 | tf_op jit(solution)/shard_map/all_to_all | solution.py:265
  10.5 1.3 %collective-permute-done.peer_ids = s32[12]{0:T(128)S(1)} collective-permute-done((s32[12]{0:T(128)}, s32[12]{0:T(128)S(1)}, u32[]{:S(2)}, u32[]{:S(2)}) %collective-permute-start) | collective-permute-done | bytes 80 | tf_op jit(solution)/shard_map/ppermute | solution.py:244
  11.7 0.7 copy-done
  12.4 0.7 copy-done.2
  13.0 0.7 copy-done.4
  13.7 1.9 %select.1.lists.refs_0_ = s32[3,32]{1,0:T(4,128)S(1)} custom-call(s32[12]{0:T(128)S(1)} %copy-done.4, s32[12]{0:T(128)S(1)} %collective-permute-done.peer_ids, s32[4]{0:T(128)S(1)} %copy-done, s32[4]{0:T(128)S(1)} %copy-done.2), custom_call_target="tpu_custom_call" | custom-call | tf_op jit(solution)/shard_map/select/pallas_call | solution.py:255
  15.6 2.6 %all-to-all-done.refs_3_ = bf16[8,2,2,16,128]{4,3,2,1,0:T(8,128)(2,1)S(1)} async-done(((bf16[8,2,2,16,128]{4,3,2,1,0:T(8,128)(2,1)}), bf16[8,2,2,16,128]{4,3,2,1,0:T(8,128)(2,1)S(1)}, u32[]{:S(2)}, u32[]{:S(2)}) %all-to-all-start) | async-done | bytes 131104 | tf_op jit(solution)/shard_map/all_to_all | solution.py:265
  18.2 3.0 %collective-permute-start.3 = (bf16[8,2,2,16,128]{4,3,2,1,0:T(8,128)(2,1)S(1)}, bf16[8,2,2,16,128]{4,3,2,1,0:T(8,128)(2,1)S(1)}, u32[]{:S(2)}, u32[]{:S(2)}) collective-permute-start(bf16[8,2,2,16,128]{4,3,2,1,0:T(8,128)(2,1)S(1)} %all-to-all-done.refs_3_), channel_id=1, source_target_pairs={{4,0},{0,4},{5,1},{1,5},{6,2},{2,6},{7,3},{3,7},{12,8},{8,12},{13,... | collective-permute-start | bytes 393224 | tf_op jit(solution)/shard_map/ppermute | solution.py:244
  21.3 3.0 %collective-permute-start.4 = (bf16[8,2,2,16,128]{4,3,2,1,0:T(8,128)(2,1)S(1)}, bf16[8,2,2,16,128]{4,3,2,1,0:T(8,128)(2,1)S(1)}, u32[]{:S(2)}, u32[]{:S(2)}) collective-permute-start(bf16[8,2,2,16,128]{4,3,2,1,0:T(8,128)(2,1)S(1)} %all-to-all-done.refs_3_), channel_id=1, source_target_pairs={{8,0},{16,8},{24,16},{0,24},{9,1},{17,9},{25,17},{1,25},{10,2},{18... | collective-permute-start | bytes 393224 | tf_op jit(solution)/shard_map/ppermute | solution.py:244
  24.3 1.3 %copy_bitcast_fusion = (bf16[2,1536,128]{2,1,0:T(8,128)(2,1)S(1)}, bf16[2,1536,128]{2,1,0:T(8,128)(2,1)S(1)}) fusion(bf16[1536,2,128]{2,1,0:T(2,128)(2,1)S(1)} %bitcast.17, bf16[1536,2,128]{2,1,0:T(2,128)(2,1)} %param.8), kind=kLoop, calls=%fused_computation | loop fusion | bytes 3145728 | tf_op jit(solution)/shard_map/transpose | solution.py:268
  25.6 0.2 copy_bitcast_fusion.2
  25.9 0.0 copy-start.1
  25.9 0.0 copy-start.3
  25.9 1.2 %pack.1 = (bf16[14,2,256,128]{3,2,1,0:T(8,128)(2,1)S(1)}, bf16[14,2,128,256]{3,2,1,0:T(8,128)(2,1)S(1)}) custom-call(s32[3,32]{1,0:T(4,128)S(1)} %select.1.lists.refs_0_, bf16[2,1536,128]{2,1,0:T(8,128)(2,1)S(1)} %get-tuple-element.38.k0, bf16[2,1536,128]{2,1,0:T(8,128)(2,1)S(1)} %get-tuple-element.37.k1, bf16[2,1536,128]{2,1,0:T(8,128)(2,1)S(1)} %get-tuple-element.36.v0, ...), custom_call_target="tpu_custom_call" | custom-call | flops 1000000000 | bytes 4194304 | tf_op jit(solution)/shard_map/pack/pallas_call | solution.py:270
  27.1 3.3 %collective-permute-done.5.refs_5_ = bf16[8,2,2,16,128]{4,3,2,1,0:T(8,128)(2,1)S(1)} collective-permute-done((bf16[8,2,2,16,128]{4,3,2,1,0:T(8,128)(2,1)S(1)}, bf16[8,2,2,16,128]{4,3,2,1,0:T(8,128)(2,1)S(1)}, u32[]{:S(2)}, u32[]{:S(2)}) %collective-permute-start.5) | collective-permute-done | bytes 131104 | tf_op jit(solution)/shard_map/ppermute | solution.py:244
  30.5 3.2 %collective-permute-start.6 = (bf16[8,2,2,16,128]{4,3,2,1,0:T(8,128)(2,1)S(1)}, bf16[8,2,2,16,128]{4,3,2,1,0:T(8,128)(2,1)S(1)}, u32[]{:S(2)}, u32[]{:S(2)}) collective-permute-start(bf16[8,2,2,16,128]{4,3,2,1,0:T(8,128)(2,1)S(1)} %collective-permute-done.3.refs_4_), channel_id=1, source_target_pairs={{8,0},{16,8},{24,16},{0,24},{9,1},{17,9},{25,17},{1,25},{10,2},{18... | collective-permute-start | bytes 393224 | tf_op jit(solution)/shard_map/ppermute | solution.py:244
  33.7 0.0 collective-permute-start.10
  33.7 3.6 %collective-permute-done.7.refs_6_ = bf16[8,2,2,16,128]{4,3,2,1,0:T(8,128)(2,1)S(1)} collective-permute-done((bf16[8,2,2,16,128]{4,3,2,1,0:T(8,128)(2,1)S(1)}, bf16[8,2,2,16,128]{4,3,2,1,0:T(8,128)(2,1)S(1)}, u32[]{:S(2)}, u32[]{:S(2)}) %collective-permute-start.7) | collective-permute-done | bytes 131104 | tf_op jit(solution)/shard_map/ppermute | solution.py:244
  37.3 2.1 %attend13.1 = (bf16[136,1024]{1,0:T(8,128)(2,1)S(1)}, bf16[136,1024]{1,0:T(8,128)(2,1)S(1)}) custom-call(s32[3,32]{1,0:T(4,128)S(1)} %select.1.lists.refs_0_, s32[4]{0:T(128)S(1)} %copy-done.1, s32[4]{0:T(128)S(1)} %copy-done.3, bf16[8,2,2,16,128]{4,3,2,1,0:T(8,128)(2,1)S(1)} %collective-permute-done.4.refs_3_, ...), custom_call_target="tpu_custom_call" | custom-call | flops 1000000000 | bytes 4194304 | tf_op jit(solution)/shard_map/attend13/pallas_call | solution.py:291
  39.5 0.1 collective-permute-start.8
  39.6 3.9 %collective-permute-start.9 = (bf16[136,1024]{1,0:T(8,128)(2,1)S(1)}, bf16[136,1024]{1,0:T(8,128)(2,1)S(1)}, u32[]{:S(2)}, u32[]{:S(2)}) collective-permute-start(bf16[136,1024]{1,0:T(8,128)(2,1)S(1)} %get-tuple-element.34), channel_id=1, source_target_pairs={{8,0},{16,8},{24,16},{0,24},{9,1},{17,9},{25,17},{1,25},{10,2},{18... | collective-permute-start | bytes 835592 | tf_op jit(solution)/shard_map/ppermute | solution.py:244
  43.5 1.7 %attend2.1 = bf16[136,1024]{1,0:T(8,128)(2,1)S(1)} custom-call(s32[3,32]{1,0:T(4,128)S(1)} %select.1.lists.refs_0_, s32[4]{0:T(128)S(1)} %copy-done.1, s32[4]{0:T(128)S(1)} %copy-done.3, bf16[8,2,2,16,128]{4,3,2,1,0:T(8,128)(2,1)S(1)} %collective-permute-done.10.refs_3_, bf16[8,2,2,16,128]{4,3,2,1,0:T(8,128)(2,1)S(1)} %collective-permute-done.11.refs_4_, ...), custom_call_target="tpu_custom_call" | custom-call | flops 1000000000 | bytes 4194304 | tf_op jit(solution)/shard_map/attend2/pallas_call | solution.py:291
  45.3 2.5 %collective-permute-start.12 = (bf16[136,1024]{1,0:T(8,128)(2,1)S(1)}, bf16[136,1024]{1,0:T(8,128)(2,1)S(1)}, u32[]{:S(2)}, u32[]{:S(2)}) collective-permute-start(bf16[136,1024]{1,0:T(8,128)(2,1)S(1)} %attend2.1), channel_id=1, source_target_pairs={{16,0},{24,8},{0,16},{8,24},{17,1},{25,9},{1,17},{9,25},{18,2},{26... | collective-permute-start | bytes 835592 | tf_op jit(solution)/shard_map/ppermute | solution.py:244
  47.7 1.7 %attend0.1.in0 = bf16[136,1024]{1,0:T(8,128)(2,1)S(1)} custom-call(s32[3,32]{1,0:T(4,128)S(1)} %select.1.lists.refs_0_, s32[4]{0:T(128)S(1)} %copy-done.1, s32[4]{0:T(128)S(1)} %copy-done.3, bf16[8,2,2,16,128]{4,3,2,1,0:T(8,128)(2,1)S(1)} %all-to-all-done.refs_3_, bf16[8,2,2,16,128]{4,3,2,1,0:T(8,128)(2,1)S(1)} %collective-permute-done.3.refs_4_, ...), custom_call_target="tpu_custom_call" | custom-call | flops 1000000000 | bytes 4194304 | tf_op jit(solution)/shard_map/attend0/pallas_call | solution.py:291
  49.5 0.8 %collective-permute-done.8.in0 = bf16[136,1024]{1,0:T(8,128)(2,1)S(1)} collective-permute-done((bf16[136,1024]{1,0:T(8,128)(2,1)S(1)}, bf16[136,1024]{1,0:T(8,128)(2,1)S(1)}, u32[]{:S(2)}, u32[]{:S(2)}) %collective-permute-start.8) | collective-permute-done | bytes 278560 | tf_op jit(solution)/shard_map/ppermute | solution.py:244
  50.2 0.1 join.1.joined
  50.4 3.0 %collective-permute-done.12.in1 = bf16[136,1024]{1,0:T(8,128)(2,1)S(1)} collective-permute-done((bf16[136,1024]{1,0:T(8,128)(2,1)S(1)}, bf16[136,1024]{1,0:T(8,128)(2,1)S(1)}, u32[]{:S(2)}, u32[]{:S(2)}) %collective-permute-start.12) | collective-permute-done | bytes 278560 | tf_op jit(solution)/shard_map/ppermute | solution.py:244
  53.4 0.3 fold.1
  53.7 18.0 %all_to_all.10.in_ref = bf16[32,40,128]{2,1,0:T(8,128)(2,1)S(1)} all-to-all(bf16[32,40,128]{2,1,0:T(8,128)(2,1)S(1)} %fold.1), channel_id=1, replica_groups=mesh['z'=8,'y'=4,'xh'=2,'core'=2,'kvh'=2] {'z','xh','kvh'}, dimensions={0} | all-to-all | bytes 655360 | tf_op jit(solution)/shard_map/all_to_all | solution.py:327
  71.6 1.1 %finish.1 = bf16[1,64,128]{2,1,0:T(8,128)(2,1)} custom-call(bf16[32,40,128]{2,1,0:T(8,128)(2,1)S(1)} %all_to_all.10.in_ref), custom_call_target="tpu_custom_call" | custom-call | tf_op jit(solution)/shard_map/finish/pallas_call | solution.py:328
  (20 shorter events, 0.0 us)
Async XLA Ops:
  0.0 18.2 %collective-permute-start.1 = (bf16[3072,128]{1,0:T(8,128)(2,1)}, bf16[3072,128]{1,0:T(8,128)(2,1)S(1)}, u32[]{:S(2)}, u32[]{:S(2)}) collective-permute-start(bf16[3072,128]{1,0:T(8,128)(2,1)} %bitcast.15), channel_id=1, source_target_pairs={{2,0},{0,2},{3,1},{1,3},{6,4},{4,6},{7,5},{5,7},{10,8},{8,10},{11,... | collective-permute-start | bytes 2359304 | tf_op jit(solution)/shard_map/ppermute | solution.py:244
  0.0 18.2 %collective-permute-start.2 = (bf16[3072,128]{1,0:T(8,128)(2,1)}, bf16[3072,128]{1,0:T(8,128)(2,1)S(1)}, u32[]{:S(2)}, u32[]{:S(2)}) collective-permute-start(bf16[3072,128]{1,0:T(8,128)(2,1)} %bitcast.14), channel_id=1, source_target_pairs={{2,0},{0,2},{3,1},{1,3},{6,4},{4,6},{7,5},{5,7},{10,8},{8,10},{11,... | collective-permute-start | bytes 2359304 | tf_op jit(solution)/shard_map/ppermute | solution.py:244
  1.9 16.3 %all-to-all-start = ((bf16[8,2,2,16,128]{4,3,2,1,0:T(8,128)(2,1)}), bf16[8,2,2,16,128]{4,3,2,1,0:T(8,128)(2,1)S(1)}, u32[]{:S(2)}, u32[]{:S(2)}) async-start(bf16[8,2,2,16,128]{4,3,2,1,0:T(8,128)(2,1)} %broadcast_in_dim.2), calls=%async_computation | async-start | bytes 262144 | tf_op jit(solution)/shard_map/all_to_all | solution.py:265
  10.5 1.3 %collective-permute-start = (s32[12]{0:T(128)}, s32[12]{0:T(128)S(1)}, u32[]{:S(2)}, u32[]{:S(2)}) collective-permute-start(s32[12]{0:T(128)} %own_ids.1), channel_id=1, source_target_pairs={{2,0},{0,2},{3,1},{1,3},{6,4},{4,6},{7,5},{5,7},{10,8},{8,10},{11,... | collective-permute-start | bytes 152 | tf_op jit(solution)/shard_map/ppermute | solution.py:244
  11.7 0.7 copy-start
  12.4 0.7 copy-start.2
  13.0 0.7 copy-start.4
  13.7 12.0 %copy-start.5 = (bf16[1536,2,128]{2,1,0:T(2,128)(2,1)S(1)}, bf16[1536,2,128]{2,1,0:T(2,128)(2,1)}, u32[]{:S(2)}) copy-start(bf16[1536,2,128]{2,1,0:T(2,128)(2,1)} %param.7) | copy-start | bytes 2359300
  18.2 8.9 %collective-permute-start.3 = (bf16[8,2,2,16,128]{4,3,2,1,0:T(8,128)(2,1)S(1)}, bf16[8,2,2,16,128]{4,3,2,1,0:T(8,128)(2,1)S(1)}, u32[]{:S(2)}, u32[]{:S(2)}) collective-permute-start(bf16[8,2,2,16,128]{4,3,2,1,0:T(8,128)(2,1)S(1)} %all-to-all-done.refs_3_), channel_id=1, source_target_pairs={{4,0},{0,4},{5,1},{1,5},{6,2},{2,6},{7,3},{3,7},{12,8},{8,12},{13,... | collective-permute-start | bytes 393224 | tf_op jit(solution)/shard_map/ppermute | solution.py:244
  21.3 5.9 %collective-permute-start.4 = (bf16[8,2,2,16,128]{4,3,2,1,0:T(8,128)(2,1)S(1)}, bf16[8,2,2,16,128]{4,3,2,1,0:T(8,128)(2,1)S(1)}, u32[]{:S(2)}, u32[]{:S(2)}) collective-permute-start(bf16[8,2,2,16,128]{4,3,2,1,0:T(8,128)(2,1)S(1)} %all-to-all-done.refs_3_), channel_id=1, source_target_pairs={{8,0},{16,8},{24,16},{0,24},{9,1},{17,9},{25,17},{1,25},{10,2},{18... | collective-permute-start | bytes 393224 | tf_op jit(solution)/shard_map/ppermute | solution.py:244
  24.3 6.2 %collective-permute-start.5 = (bf16[8,2,2,16,128]{4,3,2,1,0:T(8,128)(2,1)S(1)}, bf16[8,2,2,16,128]{4,3,2,1,0:T(8,128)(2,1)S(1)}, u32[]{:S(2)}, u32[]{:S(2)}) collective-permute-start(bf16[8,2,2,16,128]{4,3,2,1,0:T(8,128)(2,1)S(1)} %all-to-all-done.refs_3_), channel_id=1, source_target_pairs={{24,0},{0,8},{8,16},{16,24},{25,1},{1,9},{9,17},{17,25},{26,2},{2,... | collective-permute-start | bytes 393224 | tf_op jit(solution)/shard_map/ppermute | solution.py:244
  25.9 11.5 %copy-start.1 = (s32[4]{0:T(128)S(1)}, s32[4]{0:T(128)}, u32[]{:S(2)}) copy-start(s32[4]{0:T(128)} %refs_1_.5) | copy-start | bytes 52
  25.9 11.5 %copy-start.3 = (s32[4]{0:T(128)S(1)}, s32[4]{0:T(128)}, u32[]{:S(2)}) copy-start(s32[4]{0:T(128)} %refs_2_.5) | copy-start | bytes 52
  30.5 6.9 %collective-permute-start.7 = (bf16[8,2,2,16,128]{4,3,2,1,0:T(8,128)(2,1)S(1)}, bf16[8,2,2,16,128]{4,3,2,1,0:T(8,128)(2,1)S(1)}, u32[]{:S(2)}, u32[]{:S(2)}) collective-permute-start(bf16[8,2,2,16,128]{4,3,2,1,0:T(8,128)(2,1)S(1)} %collective-permute-done.3.refs_4_), channel_id=1, source_target_pairs={{24,0},{0,8},{8,16},{16,24},{25,1},{1,9},{9,17},{17,25},{26,2},{2,... | collective-permute-start | bytes 393224 | tf_op jit(solution)/shard_map/ppermute | solution.py:244
  30.5 6.9 %collective-permute-start.6 = (bf16[8,2,2,16,128]{4,3,2,1,0:T(8,128)(2,1)S(1)}, bf16[8,2,2,16,128]{4,3,2,1,0:T(8,128)(2,1)S(1)}, u32[]{:S(2)}, u32[]{:S(2)}) collective-permute-start(bf16[8,2,2,16,128]{4,3,2,1,0:T(8,128)(2,1)S(1)} %collective-permute-done.3.refs_4_), channel_id=1, source_target_pairs={{8,0},{16,8},{24,16},{0,24},{9,1},{17,9},{25,17},{1,25},{10,2},{18... | collective-permute-start | bytes 393224 | tf_op jit(solution)/shard_map/ppermute | solution.py:244
  33.7 9.8 %collective-permute-start.10 = (bf16[8,2,2,16,128]{4,3,2,1,0:T(8,128)(2,1)S(1)}, bf16[8,2,2,16,128]{4,3,2,1,0:T(8,128)(2,1)S(1)}, u32[]{:S(2)}, u32[]{:S(2)}) collective-permute-start(bf16[8,2,2,16,128]{4,3,2,1,0:T(8,128)(2,1)S(1)} %collective-permute-done.4.refs_3_), channel_id=1, source_target_pairs={{8,0},{16,8},{24,16},{0,24},{9,1},{17,9},{25,17},{1,25},{10,2},{18... | collective-permute-start | bytes 393224 | tf_op jit(solution)/shard_map/ppermute | solution.py:244
  37.3 6.2 %collective-permute-start.11 = (bf16[8,2,2,16,128]{4,3,2,1,0:T(8,128)(2,1)S(1)}, bf16[8,2,2,16,128]{4,3,2,1,0:T(8,128)(2,1)S(1)}, u32[]{:S(2)}, u32[]{:S(2)}) collective-permute-start(bf16[8,2,2,16,128]{4,3,2,1,0:T(8,128)(2,1)S(1)} %collective-permute-done.7.refs_6_), channel_id=1, source_target_pairs={{24,0},{0,8},{8,16},{16,24},{25,1},{1,9},{9,17},{17,25},{26,2},{2,... | collective-permute-start | bytes 393224 | tf_op jit(solution)/shard_map/ppermute | solution.py:244
  39.5 10.7 %collective-permute-start.8 = (bf16[136,1024]{1,0:T(8,128)(2,1)S(1)}, bf16[136,1024]{1,0:T(8,128)(2,1)S(1)}, u32[]{:S(2)}, u32[]{:S(2)}) collective-permute-start(bf16[136,1024]{1,0:T(8,128)(2,1)S(1)} %get-tuple-element.33), channel_id=1, source_target_pairs={{24,0},{0,8},{8,16},{16,24},{25,1},{1,9},{9,17},{17,25},{26,2},{2,... | collective-permute-start | bytes 835592 | tf_op jit(solution)/shard_map/ppermute | solution.py:244
  39.6 10.7 %collective-permute-start.9 = (bf16[136,1024]{1,0:T(8,128)(2,1)S(1)}, bf16[136,1024]{1,0:T(8,128)(2,1)S(1)}, u32[]{:S(2)}, u32[]{:S(2)}) collective-permute-start(bf16[136,1024]{1,0:T(8,128)(2,1)S(1)} %get-tuple-element.34), channel_id=1, source_target_pairs={{8,0},{16,8},{24,16},{0,24},{9,1},{17,9},{25,17},{1,25},{10,2},{18... | collective-permute-start | bytes 835592 | tf_op jit(solution)/shard_map/ppermute | solution.py:244
  45.3 8.1 %collective-permute-start.12 = (bf16[136,1024]{1,0:T(8,128)(2,1)S(1)}, bf16[136,1024]{1,0:T(8,128)(2,1)S(1)}, u32[]{:S(2)}, u32[]{:S(2)}) collective-permute-start(bf16[136,1024]{1,0:T(8,128)(2,1)S(1)} %attend2.1), channel_id=1, source_target_pairs={{16,0},{24,8},{0,16},{8,24},{17,1},{25,9},{1,17},{9,25},{18,2},{26... | collective-permute-start | bytes 835592 | tf_op jit(solution)/shard_map/ppermute | solution.py:244

commit v4 on v3

--- a/solution.py
+++ b/solution.py
@@ -279,10 +279,11 @@
         cost_estimate=COST,
         name="pack",
     )(lists, k0, k1, v0, v1)
-    over, near, back, k, v = lax.optimization_barrier(
-        (turn(q, "xh", 2, 1), turn(q, "y", 4, 1), turn(q, "y", 4, 3), k, v)
+    over, near, back = lax.optimization_barrier(
+        (turn(q, "xh", 2, 1), turn(q, "y", 4, 1), turn(q, "y", 4, 3))
     )
     near, back = [near, turn(over, "y", 4, 1)], [back, turn(over, "y", 4, 3)]
+    back[1], k, v = lax.optimization_barrier((back[1], k, v))
     qs = [[q, over], near, [turn(near[0], "y", 4, 1), turn(back[1], "y", 4, 3)], back]
 
     def attend(*steps):
@@ -307,6 +308,7 @@
     msg1, msg3 = attend(1, 3)
     (msg2,) = attend(2)
     (msg0,) = attend(0)
+    msg2, msg3 = lax.optimization_barrier((msg2, msg3))
     joined = pl.pallas_call(
         join_kernel,
         out_shape=jax.ShapeDtypeStruct((MSG, 8 * BLK), jnp.float32),
@@ -315,7 +317,7 @@
         compiler_params=params(12),
         cost_estimate=COST,
         name="join",
-    )(turn(msg1, "y", 4, -1), turn(msg3, "y", 4, -3))
+    )(msg0, turn(msg1, "y", 4, -1))
     msg = pl.pallas_call(
         fold_kernel,
         out_shape=jax.ShapeDtypeStruct((32, LAST, HD), jnp.bfloat16),
@@ -323,7 +325,7 @@
         out_specs=VMEM,
         compiler_params=params(12),
         name="fold",
-    )(joined, msg0, turn(msg2, "y", 4, -2))
+    )(joined, turn(msg2, "y", 4, -2), turn(msg3, "y", 4, -3))
     msg = lax.all_to_all(msg, ("z", "xh", "kvh"), split_axis=0, concat_axis=0, tiled=True)
     return pl.pallas_call(
         finish_kernel,

time: 72.8 us -> 76.1 us (1.045); the launches traced: 72.7 us -> 74.9 us
  starting transfers between devices: 24.9 us -> 20.3 us
  waiting for transfers between devices: 14.6 us -> 18.6 us
  Pallas kernels: 10.2 us -> 12.2 us
  blocking collectives: 18 us -> 18.8 us
    ppermute x13, starting transfers between devices: 16.3 us -> 11.7 us  [turn(): return lax.ppermute(x, axis, [((i + step) % size, i) for i in range(size)])]
    ppermute x13, waiting for transfers between devices: 12 us -> 15.9 us  [turn(): return lax.ppermute(x, axis, [((i + step) % size, i) for i in range(size)])]
    pallas_call x3, Pallas kernels: 5.58 us -> 7.24 us  [attend(): pl.pallas_call(functools.partial(attend_kernel, steps), out_shape=[jax.Sh...]
    all_to_all x1, blocking collectives: 18 us -> 18.8 us  [per_device(): lax.all_to_all(msg, ('z', 'xh', 'kvh'), split_axis=0, concat_axis=0, tile...]
  transfers between devices with their start and end apart: 14 -> 14, of which waited for: 6 -> 9; matrix products, arithmetic and copies ran while one was open for 4% -> 4% of each run, Pallas kernels for 12% -> 14%
where the time goes in v4:
time: 76.1 us; the launch traced here: 74.9 us
  starting transfers between devices  20.3 us (27%)
  blocking collectives  18.8 us (25%)
  waiting for transfers between devices  18.6 us (24%)
  Pallas kernels  12.2 us (16%)
  local copies, waits for them, and re-layouts  4.89 us (6%)
    all_to_all x1, blocking collectives, per_device(): lax.all_to_all(msg, ('z', 'xh', 'kvh'), split_axis=0, concat_axis=0, tile...  18.8 us
    ppermute x13, waiting for transfers between devices, turn(): return lax.ppermute(x, axis, [((i + step) % size, i) for i in range(size)])  15.9 us
    ppermute x13, starting transfers between devices, turn(): return lax.ppermute(x, axis, [((i + step) % size, i) for i in range(size)])  11.7 us
    all_to_all x1, starting transfers between devices, per_device(): q = lax.all_to_all(q, 'z', split_axis=0, concat_axis=0, tiled=True)  8.57 us
    pallas_call x3, Pallas kernels, attend(): pl.pallas_call(functools.partial(attend_kernel, steps), out_shape=[jax.Sh...  7.24 us
    all_to_all x1, waiting for transfers between devices, per_device(): q = lax.all_to_all(q, 'z', split_axis=0, concat_axis=0, tiled=True)  2.64 us
    unnamed x12, local copies, waits for them, and re-layouts  1.98 us
    pallas_call x1, Pallas kernels, per_device(): pl.pallas_call(select_kernel, out_shape=jax.ShapeDtypeStruct((3, 32), jnp...  1.91 us
  transfers between devices with their start and end apart: 14, of which 9 were waited for; matrix products, arithmetic and copies ran while one was open for 4% of the time, Pallas kernels for 14%

profile of v4, /device:TPU:32, one launch (start us, length us, event | category | flops | bytes accessed | tf_op | source)
XLA Modules:
  0.0 74.9 jit_solution(17938826147317753105)
XLA Ops:
  0.0 0.5 collective-permute-start.2
  0.5 1.4 %broadcast_in_dim.2 = bf16[8,2,2,16,128]{4,3,2,1,0:T(8,128)(2,1)} broadcast(bf16[2,2,16,128]{3,2,1,0:T(8,128)(2,1)} %param.6), dimensions={1,2,3,4} | broadcast | bytes 147456 | tf_op jit(solution)/shard_map/broadcast_in_dim | solution.py:264
  1.9 8.6 %all-to-all-start = ((bf16[8,2,2,16,128]{4,3,2,1,0:T(8,128)(2,1)}), bf16[8,2,2,16,128]{4,3,2,1,0:T(8,128)(2,1)S(1)}, u32[]{:S(2)}, u32[]{:S(2)}) async-start(bf16[8,2,2,16,128]{4,3,2,1,0:T(8,128)(2,1)} %broadcast_in_dim.2), calls=%async_computation | async-start | bytes 262144 | tf_op jit(solution)/shard_map/all_to_all | solution.py:265
  10.5 1.3 %collective-permute-done.peer_ids = s32[12]{0:T(128)S(1)} collective-permute-done((s32[12]{0:T(128)}, s32[12]{0:T(128)S(1)}, u32[]{:S(2)}, u32[]{:S(2)}) %collective-permute-start) | collective-permute-done | bytes 80 | tf_op jit(solution)/shard_map/ppermute | solution.py:244
  11.7 0.7 copy-done
  12.4 0.7 copy-done.2
  13.0 0.7 copy-done.4
  13.7 1.9 %select.1.lists.refs_0_ = s32[3,32]{1,0:T(4,128)S(1)} custom-call(s32[12]{0:T(128)S(1)} %copy-done.4, s32[12]{0:T(128)S(1)} %collective-permute-done.peer_ids, s32[4]{0:T(128)S(1)} %copy-done, s32[4]{0:T(128)S(1)} %copy-done.2), custom_call_target="tpu_custom_call" | custom-call | tf_op jit(solution)/shard_map/select/pallas_call | solution.py:255
  15.6 2.6 %all-to-all-done.refs_3_ = bf16[8,2,2,16,128]{4,3,2,1,0:T(8,128)(2,1)S(1)} async-done(((bf16[8,2,2,16,128]{4,3,2,1,0:T(8,128)(2,1)}), bf16[8,2,2,16,128]{4,3,2,1,0:T(8,128)(2,1)S(1)}, u32[]{:S(2)}, u32[]{:S(2)}) %all-to-all-start) | async-done | bytes 131104 | tf_op jit(solution)/shard_map/all_to_all | solution.py:265
  18.2 3.0 %collective-permute-start.3 = (bf16[8,2,2,16,128]{4,3,2,1,0:T(8,128)(2,1)S(1)}, bf16[8,2,2,16,128]{4,3,2,1,0:T(8,128)(2,1)S(1)}, u32[]{:S(2)}, u32[]{:S(2)}) collective-permute-start(bf16[8,2,2,16,128]{4,3,2,1,0:T(8,128)(2,1)S(1)} %all-to-all-done.refs_3_), channel_id=1, source_target_pairs={{4,0},{0,4},{5,1},{1,5},{6,2},{2,6},{7,3},{3,7},{12,8},{8,12},{13,... | collective-permute-start | bytes 393224 | tf_op jit(solution)/shard_map/ppermute | solution.py:244
  21.3 3.0 %collective-permute-start.4 = (bf16[8,2,2,16,128]{4,3,2,1,0:T(8,128)(2,1)S(1)}, bf16[8,2,2,16,128]{4,3,2,1,0:T(8,128)(2,1)S(1)}, u32[]{:S(2)}, u32[]{:S(2)}) collective-permute-start(bf16[8,2,2,16,128]{4,3,2,1,0:T(8,128)(2,1)S(1)} %all-to-all-done.refs_3_), channel_id=1, source_target_pairs={{8,0},{16,8},{24,16},{0,24},{9,1},{17,9},{25,17},{1,25},{10,2},{18... | collective-permute-start | bytes 393224 | tf_op jit(solution)/shard_map/ppermute | solution.py:244
  24.3 1.3 %copy_bitcast_fusion = (bf16[2,1536,128]{2,1,0:T(8,128)(2,1)S(1)}, bf16[2,1536,128]{2,1,0:T(8,128)(2,1)S(1)}) fusion(bf16[1536,2,128]{2,1,0:T(2,128)(2,1)S(1)} %bitcast.17, bf16[1536,2,128]{2,1,0:T(2,128)(2,1)} %param.8), kind=kLoop, calls=%fused_computation | loop fusion | bytes 3145728 | tf_op jit(solution)/shard_map/transpose | solution.py:268
  25.6 1.2 %collective-permute-done.4.refs_3_ = bf16[8,2,2,16,128]{4,3,2,1,0:T(8,128)(2,1)S(1)} collective-permute-done((bf16[8,2,2,16,128]{4,3,2,1,0:T(8,128)(2,1)S(1)}, bf16[8,2,2,16,128]{4,3,2,1,0:T(8,128)(2,1)S(1)}, u32[]{:S(2)}, u32[]{:S(2)}) %collective-permute-start.4) | collective-permute-done | bytes 131104 | tf_op jit(solution)/shard_map/ppermute | solution.py:244
  26.8 3.7 %collective-permute-done.5.refs_5_ = bf16[8,2,2,16,128]{4,3,2,1,0:T(8,128)(2,1)S(1)} collective-permute-done((bf16[8,2,2,16,128]{4,3,2,1,0:T(8,128)(2,1)S(1)}, bf16[8,2,2,16,128]{4,3,2,1,0:T(8,128)(2,1)S(1)}, u32[]{:S(2)}, u32[]{:S(2)}) %collective-permute-start.5) | collective-permute-done | bytes 131104 | tf_op jit(solution)/shard_map/ppermute | solution.py:244
  30.5 0.2 copy_bitcast_fusion.2
  30.7 3.3 %collective-permute-start.7 = (bf16[8,2,2,16,128]{4,3,2,1,0:T(8,128)(2,1)S(1)}, bf16[8,2,2,16,128]{4,3,2,1,0:T(8,128)(2,1)S(1)}, u32[]{:S(2)}, u32[]{:S(2)}) collective-permute-start(bf16[8,2,2,16,128]{4,3,2,1,0:T(8,128)(2,1)S(1)} %collective-permute-done.3.refs_4_), channel_id=1, source_target_pairs={{8,0},{16,8},{24,16},{0,24},{9,1},{17,9},{25,17},{1,25},{10,2},{18... | collective-permute-start | bytes 393224 | tf_op jit(solution)/shard_map/ppermute | solution.py:244
  34.0 1.5 %pack.1 = (bf16[14,2,256,128]{3,2,1,0:T(8,128)(2,1)S(1)}, bf16[14,2,128,256]{3,2,1,0:T(8,128)(2,1)S(1)}) custom-call(s32[3,32]{1,0:T(4,128)S(1)} %select.1.lists.refs_0_, bf16[2,1536,128]{2,1,0:T(8,128)(2,1)S(1)} %get-tuple-element.44.k0, bf16[2,1536,128]{2,1,0:T(8,128)(2,1)S(1)} %get-tuple-element.43.k1, bf16[2,1536,128]{2,1,0:T(8,128)(2,1)S(1)} %get-tuple-element.42.v0, ...), custom_call_target="tpu_custom_call" | custom-call | flops 1000000000 | bytes 4194304 | tf_op jit(solution)/shard_map/pack/pallas_call | solution.py:270
  35.5 0.1 collective-permute-start.9
  35.6 1.7 %collective-permute-done.6.refs_6_ = bf16[8,2,2,16,128]{4,3,2,1,0:T(8,128)(2,1)S(1)} collective-permute-done((bf16[8,2,2,16,128]{4,3,2,1,0:T(8,128)(2,1)S(1)}, bf16[8,2,2,16,128]{4,3,2,1,0:T(8,128)(2,1)S(1)}, u32[]{:S(2)}, u32[]{:S(2)}) %collective-permute-start.6) | collective-permute-done | bytes 131104 | tf_op jit(solution)/shard_map/ppermute | solution.py:244
  37.3 0.3 collective-permute-start.10
  37.7 2.8 %attend13.1 = (bf16[136,1024]{1,0:T(8,128)(2,1)S(1)}, bf16[136,1024]{1,0:T(8,128)(2,1)S(1)}) custom-call(s32[3,32]{1,0:T(4,128)S(1)} %select.1.lists.refs_0_, s32[4]{0:T(128)S(1)} %copy-done.1, s32[4]{0:T(128)S(1)} %copy-done.3, bf16[8,2,2,16,128]{4,3,2,1,0:T(8,128)(2,1)S(1)} %collective-permute-done.4.refs_3_, ...), custom_call_target="tpu_custom_call" | custom-call | flops 1000000000 | bytes 4194304 | tf_op jit(solution)/shard_map/attend13/pallas_call | solution.py:292
  40.6 3.7 %collective-permute-done.10.refs_4_ = bf16[8,2,2,16,128]{4,3,2,1,0:T(8,128)(2,1)S(1)} collective-permute-done((bf16[8,2,2,16,128]{4,3,2,1,0:T(8,128)(2,1)S(1)}, bf16[8,2,2,16,128]{4,3,2,1,0:T(8,128)(2,1)S(1)}, u32[]{:S(2)}, u32[]{:S(2)}) %collective-permute-start.10) | collective-permute-done | bytes 131104 | tf_op jit(solution)/shard_map/ppermute | solution.py:244
  44.3 2.2 %attend2.1 = bf16[136,1024]{1,0:T(8,128)(2,1)S(1)} custom-call(s32[3,32]{1,0:T(4,128)S(1)} %select.1.lists.refs_0_, s32[4]{0:T(128)S(1)} %copy-done.1, s32[4]{0:T(128)S(1)} %copy-done.3, bf16[8,2,2,16,128]{4,3,2,1,0:T(8,128)(2,1)S(1)} %collective-permute-done.9.refs_3_, bf16[8,2,2,16,128]{4,3,2,1,0:T(8,128)(2,1)S(1)} %collective-permute-done.10.refs_4_, ...), custom_call_target="tpu_custom_call" | custom-call | flops 1000000000 | bytes 4194304 | tf_op jit(solution)/shard_map/attend2/pallas_call | solution.py:292
  46.5 0.1 collective-permute-start.11
  46.6 1.3 %collective-permute-start.12 = (bf16[136,1024]{1,0:T(8,128)(2,1)S(1)}, bf16[136,1024]{1,0:T(8,128)(2,1)S(1)}, u32[]{:S(2)}, u32[]{:S(2)}) collective-permute-start(bf16[136,1024]{1,0:T(8,128)(2,1)S(1)} %get-tuple-element.40), channel_id=1, source_target_pairs={{8,0},{16,8},{24,16},{0,24},{9,1},{17,9},{25,17},{1,25},{10,2},{18... | collective-permute-start | bytes 835592 | tf_op jit(solution)/shard_map/ppermute | solution.py:244
  47.9 2.2 %attend0.1.in0 = bf16[136,1024]{1,0:T(8,128)(2,1)S(1)} custom-call(s32[3,32]{1,0:T(4,128)S(1)} %select.1.lists.refs_0_, s32[4]{0:T(128)S(1)} %copy-done.1, s32[4]{0:T(128)S(1)} %copy-done.3, bf16[8,2,2,16,128]{4,3,2,1,0:T(8,128)(2,1)S(1)} %all-to-all-done.refs_3_, bf16[8,2,2,16,128]{4,3,2,1,0:T(8,128)(2,1)S(1)} %collective-permute-done.3.refs_4_, ...), custom_call_target="tpu_custom_call" | custom-call | flops 1000000000 | bytes 4194304 | tf_op jit(solution)/shard_map/attend0/pallas_call | solution.py:292
  50.2 0.1 collective-permute-done.8.in1
  50.3 0.1 join.1.joined
  50.4 4.3 %collective-permute-done.11.in0 = bf16[136,1024]{1,0:T(8,128)(2,1)S(1)} collective-permute-done((bf16[136,1024]{1,0:T(8,128)(2,1)S(1)}, bf16[136,1024]{1,0:T(8,128)(2,1)S(1)}, u32[]{:S(2)}, u32[]{:S(2)}) %collective-permute-start.11) | collective-permute-done | bytes 278560 | tf_op jit(solution)/shard_map/ppermute | solution.py:244
  54.7 0.3 fold.1
  54.9 18.8 %all_to_all.10.in_ref = bf16[32,40,128]{2,1,0:T(8,128)(2,1)S(1)} all-to-all(bf16[32,40,128]{2,1,0:T(8,128)(2,1)S(1)} %fold.1), channel_id=1, replica_groups=mesh['z'=8,'y'=4,'xh'=2,'core'=2,'kvh'=2] {'z','xh','kvh'}, dimensions={0} | all-to-all | bytes 655360 | tf_op jit(solution)/shard_map/all_to_all | solution.py:329
  73.8 1.1 %finish.1 = bf16[1,64,128]{2,1,0:T(8,128)(2,1)} custom-call(bf16[32,40,128]{2,1,0:T(8,128)(2,1)S(1)} %all_to_all.10.in_ref), custom_call_target="tpu_custom_call" | custom-call | tf_op jit(solution)/shard_map/finish/pallas_call | solution.py:330
  (20 shorter events, 0.2 us)
Async XLA Ops:
  0.0 18.2 %collective-permute-start.1 = (bf16[3072,128]{1,0:T(8,128)(2,1)}, bf16[3072,128]{1,0:T(8,128)(2,1)S(1)}, u32[]{:S(2)}, u32[]{:S(2)}) collective-permute-start(bf16[3072,128]{1,0:T(8,128)(2,1)} %bitcast.15), channel_id=1, source_target_pairs={{2,0},{0,2},{3,1},{1,3},{6,4},{4,6},{7,5},{5,7},{10,8},{8,10},{11,... | collective-permute-start | bytes 2359304 | tf_op jit(solution)/shard_map/ppermute | solution.py:244
  0.0 18.2 %collective-permute-start.2 = (bf16[3072,128]{1,0:T(8,128)(2,1)}, bf16[3072,128]{1,0:T(8,128)(2,1)S(1)}, u32[]{:S(2)}, u32[]{:S(2)}) collective-permute-start(bf16[3072,128]{1,0:T(8,128)(2,1)} %bitcast.14), channel_id=1, source_target_pairs={{2,0},{0,2},{3,1},{1,3},{6,4},{4,6},{7,5},{5,7},{10,8},{8,10},{11,... | collective-permute-start | bytes 2359304 | tf_op jit(solution)/shard_map/ppermute | solution.py:244
  1.9 16.3 %all-to-all-start = ((bf16[8,2,2,16,128]{4,3,2,1,0:T(8,128)(2,1)}), bf16[8,2,2,16,128]{4,3,2,1,0:T(8,128)(2,1)S(1)}, u32[]{:S(2)}, u32[]{:S(2)}) async-start(bf16[8,2,2,16,128]{4,3,2,1,0:T(8,128)(2,1)} %broadcast_in_dim.2), calls=%async_computation | async-start | bytes 262144 | tf_op jit(solution)/shard_map/all_to_all | solution.py:265
  10.5 1.3 %collective-permute-start = (s32[12]{0:T(128)}, s32[12]{0:T(128)S(1)}, u32[]{:S(2)}, u32[]{:S(2)}) collective-permute-start(s32[12]{0:T(128)} %own_ids.1), channel_id=1, source_target_pairs={{2,0},{0,2},{3,1},{1,3},{6,4},{4,6},{7,5},{5,7},{10,8},{8,10},{11,... | collective-permute-start | bytes 152 | tf_op jit(solution)/shard_map/ppermute | solution.py:244
  11.7 0.7 copy-start
  12.4 0.7 copy-start.2
  13.0 0.7 copy-start.4
  13.7 16.8 %copy-start.5 = (bf16[1536,2,128]{2,1,0:T(2,128)(2,1)S(1)}, bf16[1536,2,128]{2,1,0:T(2,128)(2,1)}, u32[]{:S(2)}) copy-start(bf16[1536,2,128]{2,1,0:T(2,128)(2,1)} %param.7) | copy-start | bytes 2359300
  18.2 7.4 %collective-permute-start.3 = (bf16[8,2,2,16,128]{4,3,2,1,0:T(8,128)(2,1)S(1)}, bf16[8,2,2,16,128]{4,3,2,1,0:T(8,128)(2,1)S(1)}, u32[]{:S(2)}, u32[]{:S(2)}) collective-permute-start(bf16[8,2,2,16,128]{4,3,2,1,0:T(8,128)(2,1)S(1)} %all-to-all-done.refs_3_), channel_id=1, source_target_pairs={{4,0},{0,4},{5,1},{1,5},{6,2},{2,6},{7,3},{3,7},{12,8},{8,12},{13,... | collective-permute-start | bytes 393224 | tf_op jit(solution)/shard_map/ppermute | solution.py:244
  21.3 5.5 %collective-permute-start.4 = (bf16[8,2,2,16,128]{4,3,2,1,0:T(8,128)(2,1)S(1)}, bf16[8,2,2,16,128]{4,3,2,1,0:T(8,128)(2,1)S(1)}, u32[]{:S(2)}, u32[]{:S(2)}) collective-permute-start(bf16[8,2,2,16,128]{4,3,2,1,0:T(8,128)(2,1)S(1)} %all-to-all-done.refs_3_), channel_id=1, source_target_pairs={{8,0},{16,8},{24,16},{0,24},{9,1},{17,9},{25,17},{1,25},{10,2},{18... | collective-permute-start | bytes 393224 | tf_op jit(solution)/shard_map/ppermute | solution.py:244
  24.3 6.2 %collective-permute-start.5 = (bf16[8,2,2,16,128]{4,3,2,1,0:T(8,128)(2,1)S(1)}, bf16[8,2,2,16,128]{4,3,2,1,0:T(8,128)(2,1)S(1)}, u32[]{:S(2)}, u32[]{:S(2)}) collective-permute-start(bf16[8,2,2,16,128]{4,3,2,1,0:T(8,128)(2,1)S(1)} %all-to-all-done.refs_3_), channel_id=1, source_target_pairs={{24,0},{0,8},{8,16},{16,24},{25,1},{1,9},{9,17},{17,25},{26,2},{2,... | collective-permute-start | bytes 393224 | tf_op jit(solution)/shard_map/ppermute | solution.py:244
  30.5 6.9 %collective-permute-start.6 = (bf16[8,2,2,16,128]{4,3,2,1,0:T(8,128)(2,1)S(1)}, bf16[8,2,2,16,128]{4,3,2,1,0:T(8,128)(2,1)S(1)}, u32[]{:S(2)}, u32[]{:S(2)}) collective-permute-start(bf16[8,2,2,16,128]{4,3,2,1,0:T(8,128)(2,1)S(1)} %collective-permute-done.3.refs_4_), channel_id=1, source_target_pairs={{24,0},{0,8},{8,16},{16,24},{25,1},{1,9},{9,17},{17,25},{26,2},{2,... | collective-permute-start | bytes 393224 | tf_op jit(solution)/shard_map/ppermute | solution.py:244
  30.7 7.0 %collective-permute-start.7 = (bf16[8,2,2,16,128]{4,3,2,1,0:T(8,128)(2,1)S(1)}, bf16[8,2,2,16,128]{4,3,2,1,0:T(8,128)(2,1)S(1)}, u32[]{:S(2)}, u32[]{:S(2)}) collective-permute-start(bf16[8,2,2,16,128]{4,3,2,1,0:T(8,128)(2,1)S(1)} %collective-permute-done.3.refs_4_), channel_id=1, source_target_pairs={{8,0},{16,8},{24,16},{0,24},{9,1},{17,9},{25,17},{1,25},{10,2},{18... | collective-permute-start | bytes 393224 | tf_op jit(solution)/shard_map/ppermute | solution.py:244
  34.0 3.7 %copy-start.1 = (s32[4]{0:T(128)S(1)}, s32[4]{0:T(128)}, u32[]{:S(2)}) copy-start(s32[4]{0:T(128)} %refs_1_.5) | copy-start | bytes 52
  34.0 3.7 %copy-start.3 = (s32[4]{0:T(128)S(1)}, s32[4]{0:T(128)}, u32[]{:S(2)}) copy-start(s32[4]{0:T(128)} %refs_2_.5) | copy-start | bytes 52
  35.5 5.0 %collective-permute-start.9 = (bf16[8,2,2,16,128]{4,3,2,1,0:T(8,128)(2,1)S(1)}, bf16[8,2,2,16,128]{4,3,2,1,0:T(8,128)(2,1)S(1)}, u32[]{:S(2)}, u32[]{:S(2)}) collective-permute-start(bf16[8,2,2,16,128]{4,3,2,1,0:T(8,128)(2,1)S(1)} %collective-permute-done.4.refs_3_), channel_id=1, source_target_pairs={{8,0},{16,8},{24,16},{0,24},{9,1},{17,9},{25,17},{1,25},{10,2},{18... | collective-permute-start | bytes 393224 | tf_op jit(solution)/shard_map/ppermute | solution.py:244
  37.3 7.0 %collective-permute-start.10 = (bf16[8,2,2,16,128]{4,3,2,1,0:T(8,128)(2,1)S(1)}, bf16[8,2,2,16,128]{4,3,2,1,0:T(8,128)(2,1)S(1)}, u32[]{:S(2)}, u32[]{:S(2)}) collective-permute-start(bf16[8,2,2,16,128]{4,3,2,1,0:T(8,128)(2,1)S(1)} %collective-permute-done.6.refs_6_), channel_id=1, source_target_pairs={{24,0},{0,8},{8,16},{16,24},{25,1},{1,9},{9,17},{17,25},{26,2},{2,... | collective-permute-start | bytes 393224 | tf_op jit(solution)/shard_map/ppermute | solution.py:244
  40.4 9.8 %collective-permute-start.8 = (bf16[136,1024]{1,0:T(8,128)(2,1)S(1)}, bf16[136,1024]{1,0:T(8,128)(2,1)S(1)}, u32[]{:S(2)}, u32[]{:S(2)}) collective-permute-start(bf16[136,1024]{1,0:T(8,128)(2,1)S(1)} %get-tuple-element.37), channel_id=1, source_target_pairs={{24,0},{0,8},{8,16},{16,24},{25,1},{1,9},{9,17},{17,25},{26,2},{2,... | collective-permute-start | bytes 835592 | tf_op jit(solution)/shard_map/ppermute | solution.py:244
  46.5 8.1 %collective-permute-start.11 = (bf16[136,1024]{1,0:T(8,128)(2,1)S(1)}, bf16[136,1024]{1,0:T(8,128)(2,1)S(1)}, u32[]{:S(2)}, u32[]{:S(2)}) collective-permute-start(bf16[136,1024]{1,0:T(8,128)(2,1)S(1)} %attend2.1), channel_id=1, source_target_pairs={{16,0},{24,8},{0,16},{8,24},{17,1},{25,9},{1,17},{9,25},{18,2},{26... | collective-permute-start | bytes 835592 | tf_op jit(solution)/shard_map/ppermute | solution.py:244
  46.6 8.0 %collective-permute-start.12 = (bf16[136,1024]{1,0:T(8,128)(2,1)S(1)}, bf16[136,1024]{1,0:T(8,128)(2,1)S(1)}, u32[]{:S(2)}, u32[]{:S(2)}) collective-permute-start(bf16[136,1024]{1,0:T(8,128)(2,1)S(1)} %get-tuple-element.40), channel_id=1, source_target_pairs={{8,0},{16,8},{24,16},{0,24},{9,1},{17,9},{25,17},{1,25},{10,2},{18... | collective-permute-start | bytes 835592 | tf_op jit(solution)/shard_map/ppermute | solution.py:244

commit v5 on v3

--- a/solution.py
+++ b/solution.py
@@ -36,14 +36,14 @@
     return hi, mid, rest - mid
 
 
-def select_kernel(own_ids, peer_ids, cached, counts, list_ref):
+def select_kernel(meta, list_ref):
     blocks_per_seq = (BOTH * 64) // SEQS
     found = []
     for b in range(BOTH):
-        ident = own_ids[b] if b < OWN else peer_ids[b - OWN]
+        ident = meta[b]
         s = sum((ident >= n * blocks_per_seq).astype(jnp.int32) for n in range(1, SEQS))
         number = ident - s * blocks_per_seq
-        found.append((s, number, number * BLK <= cached[s] + counts[s] - 1))
+        found.append((s, number, number * BLK <= meta[BOTH + s] + meta[BOTH + SEQS + s] - 1))
     at = []
     end = jnp.int32(0)
     for n in range(SEQS):
@@ -248,6 +248,10 @@
     return pltpu.CompilerParams(vmem_limit_bytes=mib << 20)
 
 
+def by_head(x):
+    return jnp.transpose(x.reshape(OWN * BLK, HEADS, HD), (1, 0, 2))
+
+
 def per_device(queries, k_cache, v_cache, block_owner, cached_lens, new_counts):
     k0, v0 = (x.reshape(OWN * WIDE, HD) for x in (k_cache, v_cache))
     k1, v1, ids = (turn(x, "core", 2, 1) for x in (k0, v0, block_owner))
@@ -255,18 +259,17 @@
     lists = pl.pallas_call(
         select_kernel,
         out_shape=jax.ShapeDtypeStruct((3, 32), jnp.int32),
-        in_specs=[SMEM] * 4,
+        in_specs=[SMEM],
         out_specs=SMEM,
         compiler_params=params(12),
         name="select",
-    )(block_owner, ids, cached_lens, new_counts)
+    )(jnp.concatenate([block_owner, ids, cached_lens, new_counts]))
 
     q = jnp.broadcast_to(queries[None], (8,) + queries.shape)
     q = lax.all_to_all(q, "z", split_axis=0, concat_axis=0, tiled=True)
-    q, lists, *caches = lax.optimization_barrier((q, lists, k0, k1, v0, v1))
-    k0, k1, v0, v1 = (
-        jnp.transpose(x.reshape(OWN * BLK, HEADS, HD), (1, 0, 2)) for x in caches
-    )
+    k0, v0 = by_head(k0), by_head(v0)
+    q, lists, k0, k1, v0, v1 = lax.optimization_barrier((q, lists, k0, k1, v0, v1))
+    k1, v1 = by_head(k1), by_head(v1)
     k, v = pl.pallas_call(
         pack_kernel,
         out_shape=[

time: 72.8 us -> 72.2 us (level)
  waiting for transfers between devices: 14.6 us -> 17.8 us
  starting transfers between devices: 24.9 us -> 22.1 us
  Pallas kernels: 10.2 us -> 12.1 us
  local copies, waits for them, and re-layouts: 4.9 us -> 3.18 us
  blocking collectives: 18 us -> 16.4 us
    ppermute x13, starting transfers between devices: 16.3 us -> 13.6 us  [turn(): return lax.ppermute(x, axis, [((i + step) % size, i) for i in range(size)])]
    unnamed x12 -> x6, local copies, waits for them, and re-layouts: 1.98 us -> 0.01 us
    all_to_all x1, waiting for transfers between devices: 2.64 us -> 4.27 us  [per_device(): q = lax.all_to_all(q, 'z', split_axis=0, concat_axis=0, tiled=True)]
    pallas_call x3, Pallas kernels: 5.58 us -> 7.18 us  [attend(): pl.pallas_call(functools.partial(attend_kernel, steps), out_shape=[jax.Sh...]
    all_to_all x1, blocking collectives: 18 us -> 16.4 us  [per_device(): lax.all_to_all(msg, ('z', 'xh', 'kvh'), split_axis=0, concat_axis=0, tile...]
    ppermute x13, waiting for transfers between devices: 12 us -> 13.5 us  [turn(): return lax.ppermute(x, axis, [((i + step) % size, i) for i in range(size)])]
    transpose x2 -> x1, local copies, waits for them, and re-layouts: 1.54 us -> 1.57 us  [by_head(): return jnp.transpose(x.reshape(OWN * BLK, HEADS, HD), (1, 0, 2))]
  transfers between devices with their start and end apart: 14 -> 14, of which waited for: 6 -> 7; matrix products, arithmetic and copies ran while one was open for 4% -> 5% of each run, Pallas kernels for 12% -> 15%
where the time goes in v5:
time: 72.2 us; the launch traced here: 71.8 us
  starting transfers between devices  22.1 us (31%)
  waiting for transfers between devices  17.8 us (25%)
  blocking collectives  16.4 us (23%)
  Pallas kernels  12.1 us (17%)
  local copies, waits for them, and re-layouts  3.18 us (4%)
    all_to_all x1, blocking collectives, per_device(): lax.all_to_all(msg, ('z', 'xh', 'kvh'), split_axis=0, concat_axis=0, tile...  16.4 us
    ppermute x13, starting transfers between devices, turn(): return lax.ppermute(x, axis, [((i + step) % size, i) for i in range(size)])  13.6 us
    ppermute x13, waiting for transfers between devices, turn(): return lax.ppermute(x, axis, [((i + step) % size, i) for i in range(size)])  13.5 us
    all_to_all x1, starting transfers between devices, per_device(): q = lax.all_to_all(q, 'z', split_axis=0, concat_axis=0, tiled=True)  8.57 us
    pallas_call x3, Pallas kernels, attend(): pl.pallas_call(functools.partial(attend_kernel, steps), out_shape=[jax.Sh...  7.18 us
    all_to_all x1, waiting for transfers between devices, per_device(): q = lax.all_to_all(q, 'z', split_axis=0, concat_axis=0, tiled=True)  4.27 us
    pallas_call x1, Pallas kernels, per_device(): pl.pallas_call(select_kernel, out_shape=jax.ShapeDtypeStruct((3, 32), jnp...  1.9 us
    transpose x1, local copies, waits for them, and re-layouts, by_head(): return jnp.transpose(x.reshape(OWN * BLK, HEADS, HD), (1, 0, 2))  1.57 us
  transfers between devices with their start and end apart: 14, of which 7 were waited for; matrix products, arithmetic and copies ran while one was open for 5% of the time, Pallas kernels for 15%

profile of v5, /device:TPU:32, one launch (start us, length us, event | category | flops | bytes accessed | tf_op | source)
XLA Modules:
  0.0 71.8 jit_solution(3707255372963974265)
XLA Ops:
  0.0 0.1 collective-permute-start.1
  0.1 0.5 collective-permute-start.2
  0.6 1.4 %broadcast_in_dim.2 = bf16[8,2,2,16,128]{4,3,2,1,0:T(8,128)(2,1)} broadcast(bf16[2,2,16,128]{3,2,1,0:T(8,128)(2,1)} %param.6), dimensions={1,2,3,4} | broadcast | bytes 147456 | tf_op jit(solution)/shard_map/broadcast_in_dim | solution.py:268
  2.0 8.6 %all-to-all-start = ((bf16[8,2,2,16,128]{4,3,2,1,0:T(8,128)(2,1)}), bf16[8,2,2,16,128]{4,3,2,1,0:T(8,128)(2,1)S(1)}, u32[]{:S(2)}, u32[]{:S(2)}) async-start(bf16[8,2,2,16,128]{4,3,2,1,0:T(8,128)(2,1)} %broadcast_in_dim.2), calls=%async_computation | async-start | bytes 262144 | tf_op jit(solution)/shard_map/all_to_all | solution.py:269
  10.6 1.6 %copy_bitcast_fusion.2 = (bf16[2,1536,128]{2,1,0:T(8,128)(2,1)S(1)}, bf16[2,1536,128]{2,1,0:T(8,128)(2,1)S(1)}) fusion(bf16[1536,2,128]{2,1,0:T(2,128)(2,1)} %param.8, bf16[1536,2,128]{2,1,0:T(2,128)(2,1)} %param.7), kind=kLoop, calls=%fused_computation.2 | loop fusion | bytes 3145728 | tf_op jit(solution)/shard_map/transpose | solution.py:252
  12.1 0.0 collective-permute-done
  12.2 0.1 pad_add_fusion.meta
  12.3 1.9 %select.1.lists.refs_0_ = s32[3,32]{1,0:T(4,128)S(1)} custom-call(s32[32]{0:T(128)S(1)} %pad_add_fusion.meta), custom_call_target="tpu_custom_call" | custom-call | tf_op jit(solution)/shard_map/select/pallas_call | solution.py:259
  14.2 4.3 %all-to-all-done.refs_3_ = bf16[8,2,2,16,128]{4,3,2,1,0:T(8,128)(2,1)S(1)} async-done(((bf16[8,2,2,16,128]{4,3,2,1,0:T(8,128)(2,1)}), bf16[8,2,2,16,128]{4,3,2,1,0:T(8,128)(2,1)S(1)}, u32[]{:S(2)}, u32[]{:S(2)}) %all-to-all-start) | async-done | bytes 131104 | tf_op jit(solution)/shard_map/all_to_all | solution.py:269
  18.4 3.0 %collective-permute-start.3 = (bf16[8,2,2,16,128]{4,3,2,1,0:T(8,128)(2,1)S(1)}, bf16[8,2,2,16,128]{4,3,2,1,0:T(8,128)(2,1)S(1)}, u32[]{:S(2)}, u32[]{:S(2)}) collective-permute-start(bf16[8,2,2,16,128]{4,3,2,1,0:T(8,128)(2,1)S(1)} %all-to-all-done.refs_3_), channel_id=1, source_target_pairs={{4,0},{0,4},{5,1},{1,5},{6,2},{2,6},{7,3},{3,7},{12,8},{8,12},{13,... | collective-permute-start | bytes 393224 | tf_op jit(solution)/shard_map/ppermute | solution.py:244
  21.5 3.0 %collective-permute-start.4 = (bf16[8,2,2,16,128]{4,3,2,1,0:T(8,128)(2,1)S(1)}, bf16[8,2,2,16,128]{4,3,2,1,0:T(8,128)(2,1)S(1)}, u32[]{:S(2)}, u32[]{:S(2)}) collective-permute-start(bf16[8,2,2,16,128]{4,3,2,1,0:T(8,128)(2,1)S(1)} %all-to-all-done.refs_3_), channel_id=1, source_target_pairs={{8,0},{16,8},{24,16},{0,24},{9,1},{17,9},{25,17},{1,25},{10,2},{18... | collective-permute-start | bytes 393224 | tf_op jit(solution)/shard_map/ppermute | solution.py:244
  24.5 0.1 copy.17
  24.6 0.1 copy.18
  24.7 1.6 %pack.1 = (bf16[14,2,256,128]{3,2,1,0:T(8,128)(2,1)S(1)}, bf16[14,2,128,256]{3,2,1,0:T(8,128)(2,1)S(1)}) custom-call(s32[3,32]{1,0:T(4,128)S(1)} %select.1.lists.refs_0_, bf16[2,1536,128]{2,1,0:T(8,128)(2,1)S(1)} %get-tuple-element.22.k0, bf16[2,1536,128]{2,1,0:T(8,128)(2,1)S(1)} %bitcast.15, bf16[2,1536,128]{2,1,0:T(8,128)(2,1)S(1)} %get-tuple-element.24.v0, ...), custom_call_target="tpu_custom_call" | custom-call | flops 1000000000 | bytes 4194304 | tf_op jit(solution)/shard_map/pack/pallas_call | solution.py:273
  26.3 0.7 %collective-permute-done.4.refs_3_ = bf16[8,2,2,16,128]{4,3,2,1,0:T(8,128)(2,1)S(1)} collective-permute-done((bf16[8,2,2,16,128]{4,3,2,1,0:T(8,128)(2,1)S(1)}, bf16[8,2,2,16,128]{4,3,2,1,0:T(8,128)(2,1)S(1)}, u32[]{:S(2)}, u32[]{:S(2)}) %collective-permute-start.4) | collective-permute-done | bytes 131104 | tf_op jit(solution)/shard_map/ppermute | solution.py:244
  27.0 3.7 %collective-permute-done.5.refs_5_ = bf16[8,2,2,16,128]{4,3,2,1,0:T(8,128)(2,1)S(1)} collective-permute-done((bf16[8,2,2,16,128]{4,3,2,1,0:T(8,128)(2,1)S(1)}, bf16[8,2,2,16,128]{4,3,2,1,0:T(8,128)(2,1)S(1)}, u32[]{:S(2)}, u32[]{:S(2)}) %collective-permute-start.5) | collective-permute-done | bytes 131104 | tf_op jit(solution)/shard_map/ppermute | solution.py:244
  30.7 3.2 %collective-permute-start.6 = (bf16[8,2,2,16,128]{4,3,2,1,0:T(8,128)(2,1)S(1)}, bf16[8,2,2,16,128]{4,3,2,1,0:T(8,128)(2,1)S(1)}, u32[]{:S(2)}, u32[]{:S(2)}) collective-permute-start(bf16[8,2,2,16,128]{4,3,2,1,0:T(8,128)(2,1)S(1)} %collective-permute-done.3.refs_4_), channel_id=1, source_target_pairs={{8,0},{16,8},{24,16},{0,24},{9,1},{17,9},{25,17},{1,25},{10,2},{18... | collective-permute-start | bytes 393224 | tf_op jit(solution)/shard_map/ppermute | solution.py:244
  33.9 0.0 collective-permute-start.10
  33.9 3.6 %collective-permute-done.7.refs_6_ = bf16[8,2,2,16,128]{4,3,2,1,0:T(8,128)(2,1)S(1)} collective-permute-done((bf16[8,2,2,16,128]{4,3,2,1,0:T(8,128)(2,1)S(1)}, bf16[8,2,2,16,128]{4,3,2,1,0:T(8,128)(2,1)S(1)}, u32[]{:S(2)}, u32[]{:S(2)}) %collective-permute-start.7) | collective-permute-done | bytes 131104 | tf_op jit(solution)/shard_map/ppermute | solution.py:244
  37.6 2.8 %attend13.1 = (bf16[136,1024]{1,0:T(8,128)(2,1)S(1)}, bf16[136,1024]{1,0:T(8,128)(2,1)S(1)}) custom-call(s32[3,32]{1,0:T(4,128)S(1)} %select.1.lists.refs_0_, s32[4]{0:T(128)S(1)} %copy-done.1, s32[4]{0:T(128)S(1)} %copy-done, bf16[8,2,2,16,128]{4,3,2,1,0:T(8,128)(2,1)S(1)} %collective-permute-done.4.refs_3_, ...), custom_call_target="tpu_custom_call" | custom-call | flops 1000000000 | bytes 4194304 | tf_op jit(solution)/shard_map/attend13/pallas_call | solution.py:294
  40.3 0.1 collective-permute-start.8
  40.4 3.2 %collective-permute-start.9 = (bf16[136,1024]{1,0:T(8,128)(2,1)S(1)}, bf16[136,1024]{1,0:T(8,128)(2,1)S(1)}, u32[]{:S(2)}, u32[]{:S(2)}) collective-permute-start(bf16[136,1024]{1,0:T(8,128)(2,1)S(1)} %get-tuple-element.34), channel_id=1, source_target_pairs={{8,0},{16,8},{24,16},{0,24},{9,1},{17,9},{25,17},{1,25},{10,2},{18... | collective-permute-start | bytes 835592 | tf_op jit(solution)/shard_map/ppermute | solution.py:244
  43.6 0.1 collective-permute-done.11.refs_4_
  43.7 2.2 %attend2.1 = bf16[136,1024]{1,0:T(8,128)(2,1)S(1)} custom-call(s32[3,32]{1,0:T(4,128)S(1)} %select.1.lists.refs_0_, s32[4]{0:T(128)S(1)} %copy-done.1, s32[4]{0:T(128)S(1)} %copy-done, bf16[8,2,2,16,128]{4,3,2,1,0:T(8,128)(2,1)S(1)} %collective-permute-done.10.refs_3_, bf16[8,2,2,16,128]{4,3,2,1,0:T(8,128)(2,1)S(1)} %collective-permute-done.11.refs_4_, ...), custom_call_target="tpu_custom_call" | custom-call | flops 1000000000 | bytes 4194304 | tf_op jit(solution)/shard_map/attend2/pallas_call | solution.py:294
  45.9 0.3 collective-permute-start.12
  46.3 2.2 %attend0.1.in0 = bf16[136,1024]{1,0:T(8,128)(2,1)S(1)} custom-call(s32[3,32]{1,0:T(4,128)S(1)} %select.1.lists.refs_0_, s32[4]{0:T(128)S(1)} %copy-done.1, s32[4]{0:T(128)S(1)} %copy-done, bf16[8,2,2,16,128]{4,3,2,1,0:T(8,128)(2,1)S(1)} %all-to-all-done.refs_3_, bf16[8,2,2,16,128]{4,3,2,1,0:T(8,128)(2,1)S(1)} %collective-permute-done.3.refs_4_, ...), custom_call_target="tpu_custom_call" | custom-call | flops 1000000000 | bytes 4194304 | tf_op jit(solution)/shard_map/attend0/pallas_call | solution.py:294
  48.5 1.9 %collective-permute-done.8.in0 = bf16[136,1024]{1,0:T(8,128)(2,1)S(1)} collective-permute-done((bf16[136,1024]{1,0:T(8,128)(2,1)S(1)}, bf16[136,1024]{1,0:T(8,128)(2,1)S(1)}, u32[]{:S(2)}, u32[]{:S(2)}) %collective-permute-start.8) | collective-permute-done | bytes 278560 | tf_op jit(solution)/shard_map/ppermute | solution.py:244
  50.5 0.1 join.1.joined
  50.6 3.5 %collective-permute-done.12.in1 = bf16[136,1024]{1,0:T(8,128)(2,1)S(1)} collective-permute-done((bf16[136,1024]{1,0:T(8,128)(2,1)S(1)}, bf16[136,1024]{1,0:T(8,128)(2,1)S(1)}, u32[]{:S(2)}, u32[]{:S(2)}) %collective-permute-start.12) | collective-permute-done | bytes 278560 | tf_op jit(solution)/shard_map/ppermute | solution.py:244
  54.1 0.3 fold.1
  54.4 16.4 %all_to_all.10.in_ref = bf16[32,40,128]{2,1,0:T(8,128)(2,1)S(1)} all-to-all(bf16[32,40,128]{2,1,0:T(8,128)(2,1)S(1)} %fold.1), channel_id=1, replica_groups=mesh['z'=8,'y'=4,'xh'=2,'core'=2,'kvh'=2] {'z','xh','kvh'}, dimensions={0} | all-to-all | bytes 655360 | tf_op jit(solution)/shard_map/all_to_all | solution.py:330
  70.7 1.1 %finish.1 = bf16[1,64,128]{2,1,0:T(8,128)(2,1)} custom-call(bf16[32,40,128]{2,1,0:T(8,128)(2,1)S(1)} %all_to_all.10.in_ref), custom_call_target="tpu_custom_call" | custom-call | tf_op jit(solution)/shard_map/finish/pallas_call | solution.py:331
  (16 shorter events, 0.0 us)
Async XLA Ops:
  0.0 12.2 %copy-start.2 = (s32[12]{0:T(128)S(1)}, s32[12]{0:T(128)}, u32[]{:S(2)}) copy-start(s32[12]{0:T(128)} %param.9) | copy-start | bytes 148
  0.0 12.2 %copy-start.1 = (s32[4]{0:T(128)S(1)}, s32[4]{0:T(128)}, u32[]{:S(2)}) copy-start(s32[4]{0:T(128)} %refs_1_.5) | copy-start | bytes 52
  0.0 12.2 %copy-start = (s32[4]{0:T(128)S(1)}, s32[4]{0:T(128)}, u32[]{:S(2)}) copy-start(s32[4]{0:T(128)} %refs_2_.5) | copy-start | bytes 52
  0.0 18.4 %collective-permute-start.1 = (bf16[3072,128]{1,0:T(8,128)(2,1)}, bf16[3072,128]{1,0:T(8,128)(2,1)S(1)}, u32[]{:S(2)}, u32[]{:S(2)}) collective-permute-start(bf16[3072,128]{1,0:T(8,128)(2,1)} %bitcast.18), channel_id=1, source_target_pairs={{2,0},{0,2},{3,1},{1,3},{6,4},{4,6},{7,5},{5,7},{10,8},{8,10},{11,... | collective-permute-start | bytes 2359304 | tf_op jit(solution)/shard_map/ppermute | solution.py:244
  0.1 18.3 %collective-permute-start.2 = (bf16[3072,128]{1,0:T(8,128)(2,1)}, bf16[3072,128]{1,0:T(8,128)(2,1)S(1)}, u32[]{:S(2)}, u32[]{:S(2)}) collective-permute-start(bf16[3072,128]{1,0:T(8,128)(2,1)} %bitcast.19), channel_id=1, source_target_pairs={{2,0},{0,2},{3,1},{1,3},{6,4},{4,6},{7,5},{5,7},{10,8},{8,10},{11,... | collective-permute-start | bytes 2359304 | tf_op jit(solution)/shard_map/ppermute | solution.py:244
  2.0 16.4 %all-to-all-start = ((bf16[8,2,2,16,128]{4,3,2,1,0:T(8,128)(2,1)}), bf16[8,2,2,16,128]{4,3,2,1,0:T(8,128)(2,1)S(1)}, u32[]{:S(2)}, u32[]{:S(2)}) async-start(bf16[8,2,2,16,128]{4,3,2,1,0:T(8,128)(2,1)} %broadcast_in_dim.2), calls=%async_computation | async-start | bytes 262144 | tf_op jit(solution)/shard_map/all_to_all | solution.py:269
  10.6 1.6 %collective-permute-start = (s32[12]{0:T(128)}, s32[12]{0:T(128)S(1)}, u32[]{:S(2)}, u32[]{:S(2)}) collective-permute-start(s32[12]{0:T(128)} %param.9), channel_id=1, source_target_pairs={{2,0},{0,2},{3,1},{1,3},{6,4},{4,6},{7,5},{5,7},{10,8},{8,10},{11,... | collective-permute-start | bytes 152 | tf_op jit(solution)/shard_map/ppermute | solution.py:244
  18.4 7.8 %collective-permute-start.3 = (bf16[8,2,2,16,128]{4,3,2,1,0:T(8,128)(2,1)S(1)}, bf16[8,2,2,16,128]{4,3,2,1,0:T(8,128)(2,1)S(1)}, u32[]{:S(2)}, u32[]{:S(2)}) collective-permute-start(bf16[8,2,2,16,128]{4,3,2,1,0:T(8,128)(2,1)S(1)} %all-to-all-done.refs_3_), channel_id=1, source_target_pairs={{4,0},{0,4},{5,1},{1,5},{6,2},{2,6},{7,3},{3,7},{12,8},{8,12},{13,... | collective-permute-start | bytes 393224 | tf_op jit(solution)/shard_map/ppermute | solution.py:244
  21.5 5.5 %collective-permute-start.4 = (bf16[8,2,2,16,128]{4,3,2,1,0:T(8,128)(2,1)S(1)}, bf16[8,2,2,16,128]{4,3,2,1,0:T(8,128)(2,1)S(1)}, u32[]{:S(2)}, u32[]{:S(2)}) collective-permute-start(bf16[8,2,2,16,128]{4,3,2,1,0:T(8,128)(2,1)S(1)} %all-to-all-done.refs_3_), channel_id=1, source_target_pairs={{8,0},{16,8},{24,16},{0,24},{9,1},{17,9},{25,17},{1,25},{10,2},{18... | collective-permute-start | bytes 393224 | tf_op jit(solution)/shard_map/ppermute | solution.py:244
  24.5 6.2 %collective-permute-start.5 = (bf16[8,2,2,16,128]{4,3,2,1,0:T(8,128)(2,1)S(1)}, bf16[8,2,2,16,128]{4,3,2,1,0:T(8,128)(2,1)S(1)}, u32[]{:S(2)}, u32[]{:S(2)}) collective-permute-start(bf16[8,2,2,16,128]{4,3,2,1,0:T(8,128)(2,1)S(1)} %all-to-all-done.refs_3_), channel_id=1, source_target_pairs={{24,0},{0,8},{8,16},{16,24},{25,1},{1,9},{9,17},{17,25},{26,2},{2,... | collective-permute-start | bytes 393224 | tf_op jit(solution)/shard_map/ppermute | solution.py:244
  30.7 6.9 %collective-permute-start.7 = (bf16[8,2,2,16,128]{4,3,2,1,0:T(8,128)(2,1)S(1)}, bf16[8,2,2,16,128]{4,3,2,1,0:T(8,128)(2,1)S(1)}, u32[]{:S(2)}, u32[]{:S(2)}) collective-permute-start(bf16[8,2,2,16,128]{4,3,2,1,0:T(8,128)(2,1)S(1)} %collective-permute-done.3.refs_4_), channel_id=1, source_target_pairs={{24,0},{0,8},{8,16},{16,24},{25,1},{1,9},{9,17},{17,25},{26,2},{2,... | collective-permute-start | bytes 393224 | tf_op jit(solution)/shard_map/ppermute | solution.py:244
  30.7 6.9 %collective-permute-start.6 = (bf16[8,2,2,16,128]{4,3,2,1,0:T(8,128)(2,1)S(1)}, bf16[8,2,2,16,128]{4,3,2,1,0:T(8,128)(2,1)S(1)}, u32[]{:S(2)}, u32[]{:S(2)}) collective-permute-start(bf16[8,2,2,16,128]{4,3,2,1,0:T(8,128)(2,1)S(1)} %collective-permute-done.3.refs_4_), channel_id=1, source_target_pairs={{8,0},{16,8},{24,16},{0,24},{9,1},{17,9},{25,17},{1,25},{10,2},{18... | collective-permute-start | bytes 393224 | tf_op jit(solution)/shard_map/ppermute | solution.py:244
  33.9 9.7 %collective-permute-start.10 = (bf16[8,2,2,16,128]{4,3,2,1,0:T(8,128)(2,1)S(1)}, bf16[8,2,2,16,128]{4,3,2,1,0:T(8,128)(2,1)S(1)}, u32[]{:S(2)}, u32[]{:S(2)}) collective-permute-start(bf16[8,2,2,16,128]{4,3,2,1,0:T(8,128)(2,1)S(1)} %collective-permute-done.4.refs_3_), channel_id=1, source_target_pairs={{8,0},{16,8},{24,16},{0,24},{9,1},{17,9},{25,17},{1,25},{10,2},{18... | collective-permute-start | bytes 393224 | tf_op jit(solution)/shard_map/ppermute | solution.py:244
  37.6 6.2 %collective-permute-start.11 = (bf16[8,2,2,16,128]{4,3,2,1,0:T(8,128)(2,1)S(1)}, bf16[8,2,2,16,128]{4,3,2,1,0:T(8,128)(2,1)S(1)}, u32[]{:S(2)}, u32[]{:S(2)}) collective-permute-start(bf16[8,2,2,16,128]{4,3,2,1,0:T(8,128)(2,1)S(1)} %collective-permute-done.7.refs_6_), channel_id=1, source_target_pairs={{24,0},{0,8},{8,16},{16,24},{25,1},{1,9},{9,17},{17,25},{26,2},{2,... | collective-permute-start | bytes 393224 | tf_op jit(solution)/shard_map/ppermute | solution.py:244
  40.3 10.1 %collective-permute-start.8 = (bf16[136,1024]{1,0:T(8,128)(2,1)S(1)}, bf16[136,1024]{1,0:T(8,128)(2,1)S(1)}, u32[]{:S(2)}, u32[]{:S(2)}) collective-permute-start(bf16[136,1024]{1,0:T(8,128)(2,1)S(1)} %get-tuple-element.33), channel_id=1, source_target_pairs={{24,0},{0,8},{8,16},{16,24},{25,1},{1,9},{9,17},{17,25},{26,2},{2,... | collective-permute-start | bytes 835592 | tf_op jit(solution)/shard_map/ppermute | solution.py:244
  40.4 10.0 %collective-permute-start.9 = (bf16[136,1024]{1,0:T(8,128)(2,1)S(1)}, bf16[136,1024]{1,0:T(8,128)(2,1)S(1)}, u32[]{:S(2)}, u32[]{:S(2)}) collective-permute-start(bf16[136,1024]{1,0:T(8,128)(2,1)S(1)} %get-tuple-element.34), channel_id=1, source_target_pairs={{8,0},{16,8},{24,16},{0,24},{9,1},{17,9},{25,17},{1,25},{10,2},{18... | collective-permute-start | bytes 835592 | tf_op jit(solution)/shard_map/ppermute | solution.py:244
  45.9 8.1 %collective-permute-start.12 = (bf16[136,1024]{1,0:T(8,128)(2,1)S(1)}, bf16[136,1024]{1,0:T(8,128)(2,1)S(1)}, u32[]{:S(2)}, u32[]{:S(2)}) collective-permute-start(bf16[136,1024]{1,0:T(8,128)(2,1)S(1)} %attend2.1), channel_id=1, source_target_pairs={{16,0},{24,8},{0,16},{8,24},{17,1},{25,9},{1,17},{9,25},{18,2},{26... | collective-permute-start | bytes 835592 | tf_op jit(solution)/shard_map/ppermute | solution.py:244

commit v6 on v5

--- a/solution.py
+++ b/solution.py
@@ -282,9 +282,8 @@
         cost_estimate=COST,
         name="pack",
     )(lists, k0, k1, v0, v1)
-    over, near, back, k, v = lax.optimization_barrier(
-        (turn(q, "xh", 2, 1), turn(q, "y", 4, 1), turn(q, "y", 4, 3), k, v)
-    )
+    over, k, v = lax.optimization_barrier((turn(q, "xh", 2, 1), k, v))
+    near, back = lax.optimization_barrier((turn(q, "y", 4, 1), turn(q, "y", 4, 3)))
     near, back = [near, turn(over, "y", 4, 1)], [back, turn(over, "y", 4, 3)]
     qs = [[q, over], near, [turn(near[0], "y", 4, 1), turn(back[1], "y", 4, 3)], back]
 

time: 72.2 us -> 69.9 us (0.968)
  waiting for transfers between devices: 17.8 us -> 13.3 us
  starting transfers between devices: 22.1 us -> 23.3 us
    ppermute x13, waiting for transfers between devices: 13.5 us -> 9.02 us  [turn(): return lax.ppermute(x, axis, [((i + step) % size, i) for i in range(size)])]
    ppermute x13, starting transfers between devices: 13.6 us -> 14.8 us  [turn(): return lax.ppermute(x, axis, [((i + step) % size, i) for i in range(size)])]
  transfers between devices with their start and end apart: 14 -> 14, of which waited for: 7 -> 7; matrix products, arithmetic and copies ran while one was open for 5% -> 5% of each run, Pallas kernels for 15% -> 16%
where the time goes in v6:
time: 69.9 us; the launch traced here: 69.2 us
  starting transfers between devices  23.3 us (33%)
  blocking collectives  17.1 us (24%)
  waiting for transfers between devices  13.3 us (19%)
  Pallas kernels  12.1 us (17%)
  local copies, waits for them, and re-layouts  3.18 us (5%)
    all_to_all x1, blocking collectives, per_device(): lax.all_to_all(msg, ('z', 'xh', 'kvh'), split_axis=0, concat_axis=0, tile...  17.1 us
    ppermute x13, starting transfers between devices, turn(): return lax.ppermute(x, axis, [((i + step) % size, i) for i in range(size)])  14.8 us
    ppermute x13, waiting for transfers between devices, turn(): return lax.ppermute(x, axis, [((i + step) % size, i) for i in range(size)])  9.02 us
    all_to_all x1, starting transfers between devices, per_device(): q = lax.all_to_all(q, 'z', split_axis=0, concat_axis=0, tiled=True)  8.57 us
    pallas_call x3, Pallas kernels, attend(): pl.pallas_call(functools.partial(attend_kernel, steps), out_shape=[jax.Sh...  7.18 us
    all_to_all x1, waiting for transfers between devices, per_device(): q = lax.all_to_all(q, 'z', split_axis=0, concat_axis=0, tiled=True)  4.27 us
    pallas_call x1, Pallas kernels, per_device(): pl.pallas_call(select_kernel, out_shape=jax.ShapeDtypeStruct((3, 32), jnp...  1.9 us
    transpose x1, local copies, waits for them, and re-layouts, by_head(): return jnp.transpose(x.reshape(OWN * BLK, HEADS, HD), (1, 0, 2))  1.57 us
  transfers between devices with their start and end apart: 14, of which 7 were waited for; matrix products, arithmetic and copies ran while one was open for 5% of the time, Pallas kernels for 16%

profile of v6, /device:TPU:32, one launch (start us, length us, event | category | flops | bytes accessed | tf_op | source)
XLA Modules:
  0.0 69.2 jit_solution(6159237682424250547)
XLA Ops:
  0.0 0.1 collective-permute-start.1
  0.1 0.5 collective-permute-start.2
  0.6 1.4 %broadcast_in_dim.2 = bf16[8,2,2,16,128]{4,3,2,1,0:T(8,128)(2,1)} broadcast(bf16[2,2,16,128]{3,2,1,0:T(8,128)(2,1)} %param.6), dimensions={1,2,3,4} | broadcast | bytes 147456 | tf_op jit(solution)/shard_map/broadcast_in_dim | solution.py:268
  2.0 8.6 %all-to-all-start = ((bf16[8,2,2,16,128]{4,3,2,1,0:T(8,128)(2,1)}), bf16[8,2,2,16,128]{4,3,2,1,0:T(8,128)(2,1)S(1)}, u32[]{:S(2)}, u32[]{:S(2)}) async-start(bf16[8,2,2,16,128]{4,3,2,1,0:T(8,128)(2,1)} %broadcast_in_dim.2), calls=%async_computation | async-start | bytes 262144 | tf_op jit(solution)/shard_map/all_to_all | solution.py:269
  10.6 1.6 %copy_bitcast_fusion.2 = (bf16[2,1536,128]{2,1,0:T(8,128)(2,1)S(1)}, bf16[2,1536,128]{2,1,0:T(8,128)(2,1)S(1)}) fusion(bf16[1536,2,128]{2,1,0:T(2,128)(2,1)} %param.8, bf16[1536,2,128]{2,1,0:T(2,128)(2,1)} %param.7), kind=kLoop, calls=%fused_computation.2 | loop fusion | bytes 3145728 | tf_op jit(solution)/shard_map/transpose | solution.py:252
  12.3 1.9 %select.1.lists.refs_0_ = s32[3,32]{1,0:T(4,128)S(1)} custom-call(s32[32]{0:T(128)S(1)} %pad_add_fusion.meta), custom_call_target="tpu_custom_call" | custom-call | tf_op jit(solution)/shard_map/select/pallas_call | solution.py:259
  14.2 4.3 %all-to-all-done.refs_3_ = bf16[8,2,2,16,128]{4,3,2,1,0:T(8,128)(2,1)S(1)} async-done(((bf16[8,2,2,16,128]{4,3,2,1,0:T(8,128)(2,1)}), bf16[8,2,2,16,128]{4,3,2,1,0:T(8,128)(2,1)S(1)}, u32[]{:S(2)}, u32[]{:S(2)}) %all-to-all-start) | async-done | bytes 131104 | tf_op jit(solution)/shard_map/all_to_all | solution.py:269
  18.4 3.0 %collective-permute-start.5 = (bf16[8,2,2,16,128]{4,3,2,1,0:T(8,128)(2,1)S(1)}, bf16[8,2,2,16,128]{4,3,2,1,0:T(8,128)(2,1)S(1)}, u32[]{:S(2)}, u32[]{:S(2)}) collective-permute-start(bf16[8,2,2,16,128]{4,3,2,1,0:T(8,128)(2,1)S(1)} %all-to-all-done.refs_3_), channel_id=1, source_target_pairs={{4,0},{0,4},{5,1},{1,5},{6,2},{2,6},{7,3},{3,7},{12,8},{8,12},{13,... | collective-permute-start | bytes 393224 | tf_op jit(solution)/shard_map/ppermute | solution.py:244
  21.5 3.0 %collective-permute-start.3 = (bf16[8,2,2,16,128]{4,3,2,1,0:T(8,128)(2,1)S(1)}, bf16[8,2,2,16,128]{4,3,2,1,0:T(8,128)(2,1)S(1)}, u32[]{:S(2)}, u32[]{:S(2)}) collective-permute-start(bf16[8,2,2,16,128]{4,3,2,1,0:T(8,128)(2,1)S(1)} %all-to-all-done.refs_3_), channel_id=1, source_target_pairs={{8,0},{16,8},{24,16},{0,24},{9,1},{17,9},{25,17},{1,25},{10,2},{18... | collective-permute-start | bytes 393224 | tf_op jit(solution)/shard_map/ppermute | solution.py:244
  24.5 0.1 copy.17
  24.6 0.1 copy.18
  24.7 1.6 %pack.1 = (bf16[14,2,256,128]{3,2,1,0:T(8,128)(2,1)S(1)}, bf16[14,2,128,256]{3,2,1,0:T(8,128)(2,1)S(1)}) custom-call(s32[3,32]{1,0:T(4,128)S(1)} %select.1.lists.refs_0_, bf16[2,1536,128]{2,1,0:T(8,128)(2,1)S(1)} %get-tuple-element.23.k0, bf16[2,1536,128]{2,1,0:T(8,128)(2,1)S(1)} %bitcast.15, bf16[2,1536,128]{2,1,0:T(8,128)(2,1)S(1)} %get-tuple-element.25.v0, ...), custom_call_target="tpu_custom_call" | custom-call | flops 1000000000 | bytes 4194304 | tf_op jit(solution)/shard_map/pack/pallas_call | solution.py:273
  26.3 0.7 collective-permute-start.7
  26.9 2.7 %collective-permute-start.6 = (bf16[8,2,2,16,128]{4,3,2,1,0:T(8,128)(2,1)S(1)}, bf16[8,2,2,16,128]{4,3,2,1,0:T(8,128)(2,1)S(1)}, u32[]{:S(2)}, u32[]{:S(2)}) collective-permute-start(bf16[8,2,2,16,128]{4,3,2,1,0:T(8,128)(2,1)S(1)} %collective-permute-done.5.refs_4_), channel_id=1, source_target_pairs={{8,0},{16,8},{24,16},{0,24},{9,1},{17,9},{25,17},{1,25},{10,2},{18... | collective-permute-start | bytes 393224 | tf_op jit(solution)/shard_map/ppermute | solution.py:244
  29.7 1.1 %collective-permute-done.4.refs_5_ = bf16[8,2,2,16,128]{4,3,2,1,0:T(8,128)(2,1)S(1)} collective-permute-done((bf16[8,2,2,16,128]{4,3,2,1,0:T(8,128)(2,1)S(1)}, bf16[8,2,2,16,128]{4,3,2,1,0:T(8,128)(2,1)S(1)}, u32[]{:S(2)}, u32[]{:S(2)}) %collective-permute-start.4) | collective-permute-done | bytes 131104 | tf_op jit(solution)/shard_map/ppermute | solution.py:244
  30.8 0.8 %collective-permute-start.10 = (bf16[8,2,2,16,128]{4,3,2,1,0:T(8,128)(2,1)S(1)}, bf16[8,2,2,16,128]{4,3,2,1,0:T(8,128)(2,1)S(1)}, u32[]{:S(2)}, u32[]{:S(2)}) collective-permute-start(bf16[8,2,2,16,128]{4,3,2,1,0:T(8,128)(2,1)S(1)} %collective-permute-done.3.refs_3_), channel_id=1, source_target_pairs={{8,0},{16,8},{24,16},{0,24},{9,1},{17,9},{25,17},{1,25},{10,2},{18... | collective-permute-start | bytes 393224 | tf_op jit(solution)/shard_map/ppermute | solution.py:244
  31.6 0.9 %collective-permute-done.7.refs_6_ = bf16[8,2,2,16,128]{4,3,2,1,0:T(8,128)(2,1)S(1)} collective-permute-done((bf16[8,2,2,16,128]{4,3,2,1,0:T(8,128)(2,1)S(1)}, bf16[8,2,2,16,128]{4,3,2,1,0:T(8,128)(2,1)S(1)}, u32[]{:S(2)}, u32[]{:S(2)}) %collective-permute-start.7) | collective-permute-done | bytes 131104 | tf_op jit(solution)/shard_map/ppermute | solution.py:244
  32.5 0.3 collective-permute-start.11
  32.8 2.8 %attend13.1 = (bf16[136,1024]{1,0:T(8,128)(2,1)S(1)}, bf16[136,1024]{1,0:T(8,128)(2,1)S(1)}) custom-call(s32[3,32]{1,0:T(4,128)S(1)} %select.1.lists.refs_0_, s32[4]{0:T(128)S(1)} %copy-done.1, s32[4]{0:T(128)S(1)} %copy-done, bf16[8,2,2,16,128]{4,3,2,1,0:T(8,128)(2,1)S(1)} %collective-permute-done.3.refs_3_, ...), custom_call_target="tpu_custom_call" | custom-call | flops 1000000000 | bytes 4194304 | tf_op jit(solution)/shard_map/attend13/pallas_call | solution.py:293
  35.6 1.3 %collective-permute-start.8 = (bf16[136,1024]{1,0:T(8,128)(2,1)S(1)}, bf16[136,1024]{1,0:T(8,128)(2,1)S(1)}, u32[]{:S(2)}, u32[]{:S(2)}) collective-permute-start(bf16[136,1024]{1,0:T(8,128)(2,1)S(1)} %get-tuple-element.33), channel_id=1, source_target_pairs={{24,0},{0,8},{8,16},{16,24},{25,1},{1,9},{9,17},{17,25},{26,2},{2,... | collective-permute-start | bytes 835592 | tf_op jit(solution)/shard_map/ppermute | solution.py:244
  36.9 2.0 %collective-permute-start.9 = (bf16[136,1024]{1,0:T(8,128)(2,1)S(1)}, bf16[136,1024]{1,0:T(8,128)(2,1)S(1)}, u32[]{:S(2)}, u32[]{:S(2)}) collective-permute-start(bf16[136,1024]{1,0:T(8,128)(2,1)S(1)} %get-tuple-element.34), channel_id=1, source_target_pairs={{8,0},{16,8},{24,16},{0,24},{9,1},{17,9},{25,17},{1,25},{10,2},{18... | collective-permute-start | bytes 835592 | tf_op jit(solution)/shard_map/ppermute | solution.py:244
  38.9 1.2 %collective-permute-done.11.refs_4_ = bf16[8,2,2,16,128]{4,3,2,1,0:T(8,128)(2,1)S(1)} collective-permute-done((bf16[8,2,2,16,128]{4,3,2,1,0:T(8,128)(2,1)S(1)}, bf16[8,2,2,16,128]{4,3,2,1,0:T(8,128)(2,1)S(1)}, u32[]{:S(2)}, u32[]{:S(2)}) %collective-permute-start.11) | collective-permute-done | bytes 131104 | tf_op jit(solution)/shard_map/ppermute | solution.py:244
  40.1 2.2 %attend2.1 = bf16[136,1024]{1,0:T(8,128)(2,1)S(1)} custom-call(s32[3,32]{1,0:T(4,128)S(1)} %select.1.lists.refs_0_, s32[4]{0:T(128)S(1)} %copy-done.1, s32[4]{0:T(128)S(1)} %copy-done, bf16[8,2,2,16,128]{4,3,2,1,0:T(8,128)(2,1)S(1)} %collective-permute-done.10.refs_3_, bf16[8,2,2,16,128]{4,3,2,1,0:T(8,128)(2,1)S(1)} %collective-permute-done.11.refs_4_, ...), custom_call_target="tpu_custom_call" | custom-call | flops 1000000000 | bytes 4194304 | tf_op jit(solution)/shard_map/attend2/pallas_call | solution.py:293
  42.3 0.3 collective-permute-start.12
  42.6 2.2 %attend0.1.in0 = bf16[136,1024]{1,0:T(8,128)(2,1)S(1)} custom-call(s32[3,32]{1,0:T(4,128)S(1)} %select.1.lists.refs_0_, s32[4]{0:T(128)S(1)} %copy-done.1, s32[4]{0:T(128)S(1)} %copy-done, bf16[8,2,2,16,128]{4,3,2,1,0:T(8,128)(2,1)S(1)} %all-to-all-done.refs_3_, bf16[8,2,2,16,128]{4,3,2,1,0:T(8,128)(2,1)S(1)} %collective-permute-done.5.refs_4_, ...), custom_call_target="tpu_custom_call" | custom-call | flops 1000000000 | bytes 4194304 | tf_op jit(solution)/shard_map/attend0/pallas_call | solution.py:293
  44.8 0.5 collective-permute-done.8.in0
  45.4 3.4 %collective-permute-done.9.in1 = bf16[136,1024]{1,0:T(8,128)(2,1)S(1)} collective-permute-done((bf16[136,1024]{1,0:T(8,128)(2,1)S(1)}, bf16[136,1024]{1,0:T(8,128)(2,1)S(1)}, u32[]{:S(2)}, u32[]{:S(2)}) %collective-permute-start.9) | collective-permute-done | bytes 278560 | tf_op jit(solution)/shard_map/ppermute | solution.py:244
  48.8 0.1 join.1.joined
  48.9 1.8 %collective-permute-done.12.in1 = bf16[136,1024]{1,0:T(8,128)(2,1)S(1)} collective-permute-done((bf16[136,1024]{1,0:T(8,128)(2,1)S(1)}, bf16[136,1024]{1,0:T(8,128)(2,1)S(1)}, u32[]{:S(2)}, u32[]{:S(2)}) %collective-permute-start.12) | collective-permute-done | bytes 278560 | tf_op jit(solution)/shard_map/ppermute | solution.py:244
  50.8 0.3 fold.1
  51.0 17.1 %all_to_all.10.in_ref = bf16[32,40,128]{2,1,0:T(8,128)(2,1)S(1)} all-to-all(bf16[32,40,128]{2,1,0:T(8,128)(2,1)S(1)} %fold.1), channel_id=1, replica_groups=mesh['z'=8,'y'=4,'xh'=2,'core'=2,'kvh'=2] {'z','xh','kvh'}, dimensions={0} | all-to-all | bytes 655360 | tf_op jit(solution)/shard_map/all_to_all | solution.py:329
  68.1 1.1 %finish.1 = bf16[1,64,128]{2,1,0:T(8,128)(2,1)} custom-call(bf16[32,40,128]{2,1,0:T(8,128)(2,1)S(1)} %all_to_all.10.in_ref), custom_call_target="tpu_custom_call" | custom-call | tf_op jit(solution)/shard_map/finish/pallas_call | solution.py:330
  (16 shorter events, 0.1 us)
Async XLA Ops:
  0.0 12.2 %copy-start.2 = (s32[12]{0:T(128)S(1)}, s32[12]{0:T(128)}, u32[]{:S(2)}) copy-start(s32[12]{0:T(128)} %param.9) | copy-start | bytes 148
  0.0 12.2 %copy-start.1 = (s32[4]{0:T(128)S(1)}, s32[4]{0:T(128)}, u32[]{:S(2)}) copy-start(s32[4]{0:T(128)} %refs_1_.5) | copy-start | bytes 52
  0.0 12.2 %copy-start = (s32[4]{0:T(128)S(1)}, s32[4]{0:T(128)}, u32[]{:S(2)}) copy-start(s32[4]{0:T(128)} %refs_2_.5) | copy-start | bytes 52
  0.0 18.4 %collective-permute-start.1 = (bf16[3072,128]{1,0:T(8,128)(2,1)}, bf16[3072,128]{1,0:T(8,128)(2,1)S(1)}, u32[]{:S(2)}, u32[]{:S(2)}) collective-permute-start(bf16[3072,128]{1,0:T(8,128)(2,1)} %bitcast.18), channel_id=1, source_target_pairs={{2,0},{0,2},{3,1},{1,3},{6,4},{4,6},{7,5},{5,7},{10,8},{8,10},{11,... | collective-permute-start | bytes 2359304 | tf_op jit(solution)/shard_map/ppermute | solution.py:244
  0.1 18.3 %collective-permute-start.2 = (bf16[3072,128]{1,0:T(8,128)(2,1)}, bf16[3072,128]{1,0:T(8,128)(2,1)S(1)}, u32[]{:S(2)}, u32[]{:S(2)}) collective-permute-start(bf16[3072,128]{1,0:T(8,128)(2,1)} %bitcast.19), channel_id=1, source_target_pairs={{2,0},{0,2},{3,1},{1,3},{6,4},{4,6},{7,5},{5,7},{10,8},{8,10},{11,... | collective-permute-start | bytes 2359304 | tf_op jit(solution)/shard_map/ppermute | solution.py:244
  2.0 16.4 %all-to-all-start = ((bf16[8,2,2,16,128]{4,3,2,1,0:T(8,128)(2,1)}), bf16[8,2,2,16,128]{4,3,2,1,0:T(8,128)(2,1)S(1)}, u32[]{:S(2)}, u32[]{:S(2)}) async-start(bf16[8,2,2,16,128]{4,3,2,1,0:T(8,128)(2,1)} %broadcast_in_dim.2), calls=%async_computation | async-start | bytes 262144 | tf_op jit(solution)/shard_map/all_to_all | solution.py:269
  10.6 1.6 %collective-permute-start = (s32[12]{0:T(128)}, s32[12]{0:T(128)S(1)}, u32[]{:S(2)}, u32[]{:S(2)}) collective-permute-start(s32[12]{0:T(128)} %param.9), channel_id=1, source_target_pairs={{2,0},{0,2},{3,1},{1,3},{6,4},{4,6},{7,5},{5,7},{10,8},{8,10},{11,... | collective-permute-start | bytes 152 | tf_op jit(solution)/shard_map/ppermute | solution.py:244
  18.4 7.8 %collective-permute-start.5 = (bf16[8,2,2,16,128]{4,3,2,1,0:T(8,128)(2,1)S(1)}, bf16[8,2,2,16,128]{4,3,2,1,0:T(8,128)(2,1)S(1)}, u32[]{:S(2)}, u32[]{:S(2)}) collective-permute-start(bf16[8,2,2,16,128]{4,3,2,1,0:T(8,128)(2,1)S(1)} %all-to-all-done.refs_3_), channel_id=1, source_target_pairs={{4,0},{0,4},{5,1},{1,5},{6,2},{2,6},{7,3},{3,7},{12,8},{8,12},{13,... | collective-permute-start | bytes 393224 | tf_op jit(solution)/shard_map/ppermute | solution.py:244
  21.5 8.2 %collective-permute-start.3 = (bf16[8,2,2,16,128]{4,3,2,1,0:T(8,128)(2,1)S(1)}, bf16[8,2,2,16,128]{4,3,2,1,0:T(8,128)(2,1)S(1)}, u32[]{:S(2)}, u32[]{:S(2)}) collective-permute-start(bf16[8,2,2,16,128]{4,3,2,1,0:T(8,128)(2,1)S(1)} %all-to-all-done.refs_3_), channel_id=1, source_target_pairs={{8,0},{16,8},{24,16},{0,24},{9,1},{17,9},{25,17},{1,25},{10,2},{18... | collective-permute-start | bytes 393224 | tf_op jit(solution)/shard_map/ppermute | solution.py:244
  24.5 6.3 %collective-permute-start.4 = (bf16[8,2,2,16,128]{4,3,2,1,0:T(8,128)(2,1)S(1)}, bf16[8,2,2,16,128]{4,3,2,1,0:T(8,128)(2,1)S(1)}, u32[]{:S(2)}, u32[]{:S(2)}) collective-permute-start(bf16[8,2,2,16,128]{4,3,2,1,0:T(8,128)(2,1)S(1)} %all-to-all-done.refs_3_), channel_id=1, source_target_pairs={{24,0},{0,8},{8,16},{16,24},{25,1},{1,9},{9,17},{17,25},{26,2},{2,... | collective-permute-start | bytes 393224 | tf_op jit(solution)/shard_map/ppermute | solution.py:244
  26.3 6.3 %collective-permute-start.7 = (bf16[8,2,2,16,128]{4,3,2,1,0:T(8,128)(2,1)S(1)}, bf16[8,2,2,16,128]{4,3,2,1,0:T(8,128)(2,1)S(1)}, u32[]{:S(2)}, u32[]{:S(2)}) collective-permute-start(bf16[8,2,2,16,128]{4,3,2,1,0:T(8,128)(2,1)S(1)} %collective-permute-done.5.refs_4_), channel_id=1, source_target_pairs={{24,0},{0,8},{8,16},{16,24},{25,1},{1,9},{9,17},{17,25},{26,2},{2,... | collective-permute-start | bytes 393224 | tf_op jit(solution)/shard_map/ppermute | solution.py:244
  26.9 5.9 %collective-permute-start.6 = (bf16[8,2,2,16,128]{4,3,2,1,0:T(8,128)(2,1)S(1)}, bf16[8,2,2,16,128]{4,3,2,1,0:T(8,128)(2,1)S(1)}, u32[]{:S(2)}, u32[]{:S(2)}) collective-permute-start(bf16[8,2,2,16,128]{4,3,2,1,0:T(8,128)(2,1)S(1)} %collective-permute-done.5.refs_4_), channel_id=1, source_target_pairs={{8,0},{16,8},{24,16},{0,24},{9,1},{17,9},{25,17},{1,25},{10,2},{18... | collective-permute-start | bytes 393224 | tf_op jit(solution)/shard_map/ppermute | solution.py:244
  30.8 8.1 %collective-permute-start.10 = (bf16[8,2,2,16,128]{4,3,2,1,0:T(8,128)(2,1)S(1)}, bf16[8,2,2,16,128]{4,3,2,1,0:T(8,128)(2,1)S(1)}, u32[]{:S(2)}, u32[]{:S(2)}) collective-permute-start(bf16[8,2,2,16,128]{4,3,2,1,0:T(8,128)(2,1)S(1)} %collective-permute-done.3.refs_3_), channel_id=1, source_target_pairs={{8,0},{16,8},{24,16},{0,24},{9,1},{17,9},{25,17},{1,25},{10,2},{18... | collective-permute-start | bytes 393224 | tf_op jit(solution)/shard_map/ppermute | solution.py:244
  32.5 7.6 %collective-permute-start.11 = (bf16[8,2,2,16,128]{4,3,2,1,0:T(8,128)(2,1)S(1)}, bf16[8,2,2,16,128]{4,3,2,1,0:T(8,128)(2,1)S(1)}, u32[]{:S(2)}, u32[]{:S(2)}) collective-permute-start(bf16[8,2,2,16,128]{4,3,2,1,0:T(8,128)(2,1)S(1)} %collective-permute-done.7.refs_6_), channel_id=1, source_target_pairs={{24,0},{0,8},{8,16},{16,24},{25,1},{1,9},{9,17},{17,25},{26,2},{2,... | collective-permute-start | bytes 393224 | tf_op jit(solution)/shard_map/ppermute | solution.py:244
  35.6 9.8 %collective-permute-start.8 = (bf16[136,1024]{1,0:T(8,128)(2,1)S(1)}, bf16[136,1024]{1,0:T(8,128)(2,1)S(1)}, u32[]{:S(2)}, u32[]{:S(2)}) collective-permute-start(bf16[136,1024]{1,0:T(8,128)(2,1)S(1)} %get-tuple-element.33), channel_id=1, source_target_pairs={{24,0},{0,8},{8,16},{16,24},{25,1},{1,9},{9,17},{17,25},{26,2},{2,... | collective-permute-start | bytes 835592 | tf_op jit(solution)/shard_map/ppermute | solution.py:244
  36.9 11.9 %collective-permute-start.9 = (bf16[136,1024]{1,0:T(8,128)(2,1)S(1)}, bf16[136,1024]{1,0:T(8,128)(2,1)S(1)}, u32[]{:S(2)}, u32[]{:S(2)}) collective-permute-start(bf16[136,1024]{1,0:T(8,128)(2,1)S(1)} %get-tuple-element.34), channel_id=1, source_target_pairs={{8,0},{16,8},{24,16},{0,24},{9,1},{17,9},{25,17},{1,25},{10,2},{18... | collective-permute-start | bytes 835592 | tf_op jit(solution)/shard_map/ppermute | solution.py:244
  42.3 8.4 %collective-permute-start.12 = (bf16[136,1024]{1,0:T(8,128)(2,1)S(1)}, bf16[136,1024]{1,0:T(8,128)(2,1)S(1)}, u32[]{:S(2)}, u32[]{:S(2)}) collective-permute-start(bf16[136,1024]{1,0:T(8,128)(2,1)S(1)} %attend2.1), channel_id=1, source_target_pairs={{16,0},{24,8},{0,16},{8,24},{17,1},{25,9},{1,17},{9,25},{18,2},{26... | collective-permute-start | bytes 835592 | tf_op jit(solution)/shard_map/ppermute | solution.py:244

commit v7 on v6

--- a/solution.py
+++ b/solution.py
@@ -187,7 +187,7 @@
 
 def fold_kernel(joined, in0, in1, out_ref):
     def dest(s, e):
-        return 8 * s + 4 * ((e >> 1) & 1) + 2 * ((lax.axis_index("xh") + (e >> 2)) & 1) + (e & 1)
+        return 16 * ((lax.axis_index("xh") + (e >> 2)) & 1) + 8 * (e & 1) + 2 * s + ((e >> 1) & 1)
 
     for s in range(SEQS):
         tails = []
@@ -216,7 +216,7 @@
 
 def finish_kernel(in_ref, out_ref):
     for kvh in range(2):
-        sources = [2 * n + kvh for n in range(16)]
+        sources = [16 * xh + 8 * kvh + z for xh in range(2) for z in range(8)]
         t = jnp.concatenate(
             [in_ref[n, 32:LAST, :].astype(jnp.float32) for n in sources], axis=0
         )
@@ -326,7 +326,7 @@
         compiler_params=params(12),
         name="fold",
     )(joined, msg0, turn(msg2, "y", 4, -2))
-    msg = lax.all_to_all(msg, ("z", "xh", "kvh"), split_axis=0, concat_axis=0, tiled=True)
+    msg = lax.all_to_all(msg, ("xh", "kvh", "z"), split_axis=0, concat_axis=0, tiled=True)
     return pl.pallas_call(
         finish_kernel,
         out_shape=jax.ShapeDtypeStruct((1, 64, HD), jnp.bfloat16),

time: 69.9 us -> 70.1 us (level)
  Pallas kernels: 12.1 us -> 10.2 us
  starting transfers between devices: 23.3 us -> 25 us
  blocking collectives: 17.1 us -> 18.5 us
  waiting for transfers between devices: 13.3 us -> 12.4 us
    ppermute x13, starting transfers between devices: 14.8 us -> 16.4 us  [turn(): return lax.ppermute(x, axis, [((i + step) % size, i) for i in range(size)])]
    pallas_call x3, Pallas kernels: 7.18 us -> 5.56 us  [attend(): pl.pallas_call(functools.partial(attend_kernel, steps), out_shape=[jax.Sh...]
    all_to_all x1, blocking collectives: 17.1 us -> 18.5 us  [per_device(): lax.all_to_all(msg, ('xh', 'kvh', 'z'), split_axis=0, concat_axis=0, tile...]
    ppermute x13, waiting for transfers between devices: 9.02 us -> 8.16 us  [turn(): return lax.ppermute(x, axis, [((i + step) % size, i) for i in range(size)])]
  transfers between devices with their start and end apart: 14 -> 14, of which waited for: 7 -> 6; matrix products, arithmetic and copies ran while one was open for 5% -> 5% of each run, Pallas kernels for 16% -> 13%
where the time goes in v7:
time: 70.1 us; the launch traced here: 69.5 us
  starting transfers between devices  25 us (36%)
  blocking collectives  18.5 us (26%)
  waiting for transfers between devices  12.4 us (18%)
  Pallas kernels  10.2 us (15%)
  local copies, waits for them, and re-layouts  3.18 us (5%)
    all_to_all x1, blocking collectives, per_device(): lax.all_to_all(msg, ('xh', 'kvh', 'z'), split_axis=0, concat_axis=0, tile...  18.5 us
    ppermute x13, starting transfers between devices, turn(): return lax.ppermute(x, axis, [((i + step) % size, i) for i in range(size)])  16.4 us
    all_to_all x1, starting transfers between devices, per_device(): q = lax.all_to_all(q, 'z', split_axis=0, concat_axis=0, tiled=True)  8.57 us
    ppermute x13, waiting for transfers between devices, turn(): return lax.ppermute(x, axis, [((i + step) % size, i) for i in range(size)])  8.16 us
    pallas_call x3, Pallas kernels, attend(): pl.pallas_call(functools.partial(attend_kernel, steps), out_shape=[jax.Sh...  5.56 us
    all_to_all x1, waiting for transfers between devices, per_device(): q = lax.all_to_all(q, 'z', split_axis=0, concat_axis=0, tiled=True)  4.27 us
    pallas_call x1, Pallas kernels, per_device(): pl.pallas_call(select_kernel, out_shape=jax.ShapeDtypeStruct((3, 32), jnp...  1.9 us
    transpose x1, local copies, waits for them, and re-layouts, by_head(): return jnp.transpose(x.reshape(OWN * BLK, HEADS, HD), (1, 0, 2))  1.57 us
  transfers between devices with their start and end apart: 14, of which 6 were waited for; matrix products, arithmetic and copies ran while one was open for 5% of the time, Pallas kernels for 13%

profile of v7, /device:TPU:32, one launch (start us, length us, event | category | flops | bytes accessed | tf_op | source)
XLA Modules:
  0.0 69.5 jit_solution(6850466628229955265)
XLA Ops:
  0.0 0.1 collective-permute-start.1
  0.1 0.5 collective-permute-start.2
  0.6 1.4 %broadcast_in_dim.2 = bf16[8,2,2,16,128]{4,3,2,1,0:T(8,128)(2,1)} broadcast(bf16[2,2,16,128]{3,2,1,0:T(8,128)(2,1)} %param.6), dimensions={1,2,3,4} | broadcast | bytes 147456 | tf_op jit(solution)/shard_map/broadcast_in_dim | solution.py:268
  2.0 8.6 %all-to-all-start = ((bf16[8,2,2,16,128]{4,3,2,1,0:T(8,128)(2,1)}), bf16[8,2,2,16,128]{4,3,2,1,0:T(8,128)(2,1)S(1)}, u32[]{:S(2)}, u32[]{:S(2)}) async-start(bf16[8,2,2,16,128]{4,3,2,1,0:T(8,128)(2,1)} %broadcast_in_dim.2), calls=%async_computation | async-start | bytes 262144 | tf_op jit(solution)/shard_map/all_to_all | solution.py:269
  10.6 1.6 %copy_bitcast_fusion.2 = (bf16[2,1536,128]{2,1,0:T(8,128)(2,1)S(1)}, bf16[2,1536,128]{2,1,0:T(8,128)(2,1)S(1)}) fusion(bf16[1536,2,128]{2,1,0:T(2,128)(2,1)} %param.8, bf16[1536,2,128]{2,1,0:T(2,128)(2,1)} %param.7), kind=kLoop, calls=%fused_computation.2 | loop fusion | bytes 3145728 | tf_op jit(solution)/shard_map/transpose | solution.py:252
  12.2 0.1 pad_add_fusion.meta
  12.3 1.9 %select.1.lists.refs_0_ = s32[3,32]{1,0:T(4,128)S(1)} custom-call(s32[32]{0:T(128)S(1)} %pad_add_fusion.meta), custom_call_target="tpu_custom_call" | custom-call | tf_op jit(solution)/shard_map/select/pallas_call | solution.py:259
  14.2 4.3 %all-to-all-done.refs_3_ = bf16[8,2,2,16,128]{4,3,2,1,0:T(8,128)(2,1)S(1)} async-done(((bf16[8,2,2,16,128]{4,3,2,1,0:T(8,128)(2,1)}), bf16[8,2,2,16,128]{4,3,2,1,0:T(8,128)(2,1)S(1)}, u32[]{:S(2)}, u32[]{:S(2)}) %all-to-all-start) | async-done | bytes 131104 | tf_op jit(solution)/shard_map/all_to_all | solution.py:269
  18.4 3.0 %collective-permute-start.5 = (bf16[8,2,2,16,128]{4,3,2,1,0:T(8,128)(2,1)S(1)}, bf16[8,2,2,16,128]{4,3,2,1,0:T(8,128)(2,1)S(1)}, u32[]{:S(2)}, u32[]{:S(2)}) collective-permute-start(bf16[8,2,2,16,128]{4,3,2,1,0:T(8,128)(2,1)S(1)} %all-to-all-done.refs_3_), channel_id=1, source_target_pairs={{4,0},{0,4},{5,1},{1,5},{6,2},{2,6},{7,3},{3,7},{12,8},{8,12},{13,... | collective-permute-start | bytes 393224 | tf_op jit(solution)/shard_map/ppermute | solution.py:244
  21.5 3.0 %collective-permute-start.3 = (bf16[8,2,2,16,128]{4,3,2,1,0:T(8,128)(2,1)S(1)}, bf16[8,2,2,16,128]{4,3,2,1,0:T(8,128)(2,1)S(1)}, u32[]{:S(2)}, u32[]{:S(2)}) collective-permute-start(bf16[8,2,2,16,128]{4,3,2,1,0:T(8,128)(2,1)S(1)} %all-to-all-done.refs_3_), channel_id=1, source_target_pairs={{8,0},{16,8},{24,16},{0,24},{9,1},{17,9},{25,17},{1,25},{10,2},{18... | collective-permute-start | bytes 393224 | tf_op jit(solution)/shard_map/ppermute | solution.py:244
  24.5 0.1 copy.17
  24.6 0.1 copy.18
  24.7 1.2 %pack.1 = (bf16[14,2,256,128]{3,2,1,0:T(8,128)(2,1)S(1)}, bf16[14,2,128,256]{3,2,1,0:T(8,128)(2,1)S(1)}) custom-call(s32[3,32]{1,0:T(4,128)S(1)} %select.1.lists.refs_0_, bf16[2,1536,128]{2,1,0:T(8,128)(2,1)S(1)} %get-tuple-element.23.k0, bf16[2,1536,128]{2,1,0:T(8,128)(2,1)S(1)} %bitcast.15, bf16[2,1536,128]{2,1,0:T(8,128)(2,1)S(1)} %get-tuple-element.25.v0, ...), custom_call_target="tpu_custom_call" | custom-call | flops 1000000000 | bytes 4194304 | tf_op jit(solution)/shard_map/pack/pallas_call | solution.py:273
  26.0 1.0 %collective-permute-start.7 = (bf16[8,2,2,16,128]{4,3,2,1,0:T(8,128)(2,1)S(1)}, bf16[8,2,2,16,128]{4,3,2,1,0:T(8,128)(2,1)S(1)}, u32[]{:S(2)}, u32[]{:S(2)}) collective-permute-start(bf16[8,2,2,16,128]{4,3,2,1,0:T(8,128)(2,1)S(1)} %collective-permute-done.5.refs_4_), channel_id=1, source_target_pairs={{24,0},{0,8},{8,16},{16,24},{25,1},{1,9},{9,17},{17,25},{26,2},{2,... | collective-permute-start | bytes 393224 | tf_op jit(solution)/shard_map/ppermute | solution.py:244
  26.9 2.4 %collective-permute-start.6 = (bf16[8,2,2,16,128]{4,3,2,1,0:T(8,128)(2,1)S(1)}, bf16[8,2,2,16,128]{4,3,2,1,0:T(8,128)(2,1)S(1)}, u32[]{:S(2)}, u32[]{:S(2)}) collective-permute-start(bf16[8,2,2,16,128]{4,3,2,1,0:T(8,128)(2,1)S(1)} %collective-permute-done.5.refs_4_), channel_id=1, source_target_pairs={{8,0},{16,8},{24,16},{0,24},{9,1},{17,9},{25,17},{1,25},{10,2},{18... | collective-permute-start | bytes 393224 | tf_op jit(solution)/shard_map/ppermute | solution.py:244
  29.4 1.3 %collective-permute-done.4.refs_5_ = bf16[8,2,2,16,128]{4,3,2,1,0:T(8,128)(2,1)S(1)} collective-permute-done((bf16[8,2,2,16,128]{4,3,2,1,0:T(8,128)(2,1)S(1)}, bf16[8,2,2,16,128]{4,3,2,1,0:T(8,128)(2,1)S(1)}, u32[]{:S(2)}, u32[]{:S(2)}) %collective-permute-start.4) | collective-permute-done | bytes 131104 | tf_op jit(solution)/shard_map/ppermute | solution.py:244
  30.7 0.6 collective-permute-start.10
  31.3 0.9 %collective-permute-done.7.refs_6_ = bf16[8,2,2,16,128]{4,3,2,1,0:T(8,128)(2,1)S(1)} collective-permute-done((bf16[8,2,2,16,128]{4,3,2,1,0:T(8,128)(2,1)S(1)}, bf16[8,2,2,16,128]{4,3,2,1,0:T(8,128)(2,1)S(1)}, u32[]{:S(2)}, u32[]{:S(2)}) %collective-permute-start.7) | collective-permute-done | bytes 131104 | tf_op jit(solution)/shard_map/ppermute | solution.py:244
  32.2 0.5 collective-permute-start.11
  32.7 2.1 %attend13.1 = (bf16[136,1024]{1,0:T(8,128)(2,1)S(1)}, bf16[136,1024]{1,0:T(8,128)(2,1)S(1)}) custom-call(s32[3,32]{1,0:T(4,128)S(1)} %select.1.lists.refs_0_, s32[4]{0:T(128)S(1)} %copy-done.1, s32[4]{0:T(128)S(1)} %copy-done, bf16[8,2,2,16,128]{4,3,2,1,0:T(8,128)(2,1)S(1)} %collective-permute-done.3.refs_3_, ...), custom_call_target="tpu_custom_call" | custom-call | flops 1000000000 | bytes 4194304 | tf_op jit(solution)/shard_map/attend13/pallas_call | solution.py:293
  34.9 1.6 %collective-permute-start.8 = (bf16[136,1024]{1,0:T(8,128)(2,1)S(1)}, bf16[136,1024]{1,0:T(8,128)(2,1)S(1)}, u32[]{:S(2)}, u32[]{:S(2)}) collective-permute-start(bf16[136,1024]{1,0:T(8,128)(2,1)S(1)} %get-tuple-element.33), channel_id=1, source_target_pairs={{24,0},{0,8},{8,16},{16,24},{25,1},{1,9},{9,17},{17,25},{26,2},{2,... | collective-permute-start | bytes 835592 | tf_op jit(solution)/shard_map/ppermute | solution.py:244
  36.5 1.7 %collective-permute-start.9 = (bf16[136,1024]{1,0:T(8,128)(2,1)S(1)}, bf16[136,1024]{1,0:T(8,128)(2,1)S(1)}, u32[]{:S(2)}, u32[]{:S(2)}) collective-permute-start(bf16[136,1024]{1,0:T(8,128)(2,1)S(1)} %get-tuple-element.34), channel_id=1, source_target_pairs={{8,0},{16,8},{24,16},{0,24},{9,1},{17,9},{25,17},{1,25},{10,2},{18... | collective-permute-start | bytes 835592 | tf_op jit(solution)/shard_map/ppermute | solution.py:244
  38.2 1.2 %collective-permute-done.11.refs_4_ = bf16[8,2,2,16,128]{4,3,2,1,0:T(8,128)(2,1)S(1)} collective-permute-done((bf16[8,2,2,16,128]{4,3,2,1,0:T(8,128)(2,1)S(1)}, bf16[8,2,2,16,128]{4,3,2,1,0:T(8,128)(2,1)S(1)}, u32[]{:S(2)}, u32[]{:S(2)}) %collective-permute-start.11) | collective-permute-done | bytes 131104 | tf_op jit(solution)/shard_map/ppermute | solution.py:244
  39.4 1.7 %attend2.1 = bf16[136,1024]{1,0:T(8,128)(2,1)S(1)} custom-call(s32[3,32]{1,0:T(4,128)S(1)} %select.1.lists.refs_0_, s32[4]{0:T(128)S(1)} %copy-done.1, s32[4]{0:T(128)S(1)} %copy-done, bf16[8,2,2,16,128]{4,3,2,1,0:T(8,128)(2,1)S(1)} %collective-permute-done.10.refs_3_, bf16[8,2,2,16,128]{4,3,2,1,0:T(8,128)(2,1)S(1)} %collective-permute-done.11.refs_4_, ...), custom_call_target="tpu_custom_call" | custom-call | flops 1000000000 | bytes 4194304 | tf_op jit(solution)/shard_map/attend2/pallas_call | solution.py:293
  41.1 2.0 %collective-permute-start.12 = (bf16[136,1024]{1,0:T(8,128)(2,1)S(1)}, bf16[136,1024]{1,0:T(8,128)(2,1)S(1)}, u32[]{:S(2)}, u32[]{:S(2)}) collective-permute-start(bf16[136,1024]{1,0:T(8,128)(2,1)S(1)} %attend2.1), channel_id=1, source_target_pairs={{16,0},{24,8},{0,16},{8,24},{17,1},{25,9},{1,17},{9,25},{18,2},{26... | collective-permute-start | bytes 835592 | tf_op jit(solution)/shard_map/ppermute | solution.py:244
  43.1 1.7 %attend0.1.in0 = bf16[136,1024]{1,0:T(8,128)(2,1)S(1)} custom-call(s32[3,32]{1,0:T(4,128)S(1)} %select.1.lists.refs_0_, s32[4]{0:T(128)S(1)} %copy-done.1, s32[4]{0:T(128)S(1)} %copy-done, bf16[8,2,2,16,128]{4,3,2,1,0:T(8,128)(2,1)S(1)} %all-to-all-done.refs_3_, bf16[8,2,2,16,128]{4,3,2,1,0:T(8,128)(2,1)S(1)} %collective-permute-done.5.refs_4_, ...), custom_call_target="tpu_custom_call" | custom-call | flops 1000000000 | bytes 4194304 | tf_op jit(solution)/shard_map/attend0/pallas_call | solution.py:293
  44.8 0.6 collective-permute-done.9.in1
  45.4 0.1 join.1.joined
  45.5 4.1 %collective-permute-done.12.in1 = bf16[136,1024]{1,0:T(8,128)(2,1)S(1)} collective-permute-done((bf16[136,1024]{1,0:T(8,128)(2,1)S(1)}, bf16[136,1024]{1,0:T(8,128)(2,1)S(1)}, u32[]{:S(2)}, u32[]{:S(2)}) %collective-permute-start.12) | collective-permute-done | bytes 278560 | tf_op jit(solution)/shard_map/ppermute | solution.py:244
  49.6 0.3 fold.1
  49.9 18.5 %all_to_all.10.in_ref = bf16[32,40,128]{2,1,0:T(8,128)(2,1)S(1)} all-to-all(bf16[32,40,128]{2,1,0:T(8,128)(2,1)S(1)} %fold.1), channel_id=1, replica_groups=mesh['z'=8,'y'=4,'xh'=2,'core'=2,'kvh'=2] {'xh','kvh','z'}, dimensions={0} | all-to-all | bytes 655360 | tf_op jit(solution)/shard_map/all_to_all | solution.py:329
  68.4 1.1 %finish.1 = bf16[1,64,128]{2,1,0:T(8,128)(2,1)} custom-call(bf16[32,40,128]{2,1,0:T(8,128)(2,1)S(1)} %all_to_all.10.in_ref), custom_call_target="tpu_custom_call" | custom-call | tf_op jit(solution)/shard_map/finish/pallas_call | solution.py:330
  (16 shorter events, 0.1 us)
Async XLA Ops:
  0.0 12.2 %copy-start.2 = (s32[12]{0:T(128)S(1)}, s32[12]{0:T(128)}, u32[]{:S(2)}) copy-start(s32[12]{0:T(128)} %param.9) | copy-start | bytes 148
  0.0 12.2 %copy-start.1 = (s32[4]{0:T(128)S(1)}, s32[4]{0:T(128)}, u32[]{:S(2)}) copy-start(s32[4]{0:T(128)} %refs_1_.5) | copy-start | bytes 52
  0.0 12.2 %copy-start = (s32[4]{0:T(128)S(1)}, s32[4]{0:T(128)}, u32[]{:S(2)}) copy-start(s32[4]{0:T(128)} %refs_2_.5) | copy-start | bytes 52
  0.0 18.4 %collective-permute-start.1 = (bf16[3072,128]{1,0:T(8,128)(2,1)}, bf16[3072,128]{1,0:T(8,128)(2,1)S(1)}, u32[]{:S(2)}, u32[]{:S(2)}) collective-permute-start(bf16[3072,128]{1,0:T(8,128)(2,1)} %bitcast.18), channel_id=1, source_target_pairs={{2,0},{0,2},{3,1},{1,3},{6,4},{4,6},{7,5},{5,7},{10,8},{8,10},{11,... | collective-permute-start | bytes 2359304 | tf_op jit(solution)/shard_map/ppermute | solution.py:244
  0.1 18.3 %collective-permute-start.2 = (bf16[3072,128]{1,0:T(8,128)(2,1)}, bf16[3072,128]{1,0:T(8,128)(2,1)S(1)}, u32[]{:S(2)}, u32[]{:S(2)}) collective-permute-start(bf16[3072,128]{1,0:T(8,128)(2,1)} %bitcast.19), channel_id=1, source_target_pairs={{2,0},{0,2},{3,1},{1,3},{6,4},{4,6},{7,5},{5,7},{10,8},{8,10},{11,... | collective-permute-start | bytes 2359304 | tf_op jit(solution)/shard_map/ppermute | solution.py:244
  2.0 16.4 %all-to-all-start = ((bf16[8,2,2,16,128]{4,3,2,1,0:T(8,128)(2,1)}), bf16[8,2,2,16,128]{4,3,2,1,0:T(8,128)(2,1)S(1)}, u32[]{:S(2)}, u32[]{:S(2)}) async-start(bf16[8,2,2,16,128]{4,3,2,1,0:T(8,128)(2,1)} %broadcast_in_dim.2), calls=%async_computation | async-start | bytes 262144 | tf_op jit(solution)/shard_map/all_to_all | solution.py:269
  10.6 1.6 %collective-permute-start = (s32[12]{0:T(128)}, s32[12]{0:T(128)S(1)}, u32[]{:S(2)}, u32[]{:S(2)}) collective-permute-start(s32[12]{0:T(128)} %param.9), channel_id=1, source_target_pairs={{2,0},{0,2},{3,1},{1,3},{6,4},{4,6},{7,5},{5,7},{10,8},{8,10},{11,... | collective-permute-start | bytes 152 | tf_op jit(solution)/shard_map/ppermute | solution.py:244
  18.4 7.5 %collective-permute-start.5 = (bf16[8,2,2,16,128]{4,3,2,1,0:T(8,128)(2,1)S(1)}, bf16[8,2,2,16,128]{4,3,2,1,0:T(8,128)(2,1)S(1)}, u32[]{:S(2)}, u32[]{:S(2)}) collective-permute-start(bf16[8,2,2,16,128]{4,3,2,1,0:T(8,128)(2,1)S(1)} %all-to-all-done.refs_3_), channel_id=1, source_target_pairs={{4,0},{0,4},{5,1},{1,5},{6,2},{2,6},{7,3},{3,7},{12,8},{8,12},{13,... | collective-permute-start | bytes 393224 | tf_op jit(solution)/shard_map/ppermute | solution.py:244
  21.5 7.9 %collective-permute-start.3 = (bf16[8,2,2,16,128]{4,3,2,1,0:T(8,128)(2,1)S(1)}, bf16[8,2,2,16,128]{4,3,2,1,0:T(8,128)(2,1)S(1)}, u32[]{:S(2)}, u32[]{:S(2)}) collective-permute-start(bf16[8,2,2,16,128]{4,3,2,1,0:T(8,128)(2,1)S(1)} %all-to-all-done.refs_3_), channel_id=1, source_target_pairs={{8,0},{16,8},{24,16},{0,24},{9,1},{17,9},{25,17},{1,25},{10,2},{18... | collective-permute-start | bytes 393224 | tf_op jit(solution)/shard_map/ppermute | solution.py:244
  24.5 6.2 %collective-permute-start.4 = (bf16[8,2,2,16,128]{4,3,2,1,0:T(8,128)(2,1)S(1)}, bf16[8,2,2,16,128]{4,3,2,1,0:T(8,128)(2,1)S(1)}, u32[]{:S(2)}, u32[]{:S(2)}) collective-permute-start(bf16[8,2,2,16,128]{4,3,2,1,0:T(8,128)(2,1)S(1)} %all-to-all-done.refs_3_), channel_id=1, source_target_pairs={{24,0},{0,8},{8,16},{16,24},{25,1},{1,9},{9,17},{17,25},{26,2},{2,... | collective-permute-start | bytes 393224 | tf_op jit(solution)/shard_map/ppermute | solution.py:244
  26.0 6.3 %collective-permute-start.7 = (bf16[8,2,2,16,128]{4,3,2,1,0:T(8,128)(2,1)S(1)}, bf16[8,2,2,16,128]{4,3,2,1,0:T(8,128)(2,1)S(1)}, u32[]{:S(2)}, u32[]{:S(2)}) collective-permute-start(bf16[8,2,2,16,128]{4,3,2,1,0:T(8,128)(2,1)S(1)} %collective-permute-done.5.refs_4_), channel_id=1, source_target_pairs={{24,0},{0,8},{8,16},{16,24},{25,1},{1,9},{9,17},{17,25},{26,2},{2,... | collective-permute-start | bytes 393224 | tf_op jit(solution)/shard_map/ppermute | solution.py:244
  26.9 5.8 %collective-permute-start.6 = (bf16[8,2,2,16,128]{4,3,2,1,0:T(8,128)(2,1)S(1)}, bf16[8,2,2,16,128]{4,3,2,1,0:T(8,128)(2,1)S(1)}, u32[]{:S(2)}, u32[]{:S(2)}) collective-permute-start(bf16[8,2,2,16,128]{4,3,2,1,0:T(8,128)(2,1)S(1)} %collective-permute-done.5.refs_4_), channel_id=1, source_target_pairs={{8,0},{16,8},{24,16},{0,24},{9,1},{17,9},{25,17},{1,25},{10,2},{18... | collective-permute-start | bytes 393224 | tf_op jit(solution)/shard_map/ppermute | solution.py:244
  30.7 7.5 %collective-permute-start.10 = (bf16[8,2,2,16,128]{4,3,2,1,0:T(8,128)(2,1)S(1)}, bf16[8,2,2,16,128]{4,3,2,1,0:T(8,128)(2,1)S(1)}, u32[]{:S(2)}, u32[]{:S(2)}) collective-permute-start(bf16[8,2,2,16,128]{4,3,2,1,0:T(8,128)(2,1)S(1)} %collective-permute-done.3.refs_3_), channel_id=1, source_target_pairs={{8,0},{16,8},{24,16},{0,24},{9,1},{17,9},{25,17},{1,25},{10,2},{18... | collective-permute-start | bytes 393224 | tf_op jit(solution)/shard_map/ppermute | solution.py:244
  32.2 7.2 %collective-permute-start.11 = (bf16[8,2,2,16,128]{4,3,2,1,0:T(8,128)(2,1)S(1)}, bf16[8,2,2,16,128]{4,3,2,1,0:T(8,128)(2,1)S(1)}, u32[]{:S(2)}, u32[]{:S(2)}) collective-permute-start(bf16[8,2,2,16,128]{4,3,2,1,0:T(8,128)(2,1)S(1)} %collective-permute-done.7.refs_6_), channel_id=1, source_target_pairs={{24,0},{0,8},{8,16},{16,24},{25,1},{1,9},{9,17},{17,25},{26,2},{2,... | collective-permute-start | bytes 393224 | tf_op jit(solution)/shard_map/ppermute | solution.py:244
  34.9 10.0 %collective-permute-start.8 = (bf16[136,1024]{1,0:T(8,128)(2,1)S(1)}, bf16[136,1024]{1,0:T(8,128)(2,1)S(1)}, u32[]{:S(2)}, u32[]{:S(2)}) collective-permute-start(bf16[136,1024]{1,0:T(8,128)(2,1)S(1)} %get-tuple-element.33), channel_id=1, source_target_pairs={{24,0},{0,8},{8,16},{16,24},{25,1},{1,9},{9,17},{17,25},{26,2},{2,... | collective-permute-start | bytes 835592 | tf_op jit(solution)/shard_map/ppermute | solution.py:244
  36.5 8.9 %collective-permute-start.9 = (bf16[136,1024]{1,0:T(8,128)(2,1)S(1)}, bf16[136,1024]{1,0:T(8,128)(2,1)S(1)}, u32[]{:S(2)}, u32[]{:S(2)}) collective-permute-start(bf16[136,1024]{1,0:T(8,128)(2,1)S(1)} %get-tuple-element.34), channel_id=1, source_target_pairs={{8,0},{16,8},{24,16},{0,24},{9,1},{17,9},{25,17},{1,25},{10,2},{18... | collective-permute-start | bytes 835592 | tf_op jit(solution)/shard_map/ppermute | solution.py:244
  41.1 8.5 %collective-permute-start.12 = (bf16[136,1024]{1,0:T(8,128)(2,1)S(1)}, bf16[136,1024]{1,0:T(8,128)(2,1)S(1)}, u32[]{:S(2)}, u32[]{:S(2)}) collective-permute-start(bf16[136,1024]{1,0:T(8,128)(2,1)S(1)} %attend2.1), channel_id=1, source_target_pairs={{16,0},{24,8},{0,16},{8,24},{17,1},{25,9},{1,17},{9,25},{18,2},{26... | collective-permute-start | bytes 835592 | tf_op jit(solution)/shard_map/ppermute | solution.py:244

commit v8 on v6

--- a/solution.py
+++ b/solution.py
@@ -285,7 +285,7 @@
     over, k, v = lax.optimization_barrier((turn(q, "xh", 2, 1), k, v))
     near, back = lax.optimization_barrier((turn(q, "y", 4, 1), turn(q, "y", 4, 3)))
     near, back = [near, turn(over, "y", 4, 1)], [back, turn(over, "y", 4, 3)]
-    qs = [[q, over], near, [turn(near[0], "y", 4, 1), turn(back[1], "y", 4, 3)], back]
+    qs = [[q, over], near, [turn(near[0], "y", 4, 1), turn(over, "y", 4, 2)], back]
 
     def attend(*steps):
         n = len(steps)

time: 69.9 us -> 74.1 us (1.060)
  starting transfers between devices: 23.3 us -> 24.7 us
  waiting for transfers between devices: 13.3 us -> 14.6 us
  blocking collectives: 17.1 us -> 17.9 us
    ppermute x13, starting transfers between devices: 14.8 us -> 16.2 us  [turn(): return lax.ppermute(x, axis, [((i + step) % size, i) for i in range(size)])]
    ppermute x13, waiting for transfers between devices: 9.02 us -> 10.4 us  [turn(): return lax.ppermute(x, axis, [((i + step) % size, i) for i in range(size)])]
    all_to_all x1, blocking collectives: 17.1 us -> 17.9 us  [per_device(): lax.all_to_all(msg, ('z', 'xh', 'kvh'), split_axis=0, concat_axis=0, tile...]
  transfers between devices with their start and end apart: 14 -> 14, of which waited for: 7 -> 5; matrix products, arithmetic and copies ran while one was open for 5% -> 4% of each run, Pallas kernels for 16% -> 15%
where the time goes in v8:
time: 74.1 us; the launch traced here: 72.9 us
  starting transfers between devices  24.7 us (33%)
  blocking collectives  17.9 us (24%)
  waiting for transfers between devices  14.6 us (20%)
  Pallas kernels  12.2 us (16%)
  local copies, waits for them, and re-layouts  3.18 us (4%)
    all_to_all x1, blocking collectives, per_device(): lax.all_to_all(msg, ('z', 'xh', 'kvh'), split_axis=0, concat_axis=0, tile...  17.9 us
    ppermute x13, starting transfers between devices, turn(): return lax.ppermute(x, axis, [((i + step) % size, i) for i in range(size)])  16.2 us
    ppermute x13, waiting for transfers between devices, turn(): return lax.ppermute(x, axis, [((i + step) % size, i) for i in range(size)])  10.4 us
    all_to_all x1, starting transfers between devices, per_device(): q = lax.all_to_all(q, 'z', split_axis=0, concat_axis=0, tiled=True)  8.57 us
    pallas_call x3, Pallas kernels, attend(): pl.pallas_call(functools.partial(attend_kernel, steps), out_shape=[jax.Sh...  7.2 us
    all_to_all x1, waiting for transfers between devices, per_device(): q = lax.all_to_all(q, 'z', split_axis=0, concat_axis=0, tiled=True)  4.27 us
    pallas_call x1, Pallas kernels, per_device(): pl.pallas_call(select_kernel, out_shape=jax.ShapeDtypeStruct((3, 32), jnp...  1.9 us
    transpose x1, local copies, waits for them, and re-layouts, by_head(): return jnp.transpose(x.reshape(OWN * BLK, HEADS, HD), (1, 0, 2))  1.57 us
  transfers between devices with their start and end apart: 14, of which 5 were waited for; matrix products, arithmetic and copies ran while one was open for 4% of the time, Pallas kernels for 15%

profile of v8, /device:TPU:32, one launch (start us, length us, event | category | flops | bytes accessed | tf_op | source)
XLA Modules:
  0.0 72.9 jit_solution(8145990568619663147)
XLA Ops:
  0.0 0.1 collective-permute-start.1
  0.1 0.5 collective-permute-start.2
  0.6 1.4 %broadcast_in_dim.2 = bf16[8,2,2,16,128]{4,3,2,1,0:T(8,128)(2,1)} broadcast(bf16[2,2,16,128]{3,2,1,0:T(8,128)(2,1)} %param.6), dimensions={1,2,3,4} | broadcast | bytes 147456 | tf_op jit(solution)/shard_map/broadcast_in_dim | solution.py:268
  2.0 8.6 %all-to-all-start = ((bf16[8,2,2,16,128]{4,3,2,1,0:T(8,128)(2,1)}), bf16[8,2,2,16,128]{4,3,2,1,0:T(8,128)(2,1)S(1)}, u32[]{:S(2)}, u32[]{:S(2)}) async-start(bf16[8,2,2,16,128]{4,3,2,1,0:T(8,128)(2,1)} %broadcast_in_dim.2), calls=%async_computation | async-start | bytes 262144 | tf_op jit(solution)/shard_map/all_to_all | solution.py:269
  10.6 1.6 %copy_bitcast_fusion.2 = (bf16[2,1536,128]{2,1,0:T(8,128)(2,1)S(1)}, bf16[2,1536,128]{2,1,0:T(8,128)(2,1)S(1)}) fusion(bf16[1536,2,128]{2,1,0:T(2,128)(2,1)} %param.8, bf16[1536,2,128]{2,1,0:T(2,128)(2,1)} %param.7), kind=kLoop, calls=%fused_computation.2 | loop fusion | bytes 3145728 | tf_op jit(solution)/shard_map/transpose | solution.py:252
  12.1 0.0 collective-permute-done
  12.2 0.1 pad_add_fusion.meta
  12.3 1.9 %select.1.lists.refs_0_ = s32[3,32]{1,0:T(4,128)S(1)} custom-call(s32[32]{0:T(128)S(1)} %pad_add_fusion.meta), custom_call_target="tpu_custom_call" | custom-call | tf_op jit(solution)/shard_map/select/pallas_call | solution.py:259
  14.2 4.3 %all-to-all-done.refs_3_ = bf16[8,2,2,16,128]{4,3,2,1,0:T(8,128)(2,1)S(1)} async-done(((bf16[8,2,2,16,128]{4,3,2,1,0:T(8,128)(2,1)}), bf16[8,2,2,16,128]{4,3,2,1,0:T(8,128)(2,1)S(1)}, u32[]{:S(2)}, u32[]{:S(2)}) %all-to-all-start) | async-done | bytes 131104 | tf_op jit(solution)/shard_map/all_to_all | solution.py:269
  18.4 0.0 collective-permute-done.2
  18.4 3.0 %collective-permute-start.5 = (bf16[8,2,2,16,128]{4,3,2,1,0:T(8,128)(2,1)S(1)}, bf16[8,2,2,16,128]{4,3,2,1,0:T(8,128)(2,1)S(1)}, u32[]{:S(2)}, u32[]{:S(2)}) collective-permute-start(bf16[8,2,2,16,128]{4,3,2,1,0:T(8,128)(2,1)S(1)} %all-to-all-done.refs_3_), channel_id=1, source_target_pairs={{4,0},{0,4},{5,1},{1,5},{6,2},{2,6},{7,3},{3,7},{12,8},{8,12},{13,... | collective-permute-start | bytes 393224 | tf_op jit(solution)/shard_map/ppermute | solution.py:244
  21.5 3.0 %collective-permute-start.3 = (bf16[8,2,2,16,128]{4,3,2,1,0:T(8,128)(2,1)S(1)}, bf16[8,2,2,16,128]{4,3,2,1,0:T(8,128)(2,1)S(1)}, u32[]{:S(2)}, u32[]{:S(2)}) collective-permute-start(bf16[8,2,2,16,128]{4,3,2,1,0:T(8,128)(2,1)S(1)} %all-to-all-done.refs_3_), channel_id=1, source_target_pairs={{8,0},{16,8},{24,16},{0,24},{9,1},{17,9},{25,17},{1,25},{10,2},{18... | collective-permute-start | bytes 393224 | tf_op jit(solution)/shard_map/ppermute | solution.py:244
  24.5 0.1 copy.17
  24.6 0.1 copy.18
  24.7 1.6 %pack.1 = (bf16[14,2,256,128]{3,2,1,0:T(8,128)(2,1)S(1)}, bf16[14,2,128,256]{3,2,1,0:T(8,128)(2,1)S(1)}) custom-call(s32[3,32]{1,0:T(4,128)S(1)} %select.1.lists.refs_0_, bf16[2,1536,128]{2,1,0:T(8,128)(2,1)S(1)} %get-tuple-element.23.k0, bf16[2,1536,128]{2,1,0:T(8,128)(2,1)S(1)} %bitcast.15, bf16[2,1536,128]{2,1,0:T(8,128)(2,1)S(1)} %get-tuple-element.25.v0, ...), custom_call_target="tpu_custom_call" | custom-call | flops 1000000000 | bytes 4194304 | tf_op jit(solution)/shard_map/pack/pallas_call | solution.py:273
  26.3 3.0 %collective-permute-start.6 = (bf16[8,2,2,16,128]{4,3,2,1,0:T(8,128)(2,1)S(1)}, bf16[8,2,2,16,128]{4,3,2,1,0:T(8,128)(2,1)S(1)}, u32[]{:S(2)}, u32[]{:S(2)}) collective-permute-start(bf16[8,2,2,16,128]{4,3,2,1,0:T(8,128)(2,1)S(1)} %collective-permute-done.5.refs_4_), channel_id=1, source_target_pairs={{8,0},{16,8},{24,16},{0,24},{9,1},{17,9},{25,17},{1,25},{10,2},{18... | collective-permute-start | bytes 393224 | tf_op jit(solution)/shard_map/ppermute | solution.py:244
  29.3 1.6 %collective-permute-start.11 = (bf16[8,2,2,16,128]{4,3,2,1,0:T(8,128)(2,1)S(1)}, bf16[8,2,2,16,128]{4,3,2,1,0:T(8,128)(2,1)S(1)}, u32[]{:S(2)}, u32[]{:S(2)}) collective-permute-start(bf16[8,2,2,16,128]{4,3,2,1,0:T(8,128)(2,1)S(1)} %collective-permute-done.5.refs_4_), channel_id=1, source_target_pairs={{16,0},{24,8},{0,16},{8,24},{17,1},{25,9},{1,17},{9,25},{18,2},{26... | collective-permute-start | bytes 393224 | tf_op jit(solution)/shard_map/ppermute | solution.py:244
  30.8 0.2 collective-permute-done.4.refs_5_
  31.0 1.6 %collective-permute-start.10 = (bf16[8,2,2,16,128]{4,3,2,1,0:T(8,128)(2,1)S(1)}, bf16[8,2,2,16,128]{4,3,2,1,0:T(8,128)(2,1)S(1)}, u32[]{:S(2)}, u32[]{:S(2)}) collective-permute-start(bf16[8,2,2,16,128]{4,3,2,1,0:T(8,128)(2,1)S(1)} %collective-permute-done.3.refs_3_), channel_id=1, source_target_pairs={{8,0},{16,8},{24,16},{0,24},{9,1},{17,9},{25,17},{1,25},{10,2},{18... | collective-permute-start | bytes 393224 | tf_op jit(solution)/shard_map/ppermute | solution.py:244
  32.6 1.3 %collective-permute-done.6.refs_4_ = bf16[8,2,2,16,128]{4,3,2,1,0:T(8,128)(2,1)S(1)} collective-permute-done((bf16[8,2,2,16,128]{4,3,2,1,0:T(8,128)(2,1)S(1)}, bf16[8,2,2,16,128]{4,3,2,1,0:T(8,128)(2,1)S(1)}, u32[]{:S(2)}, u32[]{:S(2)}) %collective-permute-start.6) | collective-permute-done | bytes 131104 | tf_op jit(solution)/shard_map/ppermute | solution.py:244
  33.9 2.9 %collective-permute-done.7.refs_6_ = bf16[8,2,2,16,128]{4,3,2,1,0:T(8,128)(2,1)S(1)} collective-permute-done((bf16[8,2,2,16,128]{4,3,2,1,0:T(8,128)(2,1)S(1)}, bf16[8,2,2,16,128]{4,3,2,1,0:T(8,128)(2,1)S(1)}, u32[]{:S(2)}, u32[]{:S(2)}) %collective-permute-start.7) | collective-permute-done | bytes 131104 | tf_op jit(solution)/shard_map/ppermute | solution.py:244
  36.8 2.8 %attend13.1 = (bf16[136,1024]{1,0:T(8,128)(2,1)S(1)}, bf16[136,1024]{1,0:T(8,128)(2,1)S(1)}) custom-call(s32[3,32]{1,0:T(4,128)S(1)} %select.1.lists.refs_0_, s32[4]{0:T(128)S(1)} %copy-done.1, s32[4]{0:T(128)S(1)} %copy-done, bf16[8,2,2,16,128]{4,3,2,1,0:T(8,128)(2,1)S(1)} %collective-permute-done.3.refs_3_, ...), custom_call_target="tpu_custom_call" | custom-call | flops 1000000000 | bytes 4194304 | tf_op jit(solution)/shard_map/attend13/pallas_call | solution.py:293
  39.6 0.1 collective-permute-start.8
  39.7 3.2 %collective-permute-start.9 = (bf16[136,1024]{1,0:T(8,128)(2,1)S(1)}, bf16[136,1024]{1,0:T(8,128)(2,1)S(1)}, u32[]{:S(2)}, u32[]{:S(2)}) collective-permute-start(bf16[136,1024]{1,0:T(8,128)(2,1)S(1)} %get-tuple-element.34), channel_id=1, source_target_pairs={{8,0},{16,8},{24,16},{0,24},{9,1},{17,9},{25,17},{1,25},{10,2},{18... | collective-permute-start | bytes 835592 | tf_op jit(solution)/shard_map/ppermute | solution.py:244
  42.9 2.2 %attend2.1 = bf16[136,1024]{1,0:T(8,128)(2,1)S(1)} custom-call(s32[3,32]{1,0:T(4,128)S(1)} %select.1.lists.refs_0_, s32[4]{0:T(128)S(1)} %copy-done.1, s32[4]{0:T(128)S(1)} %copy-done, bf16[8,2,2,16,128]{4,3,2,1,0:T(8,128)(2,1)S(1)} %collective-permute-done.10.refs_3_, bf16[8,2,2,16,128]{4,3,2,1,0:T(8,128)(2,1)S(1)} %collective-permute-done.11.refs_4_, ...), custom_call_target="tpu_custom_call" | custom-call | flops 1000000000 | bytes 4194304 | tf_op jit(solution)/shard_map/attend2/pallas_call | solution.py:293
  45.2 0.1 collective-permute-start.12
  45.3 2.2 %attend0.1.in0 = bf16[136,1024]{1,0:T(8,128)(2,1)S(1)} custom-call(s32[3,32]{1,0:T(4,128)S(1)} %select.1.lists.refs_0_, s32[4]{0:T(128)S(1)} %copy-done.1, s32[4]{0:T(128)S(1)} %copy-done, bf16[8,2,2,16,128]{4,3,2,1,0:T(8,128)(2,1)S(1)} %all-to-all-done.refs_3_, bf16[8,2,2,16,128]{4,3,2,1,0:T(8,128)(2,1)S(1)} %collective-permute-done.5.refs_4_, ...), custom_call_target="tpu_custom_call" | custom-call | flops 1000000000 | bytes 4194304 | tf_op jit(solution)/shard_map/attend0/pallas_call | solution.py:293
  47.5 5.9 %collective-permute-done.8.in0 = bf16[136,1024]{1,0:T(8,128)(2,1)S(1)} collective-permute-done((bf16[136,1024]{1,0:T(8,128)(2,1)S(1)}, bf16[136,1024]{1,0:T(8,128)(2,1)S(1)}, u32[]{:S(2)}, u32[]{:S(2)}) %collective-permute-start.8) | collective-permute-done | bytes 278560 | tf_op jit(solution)/shard_map/ppermute | solution.py:244
  53.4 0.1 join.1.joined
  53.6 0.3 fold.1
  53.8 17.9 %all_to_all.10.in_ref = bf16[32,40,128]{2,1,0:T(8,128)(2,1)S(1)} all-to-all(bf16[32,40,128]{2,1,0:T(8,128)(2,1)S(1)} %fold.1), channel_id=1, replica_groups=mesh['z'=8,'y'=4,'xh'=2,'core'=2,'kvh'=2] {'z','xh','kvh'}, dimensions={0} | all-to-all | bytes 655360 | tf_op jit(solution)/shard_map/all_to_all | solution.py:329
  71.8 1.1 %finish.1 = bf16[1,64,128]{2,1,0:T(8,128)(2,1)} custom-call(bf16[32,40,128]{2,1,0:T(8,128)(2,1)S(1)} %all_to_all.10.in_ref), custom_call_target="tpu_custom_call" | custom-call | tf_op jit(solution)/shard_map/finish/pallas_call | solution.py:330
  (16 shorter events, 0.0 us)
Async XLA Ops:
  0.0 12.2 %copy-start.2 = (s32[12]{0:T(128)S(1)}, s32[12]{0:T(128)}, u32[]{:S(2)}) copy-start(s32[12]{0:T(128)} %param.9) | copy-start | bytes 148
  0.0 12.2 %copy-start.1 = (s32[4]{0:T(128)S(1)}, s32[4]{0:T(128)}, u32[]{:S(2)}) copy-start(s32[4]{0:T(128)} %refs_1_.5) | copy-start | bytes 52
  0.0 12.2 %copy-start = (s32[4]{0:T(128)S(1)}, s32[4]{0:T(128)}, u32[]{:S(2)}) copy-start(s32[4]{0:T(128)} %refs_2_.5) | copy-start | bytes 52
  0.0 18.4 %collective-permute-start.1 = (bf16[3072,128]{1,0:T(8,128)(2,1)}, bf16[3072,128]{1,0:T(8,128)(2,1)S(1)}, u32[]{:S(2)}, u32[]{:S(2)}) collective-permute-start(bf16[3072,128]{1,0:T(8,128)(2,1)} %bitcast.18), channel_id=1, source_target_pairs={{2,0},{0,2},{3,1},{1,3},{6,4},{4,6},{7,5},{5,7},{10,8},{8,10},{11,... | collective-permute-start | bytes 2359304 | tf_op jit(solution)/shard_map/ppermute | solution.py:244
  0.1 18.3 %collective-permute-start.2 = (bf16[3072,128]{1,0:T(8,128)(2,1)}, bf16[3072,128]{1,0:T(8,128)(2,1)S(1)}, u32[]{:S(2)}, u32[]{:S(2)}) collective-permute-start(bf16[3072,128]{1,0:T(8,128)(2,1)} %bitcast.19), channel_id=1, source_target_pairs={{2,0},{0,2},{3,1},{1,3},{6,4},{4,6},{7,5},{5,7},{10,8},{8,10},{11,... | collective-permute-start | bytes 2359304 | tf_op jit(solution)/shard_map/ppermute | solution.py:244
  2.0 16.4 %all-to-all-start = ((bf16[8,2,2,16,128]{4,3,2,1,0:T(8,128)(2,1)}), bf16[8,2,2,16,128]{4,3,2,1,0:T(8,128)(2,1)S(1)}, u32[]{:S(2)}, u32[]{:S(2)}) async-start(bf16[8,2,2,16,128]{4,3,2,1,0:T(8,128)(2,1)} %broadcast_in_dim.2), calls=%async_computation | async-start | bytes 262144 | tf_op jit(solution)/shard_map/all_to_all | solution.py:269
  10.6 1.6 %collective-permute-start = (s32[12]{0:T(128)}, s32[12]{0:T(128)S(1)}, u32[]{:S(2)}, u32[]{:S(2)}) collective-permute-start(s32[12]{0:T(128)} %param.9), channel_id=1, source_target_pairs={{2,0},{0,2},{3,1},{1,3},{6,4},{4,6},{7,5},{5,7},{10,8},{8,10},{11,... | collective-permute-start | bytes 152 | tf_op jit(solution)/shard_map/ppermute | solution.py:244
  18.4 7.8 %collective-permute-start.5 = (bf16[8,2,2,16,128]{4,3,2,1,0:T(8,128)(2,1)S(1)}, bf16[8,2,2,16,128]{4,3,2,1,0:T(8,128)(2,1)S(1)}, u32[]{:S(2)}, u32[]{:S(2)}) collective-permute-start(bf16[8,2,2,16,128]{4,3,2,1,0:T(8,128)(2,1)S(1)} %all-to-all-done.refs_3_), channel_id=1, source_target_pairs={{4,0},{0,4},{5,1},{1,5},{6,2},{2,6},{7,3},{3,7},{12,8},{8,12},{13,... | collective-permute-start | bytes 393224 | tf_op jit(solution)/shard_map/ppermute | solution.py:244
  21.5 9.3 %collective-permute-start.3 = (bf16[8,2,2,16,128]{4,3,2,1,0:T(8,128)(2,1)S(1)}, bf16[8,2,2,16,128]{4,3,2,1,0:T(8,128)(2,1)S(1)}, u32[]{:S(2)}, u32[]{:S(2)}) collective-permute-start(bf16[8,2,2,16,128]{4,3,2,1,0:T(8,128)(2,1)S(1)} %all-to-all-done.refs_3_), channel_id=1, source_target_pairs={{8,0},{16,8},{24,16},{0,24},{9,1},{17,9},{25,17},{1,25},{10,2},{18... | collective-permute-start | bytes 393224 | tf_op jit(solution)/shard_map/ppermute | solution.py:244
  24.5 6.5 %collective-permute-start.4 = (bf16[8,2,2,16,128]{4,3,2,1,0:T(8,128)(2,1)S(1)}, bf16[8,2,2,16,128]{4,3,2,1,0:T(8,128)(2,1)S(1)}, u32[]{:S(2)}, u32[]{:S(2)}) collective-permute-start(bf16[8,2,2,16,128]{4,3,2,1,0:T(8,128)(2,1)S(1)} %all-to-all-done.refs_3_), channel_id=1, source_target_pairs={{24,0},{0,8},{8,16},{16,24},{25,1},{1,9},{9,17},{17,25},{26,2},{2,... | collective-permute-start | bytes 393224 | tf_op jit(solution)/shard_map/ppermute | solution.py:244
  26.3 7.6 %collective-permute-start.6 = (bf16[8,2,2,16,128]{4,3,2,1,0:T(8,128)(2,1)S(1)}, bf16[8,2,2,16,128]{4,3,2,1,0:T(8,128)(2,1)S(1)}, u32[]{:S(2)}, u32[]{:S(2)}) collective-permute-start(bf16[8,2,2,16,128]{4,3,2,1,0:T(8,128)(2,1)S(1)} %collective-permute-done.5.refs_4_), channel_id=1, source_target_pairs={{8,0},{16,8},{24,16},{0,24},{9,1},{17,9},{25,17},{1,25},{10,2},{18... | collective-permute-start | bytes 393224 | tf_op jit(solution)/shard_map/ppermute | solution.py:244
  29.3 7.6 %collective-permute-start.7 = (bf16[8,2,2,16,128]{4,3,2,1,0:T(8,128)(2,1)S(1)}, bf16[8,2,2,16,128]{4,3,2,1,0:T(8,128)(2,1)S(1)}, u32[]{:S(2)}, u32[]{:S(2)}) collective-permute-start(bf16[8,2,2,16,128]{4,3,2,1,0:T(8,128)(2,1)S(1)} %collective-permute-done.5.refs_4_), channel_id=1, source_target_pairs={{24,0},{0,8},{8,16},{16,24},{25,1},{1,9},{9,17},{17,25},{26,2},{2,... | collective-permute-start | bytes 393224 | tf_op jit(solution)/shard_map/ppermute | solution.py:244
  29.3 13.7 %collective-permute-start.11 = (bf16[8,2,2,16,128]{4,3,2,1,0:T(8,128)(2,1)S(1)}, bf16[8,2,2,16,128]{4,3,2,1,0:T(8,128)(2,1)S(1)}, u32[]{:S(2)}, u32[]{:S(2)}) collective-permute-start(bf16[8,2,2,16,128]{4,3,2,1,0:T(8,128)(2,1)S(1)} %collective-permute-done.5.refs_4_), channel_id=1, source_target_pairs={{16,0},{24,8},{0,16},{8,24},{17,1},{25,9},{1,17},{9,25},{18,2},{26... | collective-permute-start | bytes 393224 | tf_op jit(solution)/shard_map/ppermute | solution.py:244
  31.0 11.9 %collective-permute-start.10 = (bf16[8,2,2,16,128]{4,3,2,1,0:T(8,128)(2,1)S(1)}, bf16[8,2,2,16,128]{4,3,2,1,0:T(8,128)(2,1)S(1)}, u32[]{:S(2)}, u32[]{:S(2)}) collective-permute-start(bf16[8,2,2,16,128]{4,3,2,1,0:T(8,128)(2,1)S(1)} %collective-permute-done.3.refs_3_), channel_id=1, source_target_pairs={{8,0},{16,8},{24,16},{0,24},{9,1},{17,9},{25,17},{1,25},{10,2},{18... | collective-permute-start | bytes 393224 | tf_op jit(solution)/shard_map/ppermute | solution.py:244
  39.6 13.8 %collective-permute-start.8 = (bf16[136,1024]{1,0:T(8,128)(2,1)S(1)}, bf16[136,1024]{1,0:T(8,128)(2,1)S(1)}, u32[]{:S(2)}, u32[]{:S(2)}) collective-permute-start(bf16[136,1024]{1,0:T(8,128)(2,1)S(1)} %get-tuple-element.33), channel_id=1, source_target_pairs={{24,0},{0,8},{8,16},{16,24},{25,1},{1,9},{9,17},{17,25},{26,2},{2,... | collective-permute-start | bytes 835592 | tf_op jit(solution)/shard_map/ppermute | solution.py:244
  39.7 13.7 %collective-permute-start.9 = (bf16[136,1024]{1,0:T(8,128)(2,1)S(1)}, bf16[136,1024]{1,0:T(8,128)(2,1)S(1)}, u32[]{:S(2)}, u32[]{:S(2)}) collective-permute-start(bf16[136,1024]{1,0:T(8,128)(2,1)S(1)} %get-tuple-element.34), channel_id=1, source_target_pairs={{8,0},{16,8},{24,16},{0,24},{9,1},{17,9},{25,17},{1,25},{10,2},{18... | collective-permute-start | bytes 835592 | tf_op jit(solution)/shard_map/ppermute | solution.py:244
  45.2 8.4 %collective-permute-start.12 = (bf16[136,1024]{1,0:T(8,128)(2,1)S(1)}, bf16[136,1024]{1,0:T(8,128)(2,1)S(1)}, u32[]{:S(2)}, u32[]{:S(2)}) collective-permute-start(bf16[136,1024]{1,0:T(8,128)(2,1)S(1)} %attend2.1), channel_id=1, source_target_pairs={{16,0},{24,8},{0,16},{8,24},{17,1},{25,9},{1,17},{9,25},{18,2},{26... | collective-permute-start | bytes 835592 | tf_op jit(solution)/shard_map/ppermute | solution.py:244
